TPU v7x, 512 devices: a whole 4x8x8 slice. The times are simulated.
512 devices in a mesh: seq: 32 (over z, y_lo), head: 4 (over x), user: 4 (over y_hi, core).
Axes of the slice: x: 4, y: 8 (y_hi: 2, y_lo: 4; y = y_hi * 4 + y_lo), z: 8, core: 2. Of those that a mesh axis runs over, the one named last changes fastest.
Arguments:
- cand_rows: bfloat16 [8192, 1024], P(('user', 'seq'), 'head'), parts along dimension 0, may hold values from -6 to 6
- qu_weight: bfloat16 [1024, 2, 1024], P(None, None, 'head'), may hold values from -0.1875 to 0.1875
- out_weight: bfloat16 [1024, 1024], P('head'), may hold values from -0.1875 to 0.1875
- keys: bfloat16 [8, 32768, 1024], P('user', 'seq', 'head'), parts along dimension 0, may hold values from -6 to 6
- values: bfloat16 [8, 32768, 1024], P('user', 'seq', 'head'), parts along dimension 0, may hold values from -6 to 6
- lengths: int32 [8], P('user'), parts along dimension 0, may hold values from 1 to 32768, as said below
- cand_user: int32 [8192], P(('user', 'seq')), parts along dimension 0, may hold values from 0 to 1, as said below
Outputs:
- mixed: bfloat16 [8192, 1024], P(('user', 'seq'), 'head'), parts along dimension 0
There are 4 independent parts, one for each index of `user`. A program takes and returns all parts, laid end to end along the dimension named above; an argument that names none is the same for every part. Nothing has to cross between parts.
Inputs may be any that keep to these rules, and one draw needn't show every extreme that they name: `lengths`: exactly one user of each part has 32768 positions, the others fewer. `cand_user`: each aligned block of 64 rows (the rows of one index of seq) holds exactly 32 rows of each user.
All inputs are finite; a program needn't handle non-finite values.
Results may differ from a plain program's by a relative error of at most 0.0047.
Values may be sent and summed in bfloat16 or wider, within the bound.
No kernel may reach another device: no remote copies, remote signals or barrier semaphores. Data moves between devices by JAX's collectives and lax.ppermute only.
A program may use at most 64 MiB of HBM per device.

v0:
```python
import jax
import jax.numpy as jnp
from jax import lax
from jax.sharding import PartitionSpec as P

HEAD_DIM = 64


def passed_along(value, axis, steps):
    count = lax.axis_size(axis)
    pairs = [(source, (source + steps) % count) for source in range(count)]
    return lax.ppermute(value, axis, pairs)


def local(cand_rows, qu_weight, out_weight, keys, values, lengths, cand_user):
    row_count = cand_rows.shape[0]
    local_width = qu_weight.shape[2]
    heads_here = local_width // HEAD_DIM
    user_count = keys.shape[0]
    positions = keys.shape[1]
    per_owner = row_count // user_count
    scale = HEAD_DIM ** (-0.5)
    whole = lax.all_gather(cand_rows, "head", axis=1, tiled=True)
    projected = jax.nn.silu(
        jnp.dot(
            whole,
            qu_weight.reshape(qu_weight.shape[0], 2 * local_width),
            preferred_element_type=jnp.float32,
        )
    )
    queries = projected[:, :local_width].astype(jnp.bfloat16)
    gate_rows = projected[:, local_width:].astype(jnp.bfloat16)
    order = jnp.argsort(cand_user, stable=True)
    grouped = jnp.transpose(queries[order].reshape(user_count, per_owner, local_width), (1, 0, 2))
    first_position = lax.axis_index("seq") * positions
    live_mask = (first_position + jnp.arange(positions, dtype=jnp.int32))[None, :] < lengths[
        :, None
    ]
    key_heads = keys.reshape(user_count, positions, heads_here, HEAD_DIM)
    value_heads = values.reshape(user_count, positions, heads_here, HEAD_DIM)

    def attend_block(rows_in):
        count_now = rows_in.shape[0]
        query_heads = rows_in.reshape(count_now, user_count, heads_here, HEAD_DIM)
        scores = (
            jnp.einsum(
                "ruhe,uphe->ruhp", query_heads, key_heads, preferred_element_type=jnp.float32
            )
            * scale
        )
        weight = jnp.where(live_mask[None, :, None, :], jax.nn.silu(scores), 0.0).astype(
            jnp.bfloat16
        )
        result = jnp.einsum(
            "ruhp,uphe->ruhe", weight, value_heads, preferred_element_type=jnp.float32
        )
        return result.reshape(count_now, user_count, local_width)

    def attend(rows_in):
        count_now = rows_in.shape[0]
        return attend_block(rows_in)

    blank = jnp.zeros((per_owner, user_count, local_width), jnp.float32)

    def advance(turn, state_now):
        query_now, totals_now = state_now
        totals_now = totals_now + attend(query_now)
        return (
            passed_along(query_now.astype(jnp.float32), "seq", 1).astype(query_now.dtype),
            passed_along(totals_now, "seq", 1),
        )

    _, grouped_totals = lax.fori_loop(0, lax.axis_size("seq"), advance, (grouped, blank))
    sorted_totals = jnp.transpose(grouped_totals, (1, 0, 2)).reshape(row_count, local_width)
    inverse = jnp.argsort(order)
    totals = sorted_totals[inverse]
    user_iota = jnp.arange(user_count, dtype=jnp.int32)
    row_lengths = jnp.sum(
        jnp.where(cand_user[:, None] == user_iota[None, :], lengths[None, :], 0), axis=1
    ).astype(jnp.float32)
    attn = totals.reshape(row_count, heads_here, HEAD_DIM) / row_lengths[:, None, None]
    normed = attn * lax.rsqrt(jnp.mean(attn * attn, axis=-1, keepdims=True) + 1e-06)
    gated = (normed.reshape(row_count, local_width) * gate_rows.astype(jnp.float32)).astype(
        jnp.bfloat16
    )
    partial_terms = jnp.dot(gated, out_weight, preferred_element_type=jnp.float32)
    summed = lax.psum_scatter(partial_terms, "head", scatter_dimension=1, tiled=True)
    return (cand_rows.astype(jnp.float32) + summed).astype(jnp.bfloat16)


def solution(mesh):
    return jax.shard_map(
        local,
        mesh=mesh,
        in_specs=(
            P(("user", "seq"), "head"),
            P(None, None, "head"),
            P("head", None),
            P("user", "seq", "head"),
            P("user", "seq", "head"),
            P("user"),
            P(("user", "seq")),
        ),
        out_specs=P(("user", "seq"), "head"),
        check_vma=False,
    )
```

profile of v0, /device:TPU:8, one launch (start us, length us, event | category | flops | bytes accessed | tf_op | source)
XLA Modules:
  0.0 523.2 jit_solution(14451438706527814473)
XLA Ops:
  8.1 12.5 %all_gather.3 = bf16[64,1024]{1,0:T(8,128)(2,1)S(1)} all-gather(bf16[64,256]{1,0:T(8,128)(2,1)S(1)} %copy-done.4), channel_id=1, replica_groups=mesh['seq'=32,'head'=4,'user'=4] {'head'}, dimensions={1}, use_global_device_ids=true | all-gather | bytes 163840 | tf_op jit(solution)/shard_map/all_gather | solution.py:23
  21.6 2.0 sort.34
  27.1 2.0 sort.35
  29.9 452.6 %while.13 = (s32[]{:T(128)}, bf16[32,2,256]{2,1,0:T(2,128)(2,1)S(1)}, f32[32,2,256]{2,0,1:T(8,128)S(1)}, bf16[2,1024,4,64]{1,3,2,0:T(8,128)(2,1)S(1)}, bf16[2,10...) while((s32[]{:T(128)}, bf16[32,2,256]{2,1,0:T(2,128)(2,1)S(1)}, ...), condition=%wide.region_2.3_spmd.clone, body=%wide.region_1.2_spmd.clone.sunk | while | flops 68962304 | bytes 3186861 | solution.py:73
  30.1 2.0 convolution_bitcast_fusion.2
  32.3 3.5 collective-permute-start.1
  35.8 3.5 collective-permute-start
  39.3 4.2 collective-permute-done
  43.8 2.0 convolution_bitcast_fusion.2
  47.9 3.6 collective-permute-start
  51.5 7.2 %collective-permute-done = bf16[32,2,256]{2,1,0:T(2,128)(2,1)S(1)} collective-permute-done((bf16[32,2,256]{2,1,0:T(2,128)(2,1)S(1)}, bf16[32,2,256]{2,1,0:T(2,128)(2,1)S(1)}, u32[]{:S(2)}, u32[]{:S(2)}) %collective-permute-start) | collective-permute-done | bytes 32800 | tf_op jit(solution)/shard_map/while/body/eval_jaxpr/ppermute | solution.py:12
  59.0 2.0 convolution_bitcast_fusion.2
  63.2 2.8 collective-permute-start
  66.0 6.9 %collective-permute-done = bf16[32,2,256]{2,1,0:T(2,128)(2,1)S(1)} collective-permute-done((bf16[32,2,256]{2,1,0:T(2,128)(2,1)S(1)}, bf16[32,2,256]{2,1,0:T(2,128)(2,1)S(1)}, u32[]{:S(2)}, u32[]{:S(2)}) %collective-permute-start) | collective-permute-done | bytes 32800 | tf_op jit(solution)/shard_map/while/body/eval_jaxpr/ppermute | solution.py:12
  73.1 2.0 convolution_bitcast_fusion.2
  79.2 7.8 %collective-permute-done = bf16[32,2,256]{2,1,0:T(2,128)(2,1)S(1)} collective-permute-done((bf16[32,2,256]{2,1,0:T(2,128)(2,1)S(1)}, bf16[32,2,256]{2,1,0:T(2,128)(2,1)S(1)}, u32[]{:S(2)}, u32[]{:S(2)}) %collective-permute-start) | collective-permute-done | bytes 32800 | tf_op jit(solution)/shard_map/while/body/eval_jaxpr/ppermute | solution.py:12
  87.2 2.0 convolution_bitcast_fusion.2
  93.3 7.8 %collective-permute-done = bf16[32,2,256]{2,1,0:T(2,128)(2,1)S(1)} collective-permute-done((bf16[32,2,256]{2,1,0:T(2,128)(2,1)S(1)}, bf16[32,2,256]{2,1,0:T(2,128)(2,1)S(1)}, u32[]{:S(2)}, u32[]{:S(2)}) %collective-permute-start) | collective-permute-done | bytes 32800 | tf_op jit(solution)/shard_map/while/body/eval_jaxpr/ppermute | solution.py:12
  101.3 2.0 convolution_bitcast_fusion.2
  107.4 7.8 %collective-permute-done = bf16[32,2,256]{2,1,0:T(2,128)(2,1)S(1)} collective-permute-done((bf16[32,2,256]{2,1,0:T(2,128)(2,1)S(1)}, bf16[32,2,256]{2,1,0:T(2,128)(2,1)S(1)}, u32[]{:S(2)}, u32[]{:S(2)}) %collective-permute-start) | collective-permute-done | bytes 32800 | tf_op jit(solution)/shard_map/while/body/eval_jaxpr/ppermute | solution.py:12
  115.4 2.0 convolution_bitcast_fusion.2
  121.5 7.8 %collective-permute-done = bf16[32,2,256]{2,1,0:T(2,128)(2,1)S(1)} collective-permute-done((bf16[32,2,256]{2,1,0:T(2,128)(2,1)S(1)}, bf16[32,2,256]{2,1,0:T(2,128)(2,1)S(1)}, u32[]{:S(2)}, u32[]{:S(2)}) %collective-permute-start) | collective-permute-done | bytes 32800 | tf_op jit(solution)/shard_map/while/body/eval_jaxpr/ppermute | solution.py:12
  129.5 2.0 convolution_bitcast_fusion.2
  135.6 8.0 %collective-permute-done = bf16[32,2,256]{2,1,0:T(2,128)(2,1)S(1)} collective-permute-done((bf16[32,2,256]{2,1,0:T(2,128)(2,1)S(1)}, bf16[32,2,256]{2,1,0:T(2,128)(2,1)S(1)}, u32[]{:S(2)}, u32[]{:S(2)}) %collective-permute-start) | collective-permute-done | bytes 32800 | tf_op jit(solution)/shard_map/while/body/eval_jaxpr/ppermute | solution.py:12
  150.0 7.5 %collective-permute-done = bf16[32,2,256]{2,1,0:T(2,128)(2,1)S(1)} collective-permute-done((bf16[32,2,256]{2,1,0:T(2,128)(2,1)S(1)}, bf16[32,2,256]{2,1,0:T(2,128)(2,1)S(1)}, u32[]{:S(2)}, u32[]{:S(2)}) %collective-permute-start) | collective-permute-done | bytes 32800 | tf_op jit(solution)/shard_map/while/body/eval_jaxpr/ppermute | solution.py:12
  157.7 2.0 convolution_bitcast_fusion.2
  163.8 8.1 %collective-permute-done = bf16[32,2,256]{2,1,0:T(2,128)(2,1)S(1)} collective-permute-done((bf16[32,2,256]{2,1,0:T(2,128)(2,1)S(1)}, bf16[32,2,256]{2,1,0:T(2,128)(2,1)S(1)}, u32[]{:S(2)}, u32[]{:S(2)}) %collective-permute-start) | collective-permute-done | bytes 32800 | tf_op jit(solution)/shard_map/while/body/eval_jaxpr/ppermute | solution.py:12
  172.1 2.0 convolution_bitcast_fusion.2
  178.2 7.8 %collective-permute-done = bf16[32,2,256]{2,1,0:T(2,128)(2,1)S(1)} collective-permute-done((bf16[32,2,256]{2,1,0:T(2,128)(2,1)S(1)}, bf16[32,2,256]{2,1,0:T(2,128)(2,1)S(1)}, u32[]{:S(2)}, u32[]{:S(2)}) %collective-permute-start) | collective-permute-done | bytes 32800 | tf_op jit(solution)/shard_map/while/body/eval_jaxpr/ppermute | solution.py:12
  186.2 2.0 convolution_bitcast_fusion.2
  192.3 7.8 %collective-permute-done = bf16[32,2,256]{2,1,0:T(2,128)(2,1)S(1)} collective-permute-done((bf16[32,2,256]{2,1,0:T(2,128)(2,1)S(1)}, bf16[32,2,256]{2,1,0:T(2,128)(2,1)S(1)}, u32[]{:S(2)}, u32[]{:S(2)}) %collective-permute-start) | collective-permute-done | bytes 32800 | tf_op jit(solution)/shard_map/while/body/eval_jaxpr/ppermute | solution.py:12
  200.3 2.0 convolution_bitcast_fusion.2
  206.4 7.8 %collective-permute-done = bf16[32,2,256]{2,1,0:T(2,128)(2,1)S(1)} collective-permute-done((bf16[32,2,256]{2,1,0:T(2,128)(2,1)S(1)}, bf16[32,2,256]{2,1,0:T(2,128)(2,1)S(1)}, u32[]{:S(2)}, u32[]{:S(2)}) %collective-permute-start) | collective-permute-done | bytes 32800 | tf_op jit(solution)/shard_map/while/body/eval_jaxpr/ppermute | solution.py:12
  214.4 2.0 convolution_bitcast_fusion.2
  220.5 7.8 %collective-permute-done = bf16[32,2,256]{2,1,0:T(2,128)(2,1)S(1)} collective-permute-done((bf16[32,2,256]{2,1,0:T(2,128)(2,1)S(1)}, bf16[32,2,256]{2,1,0:T(2,128)(2,1)S(1)}, u32[]{:S(2)}, u32[]{:S(2)}) %collective-permute-start) | collective-permute-done | bytes 32800 | tf_op jit(solution)/shard_map/while/body/eval_jaxpr/ppermute | solution.py:12
  228.5 2.0 convolution_bitcast_fusion.2
  234.6 7.8 %collective-permute-done = bf16[32,2,256]{2,1,0:T(2,128)(2,1)S(1)} collective-permute-done((bf16[32,2,256]{2,1,0:T(2,128)(2,1)S(1)}, bf16[32,2,256]{2,1,0:T(2,128)(2,1)S(1)}, u32[]{:S(2)}, u32[]{:S(2)}) %collective-permute-start) | collective-permute-done | bytes 32800 | tf_op jit(solution)/shard_map/while/body/eval_jaxpr/ppermute | solution.py:12
  242.6 2.0 convolution_bitcast_fusion.2
  248.7 7.8 %collective-permute-done = bf16[32,2,256]{2,1,0:T(2,128)(2,1)S(1)} collective-permute-done((bf16[32,2,256]{2,1,0:T(2,128)(2,1)S(1)}, bf16[32,2,256]{2,1,0:T(2,128)(2,1)S(1)}, u32[]{:S(2)}, u32[]{:S(2)}) %collective-permute-start) | collective-permute-done | bytes 32800 | tf_op jit(solution)/shard_map/while/body/eval_jaxpr/ppermute | solution.py:12
  256.8 2.0 convolution_bitcast_fusion.2
  262.8 7.8 %collective-permute-done = bf16[32,2,256]{2,1,0:T(2,128)(2,1)S(1)} collective-permute-done((bf16[32,2,256]{2,1,0:T(2,128)(2,1)S(1)}, bf16[32,2,256]{2,1,0:T(2,128)(2,1)S(1)}, u32[]{:S(2)}, u32[]{:S(2)}) %collective-permute-start) | collective-permute-done | bytes 32800 | tf_op jit(solution)/shard_map/while/body/eval_jaxpr/ppermute | solution.py:12
  270.9 2.0 convolution_bitcast_fusion.2
  277.0 7.8 %collective-permute-done = bf16[32,2,256]{2,1,0:T(2,128)(2,1)S(1)} collective-permute-done((bf16[32,2,256]{2,1,0:T(2,128)(2,1)S(1)}, bf16[32,2,256]{2,1,0:T(2,128)(2,1)S(1)}, u32[]{:S(2)}, u32[]{:S(2)}) %collective-permute-start) | collective-permute-done | bytes 32800 | tf_op jit(solution)/shard_map/while/body/eval_jaxpr/ppermute | solution.py:12
  285.0 2.0 convolution_bitcast_fusion.2
  291.1 7.8 %collective-permute-done = bf16[32,2,256]{2,1,0:T(2,128)(2,1)S(1)} collective-permute-done((bf16[32,2,256]{2,1,0:T(2,128)(2,1)S(1)}, bf16[32,2,256]{2,1,0:T(2,128)(2,1)S(1)}, u32[]{:S(2)}, u32[]{:S(2)}) %collective-permute-start) | collective-permute-done | bytes 32800 | tf_op jit(solution)/shard_map/while/body/eval_jaxpr/ppermute | solution.py:12
  299.1 2.0 convolution_bitcast_fusion.2
  305.2 8.1 %collective-permute-done = bf16[32,2,256]{2,1,0:T(2,128)(2,1)S(1)} collective-permute-done((bf16[32,2,256]{2,1,0:T(2,128)(2,1)S(1)}, bf16[32,2,256]{2,1,0:T(2,128)(2,1)S(1)}, u32[]{:S(2)}, u32[]{:S(2)}) %collective-permute-start) | collective-permute-done | bytes 32800 | tf_op jit(solution)/shard_map/while/body/eval_jaxpr/ppermute | solution.py:12
  319.5 7.5 %collective-permute-done = bf16[32,2,256]{2,1,0:T(2,128)(2,1)S(1)} collective-permute-done((bf16[32,2,256]{2,1,0:T(2,128)(2,1)S(1)}, bf16[32,2,256]{2,1,0:T(2,128)(2,1)S(1)}, u32[]{:S(2)}, u32[]{:S(2)}) %collective-permute-start) | collective-permute-done | bytes 32800 | tf_op jit(solution)/shard_map/while/body/eval_jaxpr/ppermute | solution.py:12
  327.3 2.0 convolution_bitcast_fusion.2
  333.4 8.0 %collective-permute-done = bf16[32,2,256]{2,1,0:T(2,128)(2,1)S(1)} collective-permute-done((bf16[32,2,256]{2,1,0:T(2,128)(2,1)S(1)}, bf16[32,2,256]{2,1,0:T(2,128)(2,1)S(1)}, u32[]{:S(2)}, u32[]{:S(2)}) %collective-permute-start) | collective-permute-done | bytes 32800 | tf_op jit(solution)/shard_map/while/body/eval_jaxpr/ppermute | solution.py:12
  341.6 2.0 convolution_bitcast_fusion.2
  347.7 7.8 %collective-permute-done = bf16[32,2,256]{2,1,0:T(2,128)(2,1)S(1)} collective-permute-done((bf16[32,2,256]{2,1,0:T(2,128)(2,1)S(1)}, bf16[32,2,256]{2,1,0:T(2,128)(2,1)S(1)}, u32[]{:S(2)}, u32[]{:S(2)}) %collective-permute-start) | collective-permute-done | bytes 32800 | tf_op jit(solution)/shard_map/while/body/eval_jaxpr/ppermute | solution.py:12
  355.7 2.0 convolution_bitcast_fusion.2
  361.8 7.8 %collective-permute-done = bf16[32,2,256]{2,1,0:T(2,128)(2,1)S(1)} collective-permute-done((bf16[32,2,256]{2,1,0:T(2,128)(2,1)S(1)}, bf16[32,2,256]{2,1,0:T(2,128)(2,1)S(1)}, u32[]{:S(2)}, u32[]{:S(2)}) %collective-permute-start) | collective-permute-done | bytes 32800 | tf_op jit(solution)/shard_map/while/body/eval_jaxpr/ppermute | solution.py:12
  369.9 2.0 convolution_bitcast_fusion.2
  375.9 7.8 %collective-permute-done = bf16[32,2,256]{2,1,0:T(2,128)(2,1)S(1)} collective-permute-done((bf16[32,2,256]{2,1,0:T(2,128)(2,1)S(1)}, bf16[32,2,256]{2,1,0:T(2,128)(2,1)S(1)}, u32[]{:S(2)}, u32[]{:S(2)}) %collective-permute-start) | collective-permute-done | bytes 32800 | tf_op jit(solution)/shard_map/while/body/eval_jaxpr/ppermute | solution.py:12
  390.1 7.8 %collective-permute-done = bf16[32,2,256]{2,1,0:T(2,128)(2,1)S(1)} collective-permute-done((bf16[32,2,256]{2,1,0:T(2,128)(2,1)S(1)}, bf16[32,2,256]{2,1,0:T(2,128)(2,1)S(1)}, u32[]{:S(2)}, u32[]{:S(2)}) %collective-permute-start) | collective-permute-done | bytes 32800 | tf_op jit(solution)/shard_map/while/body/eval_jaxpr/ppermute | solution.py:12
  404.2 7.8 %collective-permute-done = bf16[32,2,256]{2,1,0:T(2,128)(2,1)S(1)} collective-permute-done((bf16[32,2,256]{2,1,0:T(2,128)(2,1)S(1)}, bf16[32,2,256]{2,1,0:T(2,128)(2,1)S(1)}, u32[]{:S(2)}, u32[]{:S(2)}) %collective-permute-start) | collective-permute-done | bytes 32800 | tf_op jit(solution)/shard_map/while/body/eval_jaxpr/ppermute | solution.py:12
  418.3 7.8 %collective-permute-done = bf16[32,2,256]{2,1,0:T(2,128)(2,1)S(1)} collective-permute-done((bf16[32,2,256]{2,1,0:T(2,128)(2,1)S(1)}, bf16[32,2,256]{2,1,0:T(2,128)(2,1)S(1)}, u32[]{:S(2)}, u32[]{:S(2)}) %collective-permute-start) | collective-permute-done | bytes 32800 | tf_op jit(solution)/shard_map/while/body/eval_jaxpr/ppermute | solution.py:12
  432.4 7.8 %collective-permute-done = bf16[32,2,256]{2,1,0:T(2,128)(2,1)S(1)} collective-permute-done((bf16[32,2,256]{2,1,0:T(2,128)(2,1)S(1)}, bf16[32,2,256]{2,1,0:T(2,128)(2,1)S(1)}, u32[]{:S(2)}, u32[]{:S(2)}) %collective-permute-start) | collective-permute-done | bytes 32800 | tf_op jit(solution)/shard_map/while/body/eval_jaxpr/ppermute | solution.py:12
  446.5 7.8 %collective-permute-done = bf16[32,2,256]{2,1,0:T(2,128)(2,1)S(1)} collective-permute-done((bf16[32,2,256]{2,1,0:T(2,128)(2,1)S(1)}, bf16[32,2,256]{2,1,0:T(2,128)(2,1)S(1)}, u32[]{:S(2)}, u32[]{:S(2)}) %collective-permute-start) | collective-permute-done | bytes 32800 | tf_op jit(solution)/shard_map/while/body/eval_jaxpr/ppermute | solution.py:12
  460.6 7.8 %collective-permute-done = bf16[32,2,256]{2,1,0:T(2,128)(2,1)S(1)} collective-permute-done((bf16[32,2,256]{2,1,0:T(2,128)(2,1)S(1)}, bf16[32,2,256]{2,1,0:T(2,128)(2,1)S(1)}, u32[]{:S(2)}, u32[]{:S(2)}) %collective-permute-start) | collective-permute-done | bytes 32800 | tf_op jit(solution)/shard_map/while/body/eval_jaxpr/ppermute | solution.py:12
  474.7 7.8 %collective-permute-done = bf16[32,2,256]{2,1,0:T(2,128)(2,1)S(1)} collective-permute-done((bf16[32,2,256]{2,1,0:T(2,128)(2,1)S(1)}, bf16[32,2,256]{2,1,0:T(2,128)(2,1)S(1)}, u32[]{:S(2)}, u32[]{:S(2)}) %collective-permute-start) | collective-permute-done | bytes 32800 | tf_op jit(solution)/shard_map/while/body/eval_jaxpr/ppermute | solution.py:12
  484.8 30.1 %reduce-scatter.2.cloned.1.call-done = f32[64,256]{1,0:T(8,128)} async-done(((f32[64,1024]{1,0:T(8,128)}), f32[64,256]{1,0:T(8,128)}) %reduce-scatter.2.cloned.1.call-update) | async-done | bytes 65552 | tf_op jit(solution)/shard_map/reduce_scatter | solution.py:87
  (334 shorter events, 158.1 us)
Async XLA Ops:
  6.5 508.4 %reduce-scatter.2.cloned.1.call-start = ((), (), s32[]{:S(2)}) async-start(), calls=%async_computation.1 | async-start | bytes 327680 | tf_op jit(solution)/shard_map/reduce_scatter | solution.py:87
  32.3 11.2 %collective-permute-start.1 = (f32[32,2,256]{2,0,1:T(8,128)S(1)}, f32[32,2,256]{2,0,1:T(8,128)S(1)}, u32[]{:S(2)}, u32[]{:S(2)}) collective-permute-start(f32[32,2,256]{2,0,1:T(8,128)S(1)} %add.73), channel_id=1, source_target_pairs={{0,16},{16,32},{32,48},{48,64},{64,80},{80,96},{96,112},{112,128},... | collective-permute-start | bytes 196616 | tf_op jit(solution)/shard_map/while/body/eval_jaxpr/ppermute | solution.py:12
  46.0 12.8 %collective-permute-start.1 = (f32[32,2,256]{2,0,1:T(8,128)S(1)}, f32[32,2,256]{2,0,1:T(8,128)S(1)}, u32[]{:S(2)}, u32[]{:S(2)}) collective-permute-start(f32[32,2,256]{2,0,1:T(8,128)S(1)} %add.73), channel_id=1, source_target_pairs={{0,16},{16,32},{32,48},{48,64},{64,80},{80,96},{96,112},{112,128},... | collective-permute-start | bytes 196616 | tf_op jit(solution)/shard_map/while/body/eval_jaxpr/ppermute | solution.py:12
  47.9 10.8 %collective-permute-start = (bf16[32,2,256]{2,1,0:T(2,128)(2,1)S(1)}, bf16[32,2,256]{2,1,0:T(2,128)(2,1)S(1)}, u32[]{:S(2)}, u32[]{:S(2)}) collective-permute-start(bf16[32,2,256]{2,1,0:T(2,128)(2,1)S(1)} %copy.51), channel_id=1, source_target_pairs={{0,16},{16,32},{32,48},{48,64},{64,80},{80,96},{96,112},{112,128},... | collective-permute-start | bytes 98312 | tf_op jit(solution)/shard_map/while/body/eval_jaxpr/ppermute | solution.py:12
  61.2 11.6 %collective-permute-start.1 = (f32[32,2,256]{2,0,1:T(8,128)S(1)}, f32[32,2,256]{2,0,1:T(8,128)S(1)}, u32[]{:S(2)}, u32[]{:S(2)}) collective-permute-start(f32[32,2,256]{2,0,1:T(8,128)S(1)} %add.73), channel_id=1, source_target_pairs={{0,16},{16,32},{32,48},{48,64},{64,80},{80,96},{96,112},{112,128},... | collective-permute-start | bytes 196616 | tf_op jit(solution)/shard_map/while/body/eval_jaxpr/ppermute | solution.py:12
  63.2 9.7 %collective-permute-start = (bf16[32,2,256]{2,1,0:T(2,128)(2,1)S(1)}, bf16[32,2,256]{2,1,0:T(2,128)(2,1)S(1)}, u32[]{:S(2)}, u32[]{:S(2)}) collective-permute-start(bf16[32,2,256]{2,1,0:T(2,128)(2,1)S(1)} %copy.51), channel_id=1, source_target_pairs={{0,16},{16,32},{32,48},{48,64},{64,80},{80,96},{96,112},{112,128},... | collective-permute-start | bytes 98312 | tf_op jit(solution)/shard_map/while/body/eval_jaxpr/ppermute | solution.py:12
  75.3 11.6 %collective-permute-start.1 = (f32[32,2,256]{2,0,1:T(8,128)S(1)}, f32[32,2,256]{2,0,1:T(8,128)S(1)}, u32[]{:S(2)}, u32[]{:S(2)}) collective-permute-start(f32[32,2,256]{2,0,1:T(8,128)S(1)} %add.73), channel_id=1, source_target_pairs={{0,16},{16,32},{32,48},{48,64},{64,80},{80,96},{96,112},{112,128},... | collective-permute-start | bytes 196616 | tf_op jit(solution)/shard_map/while/body/eval_jaxpr/ppermute | solution.py:12
  77.3 9.7 %collective-permute-start = (bf16[32,2,256]{2,1,0:T(2,128)(2,1)S(1)}, bf16[32,2,256]{2,1,0:T(2,128)(2,1)S(1)}, u32[]{:S(2)}, u32[]{:S(2)}) collective-permute-start(bf16[32,2,256]{2,1,0:T(2,128)(2,1)S(1)} %copy.51), channel_id=1, source_target_pairs={{0,16},{16,32},{32,48},{48,64},{64,80},{80,96},{96,112},{112,128},... | collective-permute-start | bytes 98312 | tf_op jit(solution)/shard_map/while/body/eval_jaxpr/ppermute | solution.py:12
  89.4 11.6 %collective-permute-start.1 = (f32[32,2,256]{2,0,1:T(8,128)S(1)}, f32[32,2,256]{2,0,1:T(8,128)S(1)}, u32[]{:S(2)}, u32[]{:S(2)}) collective-permute-start(f32[32,2,256]{2,0,1:T(8,128)S(1)} %add.73), channel_id=1, source_target_pairs={{0,16},{16,32},{32,48},{48,64},{64,80},{80,96},{96,112},{112,128},... | collective-permute-start | bytes 196616 | tf_op jit(solution)/shard_map/while/body/eval_jaxpr/ppermute | solution.py:12
  91.4 9.7 %collective-permute-start = (bf16[32,2,256]{2,1,0:T(2,128)(2,1)S(1)}, bf16[32,2,256]{2,1,0:T(2,128)(2,1)S(1)}, u32[]{:S(2)}, u32[]{:S(2)}) collective-permute-start(bf16[32,2,256]{2,1,0:T(2,128)(2,1)S(1)} %copy.51), channel_id=1, source_target_pairs={{0,16},{16,32},{32,48},{48,64},{64,80},{80,96},{96,112},{112,128},... | collective-permute-start | bytes 98312 | tf_op jit(solution)/shard_map/while/body/eval_jaxpr/ppermute | solution.py:12
  103.5 11.6 %collective-permute-start.1 = (f32[32,2,256]{2,0,1:T(8,128)S(1)}, f32[32,2,256]{2,0,1:T(8,128)S(1)}, u32[]{:S(2)}, u32[]{:S(2)}) collective-permute-start(f32[32,2,256]{2,0,1:T(8,128)S(1)} %add.73), channel_id=1, source_target_pairs={{0,16},{16,32},{32,48},{48,64},{64,80},{80,96},{96,112},{112,128},... | collective-permute-start | bytes 196616 | tf_op jit(solution)/shard_map/while/body/eval_jaxpr/ppermute | solution.py:12
  105.5 9.7 %collective-permute-start = (bf16[32,2,256]{2,1,0:T(2,128)(2,1)S(1)}, bf16[32,2,256]{2,1,0:T(2,128)(2,1)S(1)}, u32[]{:S(2)}, u32[]{:S(2)}) collective-permute-start(bf16[32,2,256]{2,1,0:T(2,128)(2,1)S(1)} %copy.51), channel_id=1, source_target_pairs={{0,16},{16,32},{32,48},{48,64},{64,80},{80,96},{96,112},{112,128},... | collective-permute-start | bytes 98312 | tf_op jit(solution)/shard_map/while/body/eval_jaxpr/ppermute | solution.py:12
  117.7 11.6 %collective-permute-start.1 = (f32[32,2,256]{2,0,1:T(8,128)S(1)}, f32[32,2,256]{2,0,1:T(8,128)S(1)}, u32[]{:S(2)}, u32[]{:S(2)}) collective-permute-start(f32[32,2,256]{2,0,1:T(8,128)S(1)} %add.73), channel_id=1, source_target_pairs={{0,16},{16,32},{32,48},{48,64},{64,80},{80,96},{96,112},{112,128},... | collective-permute-start | bytes 196616 | tf_op jit(solution)/shard_map/while/body/eval_jaxpr/ppermute | solution.py:12
  119.6 9.7 %collective-permute-start = (bf16[32,2,256]{2,1,0:T(2,128)(2,1)S(1)}, bf16[32,2,256]{2,1,0:T(2,128)(2,1)S(1)}, u32[]{:S(2)}, u32[]{:S(2)}) collective-permute-start(bf16[32,2,256]{2,1,0:T(2,128)(2,1)S(1)} %copy.51), channel_id=1, source_target_pairs={{0,16},{16,32},{32,48},{48,64},{64,80},{80,96},{96,112},{112,128},... | collective-permute-start | bytes 98312 | tf_op jit(solution)/shard_map/while/body/eval_jaxpr/ppermute | solution.py:12
  131.8 11.9 %collective-permute-start.1 = (f32[32,2,256]{2,0,1:T(8,128)S(1)}, f32[32,2,256]{2,0,1:T(8,128)S(1)}, u32[]{:S(2)}, u32[]{:S(2)}) collective-permute-start(f32[32,2,256]{2,0,1:T(8,128)S(1)} %add.73), channel_id=1, source_target_pairs={{0,16},{16,32},{32,48},{48,64},{64,80},{80,96},{96,112},{112,128},... | collective-permute-start | bytes 196616 | tf_op jit(solution)/shard_map/while/body/eval_jaxpr/ppermute | solution.py:12
  133.7 10.0 %collective-permute-start = (bf16[32,2,256]{2,1,0:T(2,128)(2,1)S(1)}, bf16[32,2,256]{2,1,0:T(2,128)(2,1)S(1)}, u32[]{:S(2)}, u32[]{:S(2)}) collective-permute-start(bf16[32,2,256]{2,1,0:T(2,128)(2,1)S(1)} %copy.51), channel_id=1, source_target_pairs={{0,16},{16,32},{32,48},{48,64},{64,80},{80,96},{96,112},{112,128},... | collective-permute-start | bytes 98312 | tf_op jit(solution)/shard_map/while/body/eval_jaxpr/ppermute | solution.py:12
  146.1 11.4 %collective-permute-start.1 = (f32[32,2,256]{2,0,1:T(8,128)S(1)}, f32[32,2,256]{2,0,1:T(8,128)S(1)}, u32[]{:S(2)}, u32[]{:S(2)}) collective-permute-start(f32[32,2,256]{2,0,1:T(8,128)S(1)} %add.73), channel_id=1, source_target_pairs={{0,16},{16,32},{32,48},{48,64},{64,80},{80,96},{96,112},{112,128},... | collective-permute-start | bytes 196616 | tf_op jit(solution)/shard_map/while/body/eval_jaxpr/ppermute | solution.py:12
  148.1 9.5 %collective-permute-start = (bf16[32,2,256]{2,1,0:T(2,128)(2,1)S(1)}, bf16[32,2,256]{2,1,0:T(2,128)(2,1)S(1)}, u32[]{:S(2)}, u32[]{:S(2)}) collective-permute-start(bf16[32,2,256]{2,1,0:T(2,128)(2,1)S(1)} %copy.51), channel_id=1, source_target_pairs={{0,16},{16,32},{32,48},{48,64},{64,80},{80,96},{96,112},{112,128},... | collective-permute-start | bytes 98312 | tf_op jit(solution)/shard_map/while/body/eval_jaxpr/ppermute | solution.py:12
  160.0 11.9 %collective-permute-start.1 = (f32[32,2,256]{2,0,1:T(8,128)S(1)}, f32[32,2,256]{2,0,1:T(8,128)S(1)}, u32[]{:S(2)}, u32[]{:S(2)}) collective-permute-start(f32[32,2,256]{2,0,1:T(8,128)S(1)} %add.73), channel_id=1, source_target_pairs={{0,16},{16,32},{32,48},{48,64},{64,80},{80,96},{96,112},{112,128},... | collective-permute-start | bytes 196616 | tf_op jit(solution)/shard_map/while/body/eval_jaxpr/ppermute | solution.py:12
  161.9 10.0 %collective-permute-start = (bf16[32,2,256]{2,1,0:T(2,128)(2,1)S(1)}, bf16[32,2,256]{2,1,0:T(2,128)(2,1)S(1)}, u32[]{:S(2)}, u32[]{:S(2)}) collective-permute-start(bf16[32,2,256]{2,1,0:T(2,128)(2,1)S(1)} %copy.51), channel_id=1, source_target_pairs={{0,16},{16,32},{32,48},{48,64},{64,80},{80,96},{96,112},{112,128},... | collective-permute-start | bytes 98312 | tf_op jit(solution)/shard_map/while/body/eval_jaxpr/ppermute | solution.py:12
  174.4 11.6 %collective-permute-start.1 = (f32[32,2,256]{2,0,1:T(8,128)S(1)}, f32[32,2,256]{2,0,1:T(8,128)S(1)}, u32[]{:S(2)}, u32[]{:S(2)}) collective-permute-start(f32[32,2,256]{2,0,1:T(8,128)S(1)} %add.73), channel_id=1, source_target_pairs={{0,16},{16,32},{32,48},{48,64},{64,80},{80,96},{96,112},{112,128},... | collective-permute-start | bytes 196616 | tf_op jit(solution)/shard_map/while/body/eval_jaxpr/ppermute | solution.py:12
  176.3 9.7 %collective-permute-start = (bf16[32,2,256]{2,1,0:T(2,128)(2,1)S(1)}, bf16[32,2,256]{2,1,0:T(2,128)(2,1)S(1)}, u32[]{:S(2)}, u32[]{:S(2)}) collective-permute-start(bf16[32,2,256]{2,1,0:T(2,128)(2,1)S(1)} %copy.51), channel_id=1, source_target_pairs={{0,16},{16,32},{32,48},{48,64},{64,80},{80,96},{96,112},{112,128},... | collective-permute-start | bytes 98312 | tf_op jit(solution)/shard_map/while/body/eval_jaxpr/ppermute | solution.py:12
  188.5 11.6 %collective-permute-start.1 = (f32[32,2,256]{2,0,1:T(8,128)S(1)}, f32[32,2,256]{2,0,1:T(8,128)S(1)}, u32[]{:S(2)}, u32[]{:S(2)}) collective-permute-start(f32[32,2,256]{2,0,1:T(8,128)S(1)} %add.73), channel_id=1, source_target_pairs={{0,16},{16,32},{32,48},{48,64},{64,80},{80,96},{96,112},{112,128},... | collective-permute-start | bytes 196616 | tf_op jit(solution)/shard_map/while/body/eval_jaxpr/ppermute | solution.py:12
  190.4 9.7 %collective-permute-start = (bf16[32,2,256]{2,1,0:T(2,128)(2,1)S(1)}, bf16[32,2,256]{2,1,0:T(2,128)(2,1)S(1)}, u32[]{:S(2)}, u32[]{:S(2)}) collective-permute-start(bf16[32,2,256]{2,1,0:T(2,128)(2,1)S(1)} %copy.51), channel_id=1, source_target_pairs={{0,16},{16,32},{32,48},{48,64},{64,80},{80,96},{96,112},{112,128},... | collective-permute-start | bytes 98312 | tf_op jit(solution)/shard_map/while/body/eval_jaxpr/ppermute | solution.py:12
  202.6 11.6 %collective-permute-start.1 = (f32[32,2,256]{2,0,1:T(8,128)S(1)}, f32[32,2,256]{2,0,1:T(8,128)S(1)}, u32[]{:S(2)}, u32[]{:S(2)}) collective-permute-start(f32[32,2,256]{2,0,1:T(8,128)S(1)} %add.73), channel_id=1, source_target_pairs={{0,16},{16,32},{32,48},{48,64},{64,80},{80,96},{96,112},{112,128},... | collective-permute-start | bytes 196616 | tf_op jit(solution)/shard_map/while/body/eval_jaxpr/ppermute | solution.py:12
  204.5 9.7 %collective-permute-start = (bf16[32,2,256]{2,1,0:T(2,128)(2,1)S(1)}, bf16[32,2,256]{2,1,0:T(2,128)(2,1)S(1)}, u32[]{:S(2)}, u32[]{:S(2)}) collective-permute-start(bf16[32,2,256]{2,1,0:T(2,128)(2,1)S(1)} %copy.51), channel_id=1, source_target_pairs={{0,16},{16,32},{32,48},{48,64},{64,80},{80,96},{96,112},{112,128},... | collective-permute-start | bytes 98312 | tf_op jit(solution)/shard_map/while/body/eval_jaxpr/ppermute | solution.py:12
  216.7 11.6 %collective-permute-start.1 = (f32[32,2,256]{2,0,1:T(8,128)S(1)}, f32[32,2,256]{2,0,1:T(8,128)S(1)}, u32[]{:S(2)}, u32[]{:S(2)}) collective-permute-start(f32[32,2,256]{2,0,1:T(8,128)S(1)} %add.73), channel_id=1, source_target_pairs={{0,16},{16,32},{32,48},{48,64},{64,80},{80,96},{96,112},{112,128},... | collective-permute-start | bytes 196616 | tf_op jit(solution)/shard_map/while/body/eval_jaxpr/ppermute | solution.py:12
  218.6 9.7 %collective-permute-start = (bf16[32,2,256]{2,1,0:T(2,128)(2,1)S(1)}, bf16[32,2,256]{2,1,0:T(2,128)(2,1)S(1)}, u32[]{:S(2)}, u32[]{:S(2)}) collective-permute-start(bf16[32,2,256]{2,1,0:T(2,128)(2,1)S(1)} %copy.51), channel_id=1, source_target_pairs={{0,16},{16,32},{32,48},{48,64},{64,80},{80,96},{96,112},{112,128},... | collective-permute-start | bytes 98312 | tf_op jit(solution)/shard_map/while/body/eval_jaxpr/ppermute | solution.py:12
  230.8 11.6 %collective-permute-start.1 = (f32[32,2,256]{2,0,1:T(8,128)S(1)}, f32[32,2,256]{2,0,1:T(8,128)S(1)}, u32[]{:S(2)}, u32[]{:S(2)}) collective-permute-start(f32[32,2,256]{2,0,1:T(8,128)S(1)} %add.73), channel_id=1, source_target_pairs={{0,16},{16,32},{32,48},{48,64},{64,80},{80,96},{96,112},{112,128},... | collective-permute-start | bytes 196616 | tf_op jit(solution)/shard_map/while/body/eval_jaxpr/ppermute | solution.py:12
  232.7 9.7 %collective-permute-start = (bf16[32,2,256]{2,1,0:T(2,128)(2,1)S(1)}, bf16[32,2,256]{2,1,0:T(2,128)(2,1)S(1)}, u32[]{:S(2)}, u32[]{:S(2)}) collective-permute-start(bf16[32,2,256]{2,1,0:T(2,128)(2,1)S(1)} %copy.51), channel_id=1, source_target_pairs={{0,16},{16,32},{32,48},{48,64},{64,80},{80,96},{96,112},{112,128},... | collective-permute-start | bytes 98312 | tf_op jit(solution)/shard_map/while/body/eval_jaxpr/ppermute | solution.py:12
  244.9 11.6 %collective-permute-start.1 = (f32[32,2,256]{2,0,1:T(8,128)S(1)}, f32[32,2,256]{2,0,1:T(8,128)S(1)}, u32[]{:S(2)}, u32[]{:S(2)}) collective-permute-start(f32[32,2,256]{2,0,1:T(8,128)S(1)} %add.73), channel_id=1, source_target_pairs={{0,16},{16,32},{32,48},{48,64},{64,80},{80,96},{96,112},{112,128},... | collective-permute-start | bytes 196616 | tf_op jit(solution)/shard_map/while/body/eval_jaxpr/ppermute | solution.py:12
  246.8 9.7 %collective-permute-start = (bf16[32,2,256]{2,1,0:T(2,128)(2,1)S(1)}, bf16[32,2,256]{2,1,0:T(2,128)(2,1)S(1)}, u32[]{:S(2)}, u32[]{:S(2)}) collective-permute-start(bf16[32,2,256]{2,1,0:T(2,128)(2,1)S(1)} %copy.51), channel_id=1, source_target_pairs={{0,16},{16,32},{32,48},{48,64},{64,80},{80,96},{96,112},{112,128},... | collective-permute-start | bytes 98312 | tf_op jit(solution)/shard_map/while/body/eval_jaxpr/ppermute | solution.py:12
  259.0 11.6 %collective-permute-start.1 = (f32[32,2,256]{2,0,1:T(8,128)S(1)}, f32[32,2,256]{2,0,1:T(8,128)S(1)}, u32[]{:S(2)}, u32[]{:S(2)}) collective-permute-start(f32[32,2,256]{2,0,1:T(8,128)S(1)} %add.73), channel_id=1, source_target_pairs={{0,16},{16,32},{32,48},{48,64},{64,80},{80,96},{96,112},{112,128},... | collective-permute-start | bytes 196616 | tf_op jit(solution)/shard_map/while/body/eval_jaxpr/ppermute | solution.py:12
  260.9 9.7 %collective-permute-start = (bf16[32,2,256]{2,1,0:T(2,128)(2,1)S(1)}, bf16[32,2,256]{2,1,0:T(2,128)(2,1)S(1)}, u32[]{:S(2)}, u32[]{:S(2)}) collective-permute-start(bf16[32,2,256]{2,1,0:T(2,128)(2,1)S(1)} %copy.51), channel_id=1, source_target_pairs={{0,16},{16,32},{32,48},{48,64},{64,80},{80,96},{96,112},{112,128},... | collective-permute-start | bytes 98312 | tf_op jit(solution)/shard_map/while/body/eval_jaxpr/ppermute | solution.py:12
  273.1 11.6 %collective-permute-start.1 = (f32[32,2,256]{2,0,1:T(8,128)S(1)}, f32[32,2,256]{2,0,1:T(8,128)S(1)}, u32[]{:S(2)}, u32[]{:S(2)}) collective-permute-start(f32[32,2,256]{2,0,1:T(8,128)S(1)} %add.73), channel_id=1, source_target_pairs={{0,16},{16,32},{32,48},{48,64},{64,80},{80,96},{96,112},{112,128},... | collective-permute-start | bytes 196616 | tf_op jit(solution)/shard_map/while/body/eval_jaxpr/ppermute | solution.py:12
  275.0 9.7 %collective-permute-start = (bf16[32,2,256]{2,1,0:T(2,128)(2,1)S(1)}, bf16[32,2,256]{2,1,0:T(2,128)(2,1)S(1)}, u32[]{:S(2)}, u32[]{:S(2)}) collective-permute-start(bf16[32,2,256]{2,1,0:T(2,128)(2,1)S(1)} %copy.51), channel_id=1, source_target_pairs={{0,16},{16,32},{32,48},{48,64},{64,80},{80,96},{96,112},{112,128},... | collective-permute-start | bytes 98312 | tf_op jit(solution)/shard_map/while/body/eval_jaxpr/ppermute | solution.py:12
  287.2 11.6 %collective-permute-start.1 = (f32[32,2,256]{2,0,1:T(8,128)S(1)}, f32[32,2,256]{2,0,1:T(8,128)S(1)}, u32[]{:S(2)}, u32[]{:S(2)}) collective-permute-start(f32[32,2,256]{2,0,1:T(8,128)S(1)} %add.73), channel_id=1, source_target_pairs={{0,16},{16,32},{32,48},{48,64},{64,80},{80,96},{96,112},{112,128},... | collective-permute-start | bytes 196616 | tf_op jit(solution)/shard_map/while/body/eval_jaxpr/ppermute | solution.py:12
  289.1 9.7 %collective-permute-start = (bf16[32,2,256]{2,1,0:T(2,128)(2,1)S(1)}, bf16[32,2,256]{2,1,0:T(2,128)(2,1)S(1)}, u32[]{:S(2)}, u32[]{:S(2)}) collective-permute-start(bf16[32,2,256]{2,1,0:T(2,128)(2,1)S(1)} %copy.51), channel_id=1, source_target_pairs={{0,16},{16,32},{32,48},{48,64},{64,80},{80,96},{96,112},{112,128},... | collective-permute-start | bytes 98312 | tf_op jit(solution)/shard_map/while/body/eval_jaxpr/ppermute | solution.py:12
  301.3 11.9 %collective-permute-start.1 = (f32[32,2,256]{2,0,1:T(8,128)S(1)}, f32[32,2,256]{2,0,1:T(8,128)S(1)}, u32[]{:S(2)}, u32[]{:S(2)}) collective-permute-start(f32[32,2,256]{2,0,1:T(8,128)S(1)} %add.73), channel_id=1, source_target_pairs={{0,16},{16,32},{32,48},{48,64},{64,80},{80,96},{96,112},{112,128},... | collective-permute-start | bytes 196616 | tf_op jit(solution)/shard_map/while/body/eval_jaxpr/ppermute | solution.py:12
  303.2 10.0 %collective-permute-start = (bf16[32,2,256]{2,1,0:T(2,128)(2,1)S(1)}, bf16[32,2,256]{2,1,0:T(2,128)(2,1)S(1)}, u32[]{:S(2)}, u32[]{:S(2)}) collective-permute-start(bf16[32,2,256]{2,1,0:T(2,128)(2,1)S(1)} %copy.51), channel_id=1, source_target_pairs={{0,16},{16,32},{32,48},{48,64},{64,80},{80,96},{96,112},{112,128},... | collective-permute-start | bytes 98312 | tf_op jit(solution)/shard_map/while/body/eval_jaxpr/ppermute | solution.py:12
  315.7 11.4 %collective-permute-start.1 = (f32[32,2,256]{2,0,1:T(8,128)S(1)}, f32[32,2,256]{2,0,1:T(8,128)S(1)}, u32[]{:S(2)}, u32[]{:S(2)}) collective-permute-start(f32[32,2,256]{2,0,1:T(8,128)S(1)} %add.73), channel_id=1, source_target_pairs={{0,16},{16,32},{32,48},{48,64},{64,80},{80,96},{96,112},{112,128},... | collective-permute-start | bytes 196616 | tf_op jit(solution)/shard_map/while/body/eval_jaxpr/ppermute | solution.py:12
  317.6 9.4 %collective-permute-start = (bf16[32,2,256]{2,1,0:T(2,128)(2,1)S(1)}, bf16[32,2,256]{2,1,0:T(2,128)(2,1)S(1)}, u32[]{:S(2)}, u32[]{:S(2)}) collective-permute-start(bf16[32,2,256]{2,1,0:T(2,128)(2,1)S(1)} %copy.51), channel_id=1, source_target_pairs={{0,16},{16,32},{32,48},{48,64},{64,80},{80,96},{96,112},{112,128},... | collective-permute-start | bytes 98312 | tf_op jit(solution)/shard_map/while/body/eval_jaxpr/ppermute | solution.py:12
  329.5 11.9 %collective-permute-start.1 = (f32[32,2,256]{2,0,1:T(8,128)S(1)}, f32[32,2,256]{2,0,1:T(8,128)S(1)}, u32[]{:S(2)}, u32[]{:S(2)}) collective-permute-start(f32[32,2,256]{2,0,1:T(8,128)S(1)} %add.73), channel_id=1, source_target_pairs={{0,16},{16,32},{32,48},{48,64},{64,80},{80,96},{96,112},{112,128},... | collective-permute-start | bytes 196616 | tf_op jit(solution)/shard_map/while/body/eval_jaxpr/ppermute | solution.py:12
  331.4 10.0 %collective-permute-start = (bf16[32,2,256]{2,1,0:T(2,128)(2,1)S(1)}, bf16[32,2,256]{2,1,0:T(2,128)(2,1)S(1)}, u32[]{:S(2)}, u32[]{:S(2)}) collective-permute-start(bf16[32,2,256]{2,1,0:T(2,128)(2,1)S(1)} %copy.51), channel_id=1, source_target_pairs={{0,16},{16,32},{32,48},{48,64},{64,80},{80,96},{96,112},{112,128},... | collective-permute-start | bytes 98312 | tf_op jit(solution)/shard_map/while/body/eval_jaxpr/ppermute | solution.py:12
  343.9 11.7 %collective-permute-start.1 = (f32[32,2,256]{2,0,1:T(8,128)S(1)}, f32[32,2,256]{2,0,1:T(8,128)S(1)}, u32[]{:S(2)}, u32[]{:S(2)}) collective-permute-start(f32[32,2,256]{2,0,1:T(8,128)S(1)} %add.73), channel_id=1, source_target_pairs={{0,16},{16,32},{32,48},{48,64},{64,80},{80,96},{96,112},{112,128},... | collective-permute-start | bytes 196616 | tf_op jit(solution)/shard_map/while/body/eval_jaxpr/ppermute | solution.py:12
  345.8 9.7 %collective-permute-start = (bf16[32,2,256]{2,1,0:T(2,128)(2,1)S(1)}, bf16[32,2,256]{2,1,0:T(2,128)(2,1)S(1)}, u32[]{:S(2)}, u32[]{:S(2)}) collective-permute-start(bf16[32,2,256]{2,1,0:T(2,128)(2,1)S(1)} %copy.51), channel_id=1, source_target_pairs={{0,16},{16,32},{32,48},{48,64},{64,80},{80,96},{96,112},{112,128},... | collective-permute-start | bytes 98312 | tf_op jit(solution)/shard_map/while/body/eval_jaxpr/ppermute | solution.py:12
  358.0 11.7 %collective-permute-start.1 = (f32[32,2,256]{2,0,1:T(8,128)S(1)}, f32[32,2,256]{2,0,1:T(8,128)S(1)}, u32[]{:S(2)}, u32[]{:S(2)}) collective-permute-start(f32[32,2,256]{2,0,1:T(8,128)S(1)} %add.73), channel_id=1, source_target_pairs={{0,16},{16,32},{32,48},{48,64},{64,80},{80,96},{96,112},{112,128},... | collective-permute-start | bytes 196616 | tf_op jit(solution)/shard_map/while/body/eval_jaxpr/ppermute | solution.py:12
  359.9 9.7 %collective-permute-start = (bf16[32,2,256]{2,1,0:T(2,128)(2,1)S(1)}, bf16[32,2,256]{2,1,0:T(2,128)(2,1)S(1)}, u32[]{:S(2)}, u32[]{:S(2)}) collective-permute-start(bf16[32,2,256]{2,1,0:T(2,128)(2,1)S(1)} %copy.51), channel_id=1, source_target_pairs={{0,16},{16,32},{32,48},{48,64},{64,80},{80,96},{96,112},{112,128},... | collective-permute-start | bytes 98312 | tf_op jit(solution)/shard_map/while/body/eval_jaxpr/ppermute | solution.py:12
  372.1 11.7 %collective-permute-start.1 = (f32[32,2,256]{2,0,1:T(8,128)S(1)}, f32[32,2,256]{2,0,1:T(8,128)S(1)}, u32[]{:S(2)}, u32[]{:S(2)}) collective-permute-start(f32[32,2,256]{2,0,1:T(8,128)S(1)} %add.73), channel_id=1, source_target_pairs={{0,16},{16,32},{32,48},{48,64},{64,80},{80,96},{96,112},{112,128},... | collective-permute-start | bytes 196616 | tf_op jit(solution)/shard_map/while/body/eval_jaxpr/ppermute | solution.py:12
  374.0 9.7 %collective-permute-start = (bf16[32,2,256]{2,1,0:T(2,128)(2,1)S(1)}, bf16[32,2,256]{2,1,0:T(2,128)(2,1)S(1)}, u32[]{:S(2)}, u32[]{:S(2)}) collective-permute-start(bf16[32,2,256]{2,1,0:T(2,128)(2,1)S(1)} %copy.51), channel_id=1, source_target_pairs={{0,16},{16,32},{32,48},{48,64},{64,80},{80,96},{96,112},{112,128},... | collective-permute-start | bytes 98312 | tf_op jit(solution)/shard_map/while/body/eval_jaxpr/ppermute | solution.py:12
  386.2 11.7 %collective-permute-start.1 = (f32[32,2,256]{2,0,1:T(8,128)S(1)}, f32[32,2,256]{2,0,1:T(8,128)S(1)}, u32[]{:S(2)}, u32[]{:S(2)}) collective-permute-start(f32[32,2,256]{2,0,1:T(8,128)S(1)} %add.73), channel_id=1, source_target_pairs={{0,16},{16,32},{32,48},{48,64},{64,80},{80,96},{96,112},{112,128},... | collective-permute-start | bytes 196616 | tf_op jit(solution)/shard_map/while/body/eval_jaxpr/ppermute | solution.py:12
  388.1 9.7 %collective-permute-start = (bf16[32,2,256]{2,1,0:T(2,128)(2,1)S(1)}, bf16[32,2,256]{2,1,0:T(2,128)(2,1)S(1)}, u32[]{:S(2)}, u32[]{:S(2)}) collective-permute-start(bf16[32,2,256]{2,1,0:T(2,128)(2,1)S(1)} %copy.51), channel_id=1, source_target_pairs={{0,16},{16,32},{32,48},{48,64},{64,80},{80,96},{96,112},{112,128},... | collective-permute-start | bytes 98312 | tf_op jit(solution)/shard_map/while/body/eval_jaxpr/ppermute | solution.py:12
  400.3 11.7 %collective-permute-start.1 = (f32[32,2,256]{2,0,1:T(8,128)S(1)}, f32[32,2,256]{2,0,1:T(8,128)S(1)}, u32[]{:S(2)}, u32[]{:S(2)}) collective-permute-start(f32[32,2,256]{2,0,1:T(8,128)S(1)} %add.73), channel_id=1, source_target_pairs={{0,16},{16,32},{32,48},{48,64},{64,80},{80,96},{96,112},{112,128},... | collective-permute-start | bytes 196616 | tf_op jit(solution)/shard_map/while/body/eval_jaxpr/ppermute | solution.py:12
  402.2 9.7 %collective-permute-start = (bf16[32,2,256]{2,1,0:T(2,128)(2,1)S(1)}, bf16[32,2,256]{2,1,0:T(2,128)(2,1)S(1)}, u32[]{:S(2)}, u32[]{:S(2)}) collective-permute-start(bf16[32,2,256]{2,1,0:T(2,128)(2,1)S(1)} %copy.51), channel_id=1, source_target_pairs={{0,16},{16,32},{32,48},{48,64},{64,80},{80,96},{96,112},{112,128},... | collective-permute-start | bytes 98312 | tf_op jit(solution)/shard_map/while/body/eval_jaxpr/ppermute | solution.py:12
  414.4 11.7 %collective-permute-start.1 = (f32[32,2,256]{2,0,1:T(8,128)S(1)}, f32[32,2,256]{2,0,1:T(8,128)S(1)}, u32[]{:S(2)}, u32[]{:S(2)}) collective-permute-start(f32[32,2,256]{2,0,1:T(8,128)S(1)} %add.73), channel_id=1, source_target_pairs={{0,16},{16,32},{32,48},{48,64},{64,80},{80,96},{96,112},{112,128},... | collective-permute-start | bytes 196616 | tf_op jit(solution)/shard_map/while/body/eval_jaxpr/ppermute | solution.py:12
  416.3 9.7 %collective-permute-start = (bf16[32,2,256]{2,1,0:T(2,128)(2,1)S(1)}, bf16[32,2,256]{2,1,0:T(2,128)(2,1)S(1)}, u32[]{:S(2)}, u32[]{:S(2)}) collective-permute-start(bf16[32,2,256]{2,1,0:T(2,128)(2,1)S(1)} %copy.51), channel_id=1, source_target_pairs={{0,16},{16,32},{32,48},{48,64},{64,80},{80,96},{96,112},{112,128},... | collective-permute-start | bytes 98312 | tf_op jit(solution)/shard_map/while/body/eval_jaxpr/ppermute | solution.py:12
  428.5 11.7 %collective-permute-start.1 = (f32[32,2,256]{2,0,1:T(8,128)S(1)}, f32[32,2,256]{2,0,1:T(8,128)S(1)}, u32[]{:S(2)}, u32[]{:S(2)}) collective-permute-start(f32[32,2,256]{2,0,1:T(8,128)S(1)} %add.73), channel_id=1, source_target_pairs={{0,16},{16,32},{32,48},{48,64},{64,80},{80,96},{96,112},{112,128},... | collective-permute-start | bytes 196616 | tf_op jit(solution)/shard_map/while/body/eval_jaxpr/ppermute | solution.py:12
  430.4 9.7 %collective-permute-start = (bf16[32,2,256]{2,1,0:T(2,128)(2,1)S(1)}, bf16[32,2,256]{2,1,0:T(2,128)(2,1)S(1)}, u32[]{:S(2)}, u32[]{:S(2)}) collective-permute-start(bf16[32,2,256]{2,1,0:T(2,128)(2,1)S(1)} %copy.51), channel_id=1, source_target_pairs={{0,16},{16,32},{32,48},{48,64},{64,80},{80,96},{96,112},{112,128},... | collective-permute-start | bytes 98312 | tf_op jit(solution)/shard_map/while/body/eval_jaxpr/ppermute | solution.py:12
  442.6 11.7 %collective-permute-start.1 = (f32[32,2,256]{2,0,1:T(8,128)S(1)}, f32[32,2,256]{2,0,1:T(8,128)S(1)}, u32[]{:S(2)}, u32[]{:S(2)}) collective-permute-start(f32[32,2,256]{2,0,1:T(8,128)S(1)} %add.73), channel_id=1, source_target_pairs={{0,16},{16,32},{32,48},{48,64},{64,80},{80,96},{96,112},{112,128},... | collective-permute-start | bytes 196616 | tf_op jit(solution)/shard_map/while/body/eval_jaxpr/ppermute | solution.py:12
  444.5 9.7 %collective-permute-start = (bf16[32,2,256]{2,1,0:T(2,128)(2,1)S(1)}, bf16[32,2,256]{2,1,0:T(2,128)(2,1)S(1)}, u32[]{:S(2)}, u32[]{:S(2)}) collective-permute-start(bf16[32,2,256]{2,1,0:T(2,128)(2,1)S(1)} %copy.51), channel_id=1, source_target_pairs={{0,16},{16,32},{32,48},{48,64},{64,80},{80,96},{96,112},{112,128},... | collective-permute-start | bytes 98312 | tf_op jit(solution)/shard_map/while/body/eval_jaxpr/ppermute | solution.py:12
  456.7 11.7 %collective-permute-start.1 = (f32[32,2,256]{2,0,1:T(8,128)S(1)}, f32[32,2,256]{2,0,1:T(8,128)S(1)}, u32[]{:S(2)}, u32[]{:S(2)}) collective-permute-start(f32[32,2,256]{2,0,1:T(8,128)S(1)} %add.73), channel_id=1, source_target_pairs={{0,16},{16,32},{32,48},{48,64},{64,80},{80,96},{96,112},{112,128},... | collective-permute-start | bytes 196616 | tf_op jit(solution)/shard_map/while/body/eval_jaxpr/ppermute | solution.py:12
  458.6 9.7 %collective-permute-start = (bf16[32,2,256]{2,1,0:T(2,128)(2,1)S(1)}, bf16[32,2,256]{2,1,0:T(2,128)(2,1)S(1)}, u32[]{:S(2)}, u32[]{:S(2)}) collective-permute-start(bf16[32,2,256]{2,1,0:T(2,128)(2,1)S(1)} %copy.51), channel_id=1, source_target_pairs={{0,16},{16,32},{32,48},{48,64},{64,80},{80,96},{96,112},{112,128},... | collective-permute-start | bytes 98312 | tf_op jit(solution)/shard_map/while/body/eval_jaxpr/ppermute | solution.py:12
  470.8 11.7 %collective-permute-start.1 = (f32[32,2,256]{2,0,1:T(8,128)S(1)}, f32[32,2,256]{2,0,1:T(8,128)S(1)}, u32[]{:S(2)}, u32[]{:S(2)}) collective-permute-start(f32[32,2,256]{2,0,1:T(8,128)S(1)} %add.73), channel_id=1, source_target_pairs={{0,16},{16,32},{32,48},{48,64},{64,80},{80,96},{96,112},{112,128},... | collective-permute-start | bytes 196616 | tf_op jit(solution)/shard_map/while/body/eval_jaxpr/ppermute | solution.py:12
  472.8 9.7 %collective-permute-start = (bf16[32,2,256]{2,1,0:T(2,128)(2,1)S(1)}, bf16[32,2,256]{2,1,0:T(2,128)(2,1)S(1)}, u32[]{:S(2)}, u32[]{:S(2)}) collective-permute-start(bf16[32,2,256]{2,1,0:T(2,128)(2,1)S(1)} %copy.51), channel_id=1, source_target_pairs={{0,16},{16,32},{32,48},{48,64},{64,80},{80,96},{96,112},{112,128},... | collective-permute-start | bytes 98312 | tf_op jit(solution)/shard_map/while/body/eval_jaxpr/ppermute | solution.py:12
  (8 other events, 509.6 us)
Sparse Core Ops, SparseCore 0:
  484.9 29.9 reduce-scatter.1
where the time goes:
time: 526 us; the launch traced here: 523 us
  waiting for transfers between devices  275 us (52%)
  starting transfers between devices  129 us (25%)
  matrix products  64.6 us (12%)
  local copies, waits for them, and re-layouts  19.2 us (4%)
  between operations  13.5 us (3%)
  blocking collectives  12.5 us (2%)
  other arithmetic  8.63 us (2%)
    ppermute x64, waiting for transfers between devices, passed_along(): return lax.ppermute(value, axis, pairs)  245 us
    ppermute x64, starting transfers between devices, passed_along(): return lax.ppermute(value, axis, pairs)  129 us
    dot_general x32, matrix products, attend_block(): jnp.einsum('ruhp,uphe->ruhe', weight, value_heads, preferred_element_type...  63.3 us
    reduce_scatter x1, waiting for transfers between devices, local(): lax.psum_scatter(partial_terms, 'head', scatter_dimension=1, tiled=True)  30.1 us
    all_gather x1, blocking collectives, local(): whole = lax.all_gather(cand_rows, 'head', axis=1, tiled=True)  12.5 us
  transfers between devices with their start and end apart: 65, of which 33 were waited for; matrix products, arithmetic and copies ran while one was open for 0% of the time, Pallas kernels for 0%

commit v1 on v0

v1 whole, which is shorter than its diff:
```python
import functools

import jax
import jax.numpy as jnp
from jax import lax
from jax.experimental import pallas as pl
from jax.experimental.pallas import tpu as pltpu
from jax.sharding import PartitionSpec as P

HEAD_DIM = 64
USERS = 2
VMEM = pl.BlockSpec(memory_space=pltpu.VMEM)
SMEM = pl.BlockSpec(memory_space=pltpu.SMEM)
PARAMS = pltpu.CompilerParams(vmem_limit_bytes=48 * 2**20)


def head_mask(shape, head):
    lane = lax.broadcasted_iota(jnp.int32, shape, len(shape) - 1)
    return (lane >= head * HEAD_DIM) & (lane < (head + 1) * HEAD_DIM)


def project_kernel(user_ref, cand_ref, weight_ref, query_ref, gate_ref):
    slices, rows, depth = cand_ref.shape
    width = weight_ref.shape[1] // 2
    total = jnp.zeros((rows, 2 * width), jnp.float32)
    for part in range(slices):
        total += jnp.dot(
            cand_ref[part],
            weight_ref[part * depth : (part + 1) * depth, :],
            preferred_element_type=jnp.float32,
        )
    projected = total / (1.0 + jnp.exp(-total))
    first = lax.broadcasted_iota(jnp.int32, (rows, rows), 0)
    second = lax.broadcasted_iota(jnp.int32, (rows, rows), 1)
    users = jnp.broadcast_to(user_ref[...], (rows, rows)).astype(jnp.bfloat16)
    before = jnp.dot(
        users, (first < second).astype(jnp.bfloat16), preferred_element_type=jnp.float32
    ).astype(jnp.int32)
    target = jnp.where(users > 0, rows // USERS + before, second - before)
    place = (target == first).astype(jnp.bfloat16)
    ordered = jnp.dot(
        place, projected.astype(jnp.bfloat16), preferred_element_type=jnp.float32
    )
    query = (ordered[:, :width] * (0.5 * HEAD_DIM**-0.5)).astype(jnp.bfloat16)
    for copy in range(query_ref.shape[0]):
        query_ref[copy] = query
    gate_ref[...] = ordered[:, width:].astype(jnp.bfloat16)


def attend_kernel(
    rows_now, positions_now, live_ref, query_ref, key_ref, value_ref, out_ref, keys, masked
):
    blocks, block_rows, width = query_ref.shape
    heads = width // HEAD_DIM
    positions = key_ref.shape[1]
    per_user = block_rows // USERS
    step_blocks = rows_now // per_user
    for user in range(USERS):
        keys[user] = key_ref[user].T
        position = lax.broadcasted_iota(jnp.int32, (positions, width), 0)
        value = value_ref[user]
        for head in range(heads):
            keep = (position < live_ref[user]) & head_mask((positions, width), head)
            masked[user, head * positions : (head + 1) * positions, :] = jnp.where(
                keep, value, jnp.zeros_like(value)
            )

        def step(index, carry, user=user):
            here = pl.ds(index * step_blocks, step_blocks)
            mine = slice(user * per_user, (user + 1) * per_user)
            query = query_ref[here, mine, :].reshape(rows_now, width)
            total = jnp.zeros((rows_now, width), jnp.float32)
            for start in range(0, positions, positions_now):
                for head in range(heads):
                    own = jnp.where(
                        head_mask((rows_now, width), head), query, jnp.zeros_like(query)
                    )
                    half = jnp.dot(
                        own,
                        keys[user, :, start : start + positions_now],
                        preferred_element_type=jnp.float32,
                    )
                    weight = (half + half * jnp.tanh(half)).astype(jnp.bfloat16)
                    at = head * positions + start
                    total += jnp.dot(
                        weight,
                        masked[user, at : at + positions_now, :],
                        preferred_element_type=jnp.float32,
                    )
            out_ref[here, mine, :] = total.astype(jnp.bfloat16).reshape(
                step_blocks, per_user, width
            )
            return carry

        lax.fori_loop(0, blocks // step_blocks, step, 0)


def finish_kernel(length_ref, user_ref, partial_ref, gate_ref, weight_ref, out_ref):
    blocks, rows, width = partial_ref.shape
    total = partial_ref[0].astype(jnp.float32)
    for block in range(1, blocks):
        total += partial_ref[block].astype(jnp.float32)
    row = lax.broadcasted_iota(jnp.int32, (rows, width), 0)
    length = jnp.where(row < rows // USERS, length_ref[0], length_ref[1]).astype(jnp.float32)
    attn = total / length
    square = attn * attn
    mean = jnp.zeros((rows, width), jnp.float32)
    for head in range(width // HEAD_DIM):
        mask = head_mask((rows, width), head)
        summed = jnp.sum(jnp.where(mask, square, 0.0), axis=1, keepdims=True)
        mean = jnp.where(mask, summed * (1.0 / HEAD_DIM), mean)
    normed = attn * lax.rsqrt(mean + 1e-06)
    gated = (normed * gate_ref[...].astype(jnp.float32)).astype(jnp.bfloat16)
    first = lax.broadcasted_iota(jnp.int32, (rows, rows), 0)
    second = lax.broadcasted_iota(jnp.int32, (rows, rows), 1)
    users = jnp.broadcast_to(user_ref[...], (rows, rows)).astype(jnp.bfloat16)
    before = jnp.dot(
        (second < first).astype(jnp.bfloat16), users, preferred_element_type=jnp.float32
    ).astype(jnp.int32)
    target = jnp.where(users > 0, rows // USERS + before, first - before)
    back = (target == second).astype(jnp.bfloat16)
    gated = jnp.dot(back, gated, preferred_element_type=jnp.float32).astype(jnp.bfloat16)
    for part in range(out_ref.shape[0]):
        out_ref[part] = jnp.dot(
            gated,
            weight_ref[:, part * width : (part + 1) * width],
            preferred_element_type=jnp.float32,
        )


def local(cand_rows, qu_weight, out_weight, keys, values, lengths, cand_user):
    rows, depth = cand_rows.shape
    width = qu_weight.shape[2]
    positions = keys.shape[1]
    groups = lax.axis_size("head")
    owners = lax.axis_size("seq")
    first_position = lax.axis_index("seq") * positions
    live = jnp.clip(lengths - first_position, 0, positions).astype(jnp.int32)

    copies = jnp.broadcast_to(cand_rows[None], (groups, rows, depth))
    cand_parts = lax.all_to_all(copies, "head", 0, 0, tiled=True)
    queries, gates = pl.pallas_call(
        project_kernel,
        out_shape=(
            jax.ShapeDtypeStruct((owners, rows, width), jnp.bfloat16),
            jax.ShapeDtypeStruct((rows, width), jnp.bfloat16),
        ),
        in_specs=[VMEM] * 3,
        out_specs=(VMEM, VMEM),
        compiler_params=PARAMS,
        name="project",
    )(
        cand_user.reshape(1, rows),
        cand_parts,
        qu_weight.reshape(qu_weight.shape[0], 2 * width),
    )
    queries = lax.all_to_all(queries, "seq", 0, 0, tiled=True)
    totals = pl.pallas_call(
        functools.partial(attend_kernel, 512, 256),
        out_shape=jax.ShapeDtypeStruct((owners, rows, width), jnp.bfloat16),
        in_specs=[SMEM] + [VMEM] * 3,
        out_specs=VMEM,
        scratch_shapes=[
            pltpu.VMEM((USERS, width, positions), jnp.bfloat16),
            pltpu.VMEM((USERS, width // HEAD_DIM * positions, width), jnp.bfloat16),
        ],
        compiler_params=PARAMS,
        name="attend",
    )(live, queries, keys, values)
    totals = lax.all_to_all(totals, "seq", 0, 0, tiled=True)
    terms = pl.pallas_call(
        finish_kernel,
        out_shape=jax.ShapeDtypeStruct((groups, rows, depth), jnp.float32),
        in_specs=[SMEM] + [VMEM] * 4,
        out_specs=VMEM,
        compiler_params=PARAMS,
        name="finish",
    )(lengths, cand_user.reshape(rows, 1), totals, gates, out_weight)
    terms = lax.all_to_all(terms, "head", 0, 0, tiled=True)
    return (cand_rows.astype(jnp.float32) + jnp.sum(terms, axis=0)).astype(jnp.bfloat16)


def solution(mesh):
    return jax.shard_map(
        local,
        mesh=mesh,
        in_specs=(
            P(("user", "seq"), "head"),
            P(None, None, "head"),
            P("head", None),
            P("user", "seq", "head"),
            P("user", "seq", "head"),
            P("user"),
            P(("user", "seq")),
        ),
        out_specs=P(("user", "seq"), "head"),
        check_vma=False,
    )
```

time: 526 us -> 114 us (0.22)
  waiting for transfers between devices: 275 us -> 57.5 us
  starting transfers between devices: 129 us -> 25.4 us
  matrix products: 64.6 us -> 0 us
  Pallas kernels: 0 us -> 15.1 us
  between operations: 13.5 us -> 0.07 us
  local copies, waits for them, and re-layouts: 19.2 us -> 5.97 us
  other arithmetic: 8.63 us -> 0.64 us
    ppermute x64 -> x0, waiting for transfers between devices: 245 us -> none  [passed_along(): return lax.ppermute(value, axis, pairs)]
    ppermute x64 -> x0, starting transfers between devices: 129 us -> none  [passed_along(): return lax.ppermute(value, axis, pairs)]
    dot_general x34 -> x0, matrix products: 64.6 us -> none  [the longest x32 63.3 us: attend_block(): jnp.einsum('ruhp,uphe->ruhe', weight, value_heads, preferred_element_type...]
    all_to_all x0 -> x3, waiting for transfers between devices: none -> 57.5 us  [the longest x1 27.5 us: local(): totals = lax.all_to_all(totals, 'seq', 0, 0, tiled=True)]
    reduce_scatter x1 -> x0, waiting for transfers between devices: 30.1 us -> none  [local(): lax.psum_scatter(partial_terms, 'head', scatter_dimension=1, tiled=True)]
    all_to_all x0 -> x3, starting transfers between devices: none -> 25.4 us  [the longest x1 14.1 us: local(): queries = lax.all_to_all(queries, 'seq', 0, 0, tiled=True)]
    pallas_call x0 -> x3, Pallas kernels: none -> 15.1 us  [the longest x1 13.5 us: local(): pl.pallas_call(functools.partial(attend_kernel, 512, 256), out_shape=jax....]
    all_gather x1 -> x0, blocking collectives: 12.5 us -> none  [local(): whole = lax.all_gather(cand_rows, 'head', axis=1, tiled=True)]
  transfers between devices with their start and end apart: 65 -> 3, of which waited for: 33 -> 3; matrix products, arithmetic and copies ran while one was open for 0% -> 1% of each run, Pallas kernels for 0% -> 0%
where the time goes in v1:
time: 114 us
  waiting for transfers between devices  57.5 us (50%)
  starting transfers between devices  25.4 us (22%)
  Pallas kernels  15.1 us (13%)
  blocking collectives  9.07 us (8%)
  local copies, waits for them, and re-layouts  5.97 us (5%)
    all_to_all x1, waiting for transfers between devices, local(): totals = lax.all_to_all(totals, 'seq', 0, 0, tiled=True)  27.5 us
    all_to_all x1, waiting for transfers between devices, local(): queries = lax.all_to_all(queries, 'seq', 0, 0, tiled=True)  25.5 us
    all_to_all x1, starting transfers between devices, local(): queries = lax.all_to_all(queries, 'seq', 0, 0, tiled=True)  14.1 us
    pallas_call x1, Pallas kernels, local(): pl.pallas_call(functools.partial(attend_kernel, 512, 256), out_shape=jax....  13.5 us
    all_to_all x1, blocking collectives, local(): terms = lax.all_to_all(terms, 'head', 0, 0, tiled=True)  9.07 us
    all_to_all x1, starting transfers between devices, local(): totals = lax.all_to_all(totals, 'seq', 0, 0, tiled=True)  7.02 us
    all_to_all x1, waiting for transfers between devices, local(): cand_parts = lax.all_to_all(copies, 'head', 0, 0, tiled=True)  4.52 us
    unnamed x15, local copies, waits for them, and re-layouts  4.47 us
  transfers between devices with their start and end apart: 3, of which 3 were waited for; matrix products, arithmetic and copies ran while one was open for 1% of the time, Pallas kernels for 0%

profile of v1, /device:TPU:8, one launch (start us, length us, event | category | flops | bytes accessed | tf_op | source)
XLA Modules:
  0.0 113.8 jit_solution(13472320987104213418)
XLA Ops:
  0.0 1.4 %broadcast_in_dim.2 = bf16[4,64,256]{2,1,0:T(8,128)(2,1)} broadcast(bf16[64,256]{1,0:T(8,128)(2,1)} %param.7), dimensions={1,2} | broadcast | bytes 163840 | tf_op jit(solution)/shard_map/broadcast_in_dim | solution.py:140
  1.4 4.3 %all-to-all-start = ((bf16[4,64,256]{2,1,0:T(8,128)(2,1)}), bf16[4,64,256]{2,1,0:T(8,128)(2,1)S(1)}, u32[]{:S(2)}, u32[]{:S(2)}) async-start(bf16[4,64,256]{2,1,0:T(8,128)(2,1)} %broadcast_in_dim.2), calls=%async_computation | async-start | bytes 262144 | tf_op jit(solution)/shard_map/all_to_all | solution.py:141
  5.7 1.4 %copy.9 = bf16[128,8,2,256]{3,1,2,0:T(8,128)(2,1)S(1)} copy(bf16[128,8,2,256]{3,2,1,0:T(2,128)(2,1)} %bitcast.7) | data formatting | bytes 2097152
  7.2 4.5 %all-to-all-done.cand_ref = bf16[4,64,256]{2,1,0:T(8,128)(2,1)S(1)} async-done(((bf16[4,64,256]{2,1,0:T(8,128)(2,1)}), bf16[4,64,256]{2,1,0:T(8,128)(2,1)S(1)}, u32[]{:S(2)}, u32[]{:S(2)}) %all-to-all-start) | async-done | bytes 131104 | tf_op jit(solution)/shard_map/all_to_all | solution.py:141
  11.7 0.0 copy-start.4
  11.7 0.7 copy-done.4
  12.3 0.6 project.1
  12.9 0.0 copy-start.2
  12.9 1.0 copy-done.2
  13.9 0.0 copy-start
  13.9 0.0 copy-start.1
  13.9 14.1 %all-to-all-start.1 = ((bf16[32,64,256]{2,1,0:T(8,128)(2,1)}), bf16[32,64,256]{2,1,0:T(8,128)(2,1)S(1)}, u32[]{:S(2)}, u32[]{:S(2)}) async-start(bf16[32,64,256]{2,1,0:T(8,128)(2,1)} %copy-done.2), calls=%async_computation.1 | async-start | bytes 2097152 | tf_op jit(solution)/shard_map/all_to_all | solution.py:157
  28.0 0.0 copy-start.5
  28.0 0.6 copy-done.5
  28.7 25.5 %all-to-all-done.1.query_ref = bf16[32,64,256]{2,1,0:T(8,128)(2,1)S(1)} async-done(((bf16[32,64,256]{2,1,0:T(8,128)(2,1)}), bf16[32,64,256]{2,1,0:T(8,128)(2,1)S(1)}, u32[]{:S(2)}, u32[]{:S(2)}) %all-to-all-start.1) | async-done | bytes 1048608 | tf_op jit(solution)/shard_map/all_to_all | solution.py:157
  54.2 0.0 copy-done
  54.2 0.0 copy-done.1
  54.2 13.5 %attend.1 = bf16[32,64,256]{2,1,0:T(8,128)(2,1)} custom-call(s32[2]{0:T(128)S(1)} %subtract_clamp_fusion.live_ref, bf16[32,64,256]{2,1,0:T(8,128)(2,1)S(1)} %all-to-all-done.1.query_ref, bf16[2,1024,256]{2,1,0:T(8,128)(2,1)S(1)} %copy-done, bf16[2,1024,256]{2,1,0:T(8,128)(2,1)S(1)} %copy-done.1), custom_call_target="tpu_custom_call" | custom-call | tf_op jit(solution)/shard_map/attend/pallas_call | solution.py:158
  67.7 0.0 copy-start.3
  67.7 7.0 %all-to-all-start.2 = ((bf16[32,64,256]{2,1,0:T(8,128)(2,1)}), bf16[32,64,256]{2,1,0:T(8,128)(2,1)S(1)}, u32[]{:S(2)}, u32[]{:S(2)}) async-start(bf16[32,64,256]{2,1,0:T(8,128)(2,1)} %attend.1), calls=%async_computation.2 | async-start | bytes 2097152 | tf_op jit(solution)/shard_map/all_to_all | solution.py:170
  74.7 0.1 copy.8.user_ref
  74.8 27.5 %all-to-all-done.2.partial_ref = bf16[32,64,256]{2,1,0:T(8,128)(2,1)S(1)} async-done(((bf16[32,64,256]{2,1,0:T(8,128)(2,1)}), bf16[32,64,256]{2,1,0:T(8,128)(2,1)S(1)}, u32[]{:S(2)}, u32[]{:S(2)}) %all-to-all-start.2) | async-done | bytes 1048608 | tf_op jit(solution)/shard_map/all_to_all | solution.py:170
  102.3 0.0 copy-done.3
  102.3 1.1 finish.1
  103.4 9.1 %all_to_all.20 = f32[4,64,256]{2,1,0:T(8,128)S(1)} all-to-all(f32[4,64,256]{2,1,0:T(8,128)S(1)} %finish.1), channel_id=1, replica_groups=mesh['seq'=32,'head'=4,'user'=4] {'head'}, dimensions={0} | all-to-all | bytes 524288 | tf_op jit(solution)/shard_map/all_to_all | solution.py:179
  112.4 0.0 copy-start.6
  112.5 0.7 copy-done.6
  113.2 0.6 add_convert_fusion
  (2 shorter events, 0.0 us)
Async XLA Ops:
  1.4 10.3 %all-to-all-start = ((bf16[4,64,256]{2,1,0:T(8,128)(2,1)}), bf16[4,64,256]{2,1,0:T(8,128)(2,1)S(1)}, u32[]{:S(2)}, u32[]{:S(2)}) async-start(bf16[4,64,256]{2,1,0:T(8,128)(2,1)} %broadcast_in_dim.2), calls=%async_computation | async-start | bytes 262144 | tf_op jit(solution)/shard_map/all_to_all | solution.py:141
  11.7 0.7 copy-start.4
  12.9 1.0 copy-start.2
  13.9 40.3 %copy-start = (bf16[2,1024,256]{2,1,0:T(8,128)(2,1)S(1)}, bf16[2,1024,256]{2,1,0:T(8,128)(2,1)}, u32[]{:S(2)}) copy-start(bf16[2,1024,256]{2,1,0:T(8,128)(2,1)} %key_ref.1) | copy-start | bytes 3145732
  13.9 40.3 %copy-start.1 = (bf16[2,1024,256]{2,1,0:T(8,128)(2,1)S(1)}, bf16[2,1024,256]{2,1,0:T(8,128)(2,1)}, u32[]{:S(2)}) copy-start(bf16[2,1024,256]{2,1,0:T(8,128)(2,1)} %value_ref.1) | copy-start | bytes 3145732
  13.9 40.3 %all-to-all-start.1 = ((bf16[32,64,256]{2,1,0:T(8,128)(2,1)}), bf16[32,64,256]{2,1,0:T(8,128)(2,1)S(1)}, u32[]{:S(2)}, u32[]{:S(2)}) async-start(bf16[32,64,256]{2,1,0:T(8,128)(2,1)} %copy-done.2), calls=%async_computation.1 | async-start | bytes 2097152 | tf_op jit(solution)/shard_map/all_to_all | solution.py:157
  28.0 0.7 copy-start.5
  67.7 34.6 %copy-start.3 = (bf16[256,1024]{1,0:T(8,128)(2,1)S(1)}, bf16[256,1024]{1,0:T(8,128)(2,1)}, u32[]{:S(2)}) copy-start(bf16[256,1024]{1,0:T(8,128)(2,1)} %weight_ref.1) | copy-start | bytes 1572868
  67.7 34.6 %all-to-all-start.2 = ((bf16[32,64,256]{2,1,0:T(8,128)(2,1)}), bf16[32,64,256]{2,1,0:T(8,128)(2,1)S(1)}, u32[]{:S(2)}, u32[]{:S(2)}) async-start(bf16[32,64,256]{2,1,0:T(8,128)(2,1)} %attend.1), calls=%async_computation.2 | async-start | bytes 2097152 | tf_op jit(solution)/shard_map/all_to_all | solution.py:170
  112.4 0.8 copy-start.6

commit v2 on v1

--- a/solution.py
+++ b/solution.py
@@ -12,6 +12,13 @@
 VMEM = pl.BlockSpec(memory_space=pltpu.VMEM)
 SMEM = pl.BlockSpec(memory_space=pltpu.SMEM)
 PARAMS = pltpu.CompilerParams(vmem_limit_bytes=48 * 2**20)
+
+
+SQUARE = (0, 4, 1, 5)
+
+
+def role(place):
+    return (place // 4) % 2, place % 2
 
 
 def head_mask(shape, head):
@@ -42,64 +49,76 @@
         place, projected.astype(jnp.bfloat16), preferred_element_type=jnp.float32
     )
     query = (ordered[:, :width] * (0.5 * HEAD_DIM**-0.5)).astype(jnp.bfloat16)
-    for copy in range(query_ref.shape[0]):
-        query_ref[copy] = query
+    _, block_rows, lanes = query_ref.shape
+    for owner in range(query_ref.shape[0]):
+        user, half = role(owner)
+        query_ref[owner] = query[
+            user * block_rows : (user + 1) * block_rows, half * lanes : (half + 1) * lanes
+        ]
     gate_ref[...] = ordered[:, width:].astype(jnp.bfloat16)
 
 
+def share_kernel(place_ref, key_ref, value_ref, *out_refs):
+    lanes = out_refs[0].shape[2]
+    for out_ref, offset in zip(out_refs, SQUARE):
+        user, half = role(place_ref[0] ^ offset)
+        here = pl.ds(pl.multiple_of(half * lanes, lanes), lanes)
+        out_ref[0] = key_ref[user, :, here]
+        out_ref[1] = value_ref[user, :, here]
+
+
 def attend_kernel(
-    rows_now, positions_now, live_ref, query_ref, key_ref, value_ref, out_ref, keys, masked
+    rows_now, positions_now, place_ref, length_ref, query_ref, *rest
 ):
+    history_refs, (out_ref, keys, masked) = rest[: len(SQUARE)], rest[len(SQUARE) :]
     blocks, block_rows, width = query_ref.shape
     heads = width // HEAD_DIM
-    positions = key_ref.shape[1]
-    per_user = block_rows // USERS
-    step_blocks = rows_now // per_user
-    for user in range(USERS):
-        keys[user] = key_ref[user].T
-        position = lax.broadcasted_iota(jnp.int32, (positions, width), 0)
-        value = value_ref[user]
+    span = history_refs[0].shape[1]
+    positions = span * len(SQUARE)
+    step_blocks = rows_now // block_rows
+    user, _ = role(place_ref[0])
+    length = length_ref[user]
+    for index, (offset, history_ref) in enumerate(zip(SQUARE, history_refs)):
+        at = slice(index * span, (index + 1) * span)
+        live = length - (place_ref[0] ^ offset) * span
+        keys[:, at] = history_ref[0].T
+        position = lax.broadcasted_iota(jnp.int32, (span, width), 0)
+        value = history_ref[1]
         for head in range(heads):
-            keep = (position < live_ref[user]) & head_mask((positions, width), head)
-            masked[user, head * positions : (head + 1) * positions, :] = jnp.where(
-                keep, value, jnp.zeros_like(value)
-            )
-
-        def step(index, carry, user=user):
-            here = pl.ds(index * step_blocks, step_blocks)
-            mine = slice(user * per_user, (user + 1) * per_user)
-            query = query_ref[here, mine, :].reshape(rows_now, width)
-            total = jnp.zeros((rows_now, width), jnp.float32)
-            for start in range(0, positions, positions_now):
-                for head in range(heads):
-                    own = jnp.where(
-                        head_mask((rows_now, width), head), query, jnp.zeros_like(query)
-                    )
-                    half = jnp.dot(
-                        own,
-                        keys[user, :, start : start + positions_now],
-                        preferred_element_type=jnp.float32,
-                    )
-                    weight = (half + half * jnp.tanh(half)).astype(jnp.bfloat16)
-                    at = head * positions + start
-                    total += jnp.dot(
-                        weight,
-                        masked[user, at : at + positions_now, :],
-                        preferred_element_type=jnp.float32,
-                    )
-            out_ref[here, mine, :] = total.astype(jnp.bfloat16).reshape(
-                step_blocks, per_user, width
-            )
-            return carry
-
-        lax.fori_loop(0, blocks // step_blocks, step, 0)
+            keep = (position < live) & head_mask((span, width), head)
+            masked[head, at, :] = jnp.where(keep, value, jnp.zeros_like(value))
+
+    def step(index, carry):
+        here = pl.ds(index * step_blocks, step_blocks)
+        query = query_ref[here].reshape(rows_now, width)
+        total = jnp.zeros((rows_now, width), jnp.float32)
+        for start in range(0, positions, positions_now):
+            at = slice(start, start + positions_now)
+            for head in range(heads):
+                own = jnp.where(
+                    head_mask((rows_now, width), head), query, jnp.zeros_like(query)
+                )
+                half = jnp.dot(own, keys[:, at], preferred_element_type=jnp.float32)
+                weight = (half + half * jnp.tanh(half)).astype(jnp.bfloat16)
+                total += jnp.dot(
+                    weight, masked[head, at, :], preferred_element_type=jnp.float32
+                )
+        out_ref[here] = total.astype(jnp.bfloat16).reshape(step_blocks, block_rows, width)
+        return carry
+
+    lax.fori_loop(0, blocks // step_blocks, step, 0)
 
 
 def finish_kernel(length_ref, user_ref, partial_ref, gate_ref, weight_ref, out_ref):
-    blocks, rows, width = partial_ref.shape
-    total = partial_ref[0].astype(jnp.float32)
-    for block in range(1, blocks):
-        total += partial_ref[block].astype(jnp.float32)
+    rows, width = gate_ref.shape
+    sums = {}
+    for block in range(partial_ref.shape[0]):
+        term = partial_ref[block].astype(jnp.float32)
+        sums[role(block)] = sums[role(block)] + term if role(block) in sums else term
+    total = jnp.concatenate(
+        [jnp.concatenate([sums[user, half] for half in range(2)], axis=1) for user in range(USERS)],
+        axis=0,
+    )
     row = lax.broadcasted_iota(jnp.int32, (rows, width), 0)
     length = jnp.where(row < rows // USERS, length_ref[0], length_ref[1]).astype(jnp.float32)
     attn = total / length
@@ -134,15 +153,28 @@
     positions = keys.shape[1]
     groups = lax.axis_size("head")
     owners = lax.axis_size("seq")
-    first_position = lax.axis_index("seq") * positions
-    live = jnp.clip(lengths - first_position, 0, positions).astype(jnp.int32)
+    place = jnp.reshape(lax.axis_index("seq"), (1,)).astype(jnp.int32)
+    block_rows, lanes = rows // USERS, width // 2
+
+    shares = pl.pallas_call(
+        share_kernel,
+        out_shape=[jax.ShapeDtypeStruct((2, positions, lanes), jnp.bfloat16) for _ in SQUARE],
+        in_specs=[SMEM, VMEM, VMEM],
+        out_specs=[VMEM for _ in SQUARE],
+        compiler_params=PARAMS,
+        name="share",
+    )(place, keys, values)
+    history = [
+        lax.ppermute(share, "seq", [(s, s ^ offset) for s in range(owners)]) if offset else share
+        for share, offset in zip(shares, SQUARE)
+    ]
 
     copies = jnp.broadcast_to(cand_rows[None], (groups, rows, depth))
     cand_parts = lax.all_to_all(copies, "head", 0, 0, tiled=True)
     queries, gates = pl.pallas_call(
         project_kernel,
         out_shape=(
-            jax.ShapeDtypeStruct((owners, rows, width), jnp.bfloat16),
+            jax.ShapeDtypeStruct((owners, block_rows, lanes), jnp.bfloat16),
             jax.ShapeDtypeStruct((rows, width), jnp.bfloat16),
         ),
         in_specs=[VMEM] * 3,
@@ -156,17 +188,17 @@
     )
     queries = lax.all_to_all(queries, "seq", 0, 0, tiled=True)
     totals = pl.pallas_call(
-        functools.partial(attend_kernel, 512, 256),
-        out_shape=jax.ShapeDtypeStruct((owners, rows, width), jnp.bfloat16),
-        in_specs=[SMEM] + [VMEM] * 3,
+        functools.partial(attend_kernel, 1024, 256),
+        out_shape=jax.ShapeDtypeStruct((owners, block_rows, lanes), jnp.bfloat16),
+        in_specs=[SMEM] * 2 + [VMEM] * (1 + len(SQUARE)),
         out_specs=VMEM,
         scratch_shapes=[
-            pltpu.VMEM((USERS, width, positions), jnp.bfloat16),
-            pltpu.VMEM((USERS, width // HEAD_DIM * positions, width), jnp.bfloat16),
+            pltpu.VMEM((lanes, len(SQUARE) * positions), jnp.bfloat16),
+            pltpu.VMEM((lanes // HEAD_DIM, len(SQUARE) * positions, lanes), jnp.bfloat16),
         ],
         compiler_params=PARAMS,
         name="attend",
-    )(live, queries, keys, values)
+    )(place, lengths, queries, *history)
     totals = lax.all_to_all(totals, "seq", 0, 0, tiled=True)
     terms = pl.pallas_call(
         finish_kernel,

time: 114 us -> 97 us (0.85)
  the two profiles are of different devices: /device:TPU:8 before, /device:TPU:2 now
where the time goes in v2:
time: 97 us; the launch traced here: 96.3 us
  starting transfers between devices  33.1 us (34%)
  waiting for transfers between devices  32.7 us (34%)
  Pallas kernels  14.4 us (15%)
  blocking collectives  9.82 us (10%)
  local copies, waits for them, and re-layouts  5.58 us (6%)
    all_to_all x1, waiting for transfers between devices, local(): queries = lax.all_to_all(queries, 'seq', 0, 0, tiled=True)  13.1 us
    all_to_all x1, waiting for transfers between devices, local(): totals = lax.all_to_all(totals, 'seq', 0, 0, tiled=True)  11.8 us
    pallas_call x1, Pallas kernels, local(): pl.pallas_call(functools.partial(attend_kernel, 1024, 256), out_shape=jax...  10.8 us
    all_to_all x1, blocking collectives, local(): terms = lax.all_to_all(terms, 'head', 0, 0, tiled=True)  9.82 us
    all_to_all x1, starting transfers between devices, local(): queries = lax.all_to_all(queries, 'seq', 0, 0, tiled=True)  9.37 us
    ppermute x3, starting transfers between devices, local(): lax.ppermute(share, 'seq', [(s, s ^ offset) for s in range(owners)])  9.2 us
    all_to_all x1, starting transfers between devices, local(): cand_parts = lax.all_to_all(copies, 'head', 0, 0, tiled=True)  9.2 us
    ppermute x3, waiting for transfers between devices, local(): lax.ppermute(share, 'seq', [(s, s ^ offset) for s in range(owners)])  7.77 us
  transfers between devices with their start and end apart: 6, of which 3 were waited for; matrix products, arithmetic and copies ran while one was open for 0% of the time, Pallas kernels for 3%

profile of v2, /device:TPU:2, one launch (start us, length us, event | category | flops | bytes accessed | tf_op | source)
XLA Modules:
  0.0 96.3 jit_solution(11213944706745918106)
XLA Ops:
  0.0 1.4 %broadcast_in_dim.2 = bf16[4,64,256]{2,1,0:T(8,128)(2,1)} broadcast(bf16[64,256]{1,0:T(8,128)(2,1)} %param.7), dimensions={1,2} | broadcast | bytes 163840 | tf_op jit(solution)/shard_map/broadcast_in_dim | solution.py:172
  1.4 9.2 %all-to-all-start = ((bf16[4,64,256]{2,1,0:T(8,128)(2,1)}), bf16[4,64,256]{2,1,0:T(8,128)(2,1)S(1)}, u32[]{:S(2)}, u32[]{:S(2)}) async-start(bf16[4,64,256]{2,1,0:T(8,128)(2,1)} %broadcast_in_dim.2), calls=%async_computation | async-start | bytes 262144 | tf_op jit(solution)/shard_map/all_to_all | solution.py:173
  10.6 0.0 copy-start
  10.6 1.2 %copy-done = bf16[2,1024,256]{2,1,0:T(8,128)(2,1)S(1)} copy-done((bf16[2,1024,256]{2,1,0:T(8,128)(2,1)S(1)}, bf16[2,1024,256]{2,1,0:T(8,128)(2,1)}, u32[]{:S(2)}) %copy-start) | copy-done | bytes 1048600
  11.8 0.0 copy-start.1
  11.8 1.2 %copy-done.1 = bf16[2,1024,256]{2,1,0:T(8,128)(2,1)S(1)} copy-done((bf16[2,1024,256]{2,1,0:T(8,128)(2,1)S(1)}, bf16[2,1024,256]{2,1,0:T(8,128)(2,1)}, u32[]{:S(2)}) %copy-start.1) | copy-done | bytes 1048600
  13.1 0.0 copy-start.5
  13.1 1.3 %share.1 = (bf16[2,1024,128]{2,1,0:T(8,128)(2,1)S(1)}, bf16[2,1024,128]{2,1,0:T(8,128)(2,1)}, bf16[2,1024,128]{2,1,0:T(8,128)(2,1)}, bf16[2,1024,128]{2,1,0:T(8,128)(2,1)}) custom-call(s32[1]{0:T(128)} %bitcast.1.place_ref, bf16[2,1024,256]{2,1,0:T(8,128)(2,1)S(1)} %copy-done, bf16[2,1024,256]{2,1,0:T(8,128)(2,1)S(1)} %copy-done.1), custom_call_target="tpu_custom_call" | custom-call | tf_op jit(solution)/shard_map/share/pallas_call | solution.py:159
  14.4 1.9 %collective-permute-start = (bf16[2,1024,128]{2,1,0:T(8,128)(2,1)}, bf16[2,1024,128]{2,1,0:T(8,128)(2,1)S(1)}, u32[]{:S(2)}, u32[]{:S(2)}) collective-permute-start(bf16[2,1024,128]{2,1,0:T(8,128)(2,1)} %get-tuple-element.13), channel_id=1, source_target_pairs={{0,64},{16,80},{32,96},{48,112},{64,0},{80,16},{96,32},{112,48},{1... | collective-permute-start | bytes 1572872 | tf_op jit(solution)/shard_map/ppermute | solution.py:168
  16.3 1.9 %collective-permute-start.1 = (bf16[2,1024,128]{2,1,0:T(8,128)(2,1)}, bf16[2,1024,128]{2,1,0:T(8,128)(2,1)S(1)}, u32[]{:S(2)}, u32[]{:S(2)}) collective-permute-start(bf16[2,1024,128]{2,1,0:T(8,128)(2,1)} %get-tuple-element.14), channel_id=1, source_target_pairs={{0,16},{16,0},{32,48},{48,32},{64,80},{80,64},{96,112},{112,96},{1... | collective-permute-start | bytes 1572872 | tf_op jit(solution)/shard_map/ppermute | solution.py:168
  18.2 5.4 %collective-permute-start.2 = (bf16[2,1024,128]{2,1,0:T(8,128)(2,1)}, bf16[2,1024,128]{2,1,0:T(8,128)(2,1)S(1)}, u32[]{:S(2)}, u32[]{:S(2)}) collective-permute-start(bf16[2,1024,128]{2,1,0:T(8,128)(2,1)} %get-tuple-element.15), channel_id=1, source_target_pairs={{0,80},{16,64},{32,112},{48,96},{64,16},{80,0},{96,48},{112,32},{1... | collective-permute-start | bytes 1572872 | tf_op jit(solution)/shard_map/ppermute | solution.py:168
  23.6 0.0 copy-done.5
  23.6 0.2 copy.9
  23.9 0.0 all-to-all-done.cand_ref
  23.9 0.0 copy-start.3
  23.9 0.6 copy-done.3
  24.5 1.2 %project.1 = (bf16[32,32,128]{2,1,0:T(8,128)(2,1)}, bf16[64,256]{1,0:T(8,128)(2,1)S(1)}) custom-call(s32[1,64]{1,0:T(1,128)S(1)} %bitcast.6, bf16[4,64,256]{2,1,0:T(8,128)(2,1)S(1)} %all-to-all-done.cand_ref, bf16[1024,512]{1,0:T(8,128)(2,1)S(1)} %bitcast.5), custom_call_target="tpu_custom_call" | custom-call | tf_op jit(solution)/shard_map/project/pallas_call | solution.py:174
  25.7 9.4 %all-to-all-start.1 = ((bf16[32,32,128]{2,1,0:T(8,128)(2,1)}), bf16[32,32,128]{2,1,0:T(8,128)(2,1)S(1)}, u32[]{:S(2)}, u32[]{:S(2)}) async-start(bf16[32,32,128]{2,1,0:T(8,128)(2,1)} %get-tuple-element.11), calls=%async_computation.1 | async-start | bytes 524288 | tf_op jit(solution)/shard_map/all_to_all | solution.py:189
  35.1 0.0 copy-start.4
  35.1 0.0 collective-permute-done.rest_1_
  35.1 0.0 collective-permute-done.1.rest_2_
  35.1 7.8 %collective-permute-done.2.rest_3_ = bf16[2,1024,128]{2,1,0:T(8,128)(2,1)S(1)} collective-permute-done((bf16[2,1024,128]{2,1,0:T(8,128)(2,1)}, bf16[2,1024,128]{2,1,0:T(8,128)(2,1)S(1)}, u32[]{:S(2)}, u32[]{:S(2)}) %collective-permute-start.2) | collective-permute-done | bytes 524320 | tf_op jit(solution)/shard_map/ppermute | solution.py:168
  42.9 13.1 %all-to-all-done.1.query_ref = bf16[32,32,128]{2,1,0:T(8,128)(2,1)S(1)} async-done(((bf16[32,32,128]{2,1,0:T(8,128)(2,1)}), bf16[32,32,128]{2,1,0:T(8,128)(2,1)S(1)}, u32[]{:S(2)}, u32[]{:S(2)}) %all-to-all-start.1) | async-done | bytes 262176 | tf_op jit(solution)/shard_map/all_to_all | solution.py:189
  56.0 0.0 copy-done.4
  56.0 10.8 %attend.1 = bf16[32,32,128]{2,1,0:T(8,128)(2,1)} custom-call(s32[1]{0:T(128)} %bitcast.1.place_ref, s32[2]{0:T(128)S(1)} %copy-done.4, bf16[32,32,128]{2,1,0:T(8,128)(2,1)S(1)} %all-to-all-done.1.query_ref, bf16[2,1024,128]{2,1,0:T(8,128)(2,1)S(1)} %get-tuple-element.12.rest_0_, bf16[2,1024,128]{2,1,0:T(8,128)(2,1)S(1)} %collective-permute-done.rest_1_, ...), custom_call_target="tpu_custom_call" | custom-call | tf_op jit(solution)/shard_map/attend/pallas_call | solution.py:190
  66.8 0.0 copy-start.2
  66.8 5.3 %all-to-all-start.2 = ((bf16[32,32,128]{2,1,0:T(8,128)(2,1)}), bf16[32,32,128]{2,1,0:T(8,128)(2,1)S(1)}, u32[]{:S(2)}, u32[]{:S(2)}) async-start(bf16[32,32,128]{2,1,0:T(8,128)(2,1)} %attend.1), calls=%async_computation.2 | async-start | bytes 524288 | tf_op jit(solution)/shard_map/all_to_all | solution.py:202
  72.2 0.1 copy.8.user_ref
  72.3 11.8 %all-to-all-done.2.partial_ref = bf16[32,32,128]{2,1,0:T(8,128)(2,1)S(1)} async-done(((bf16[32,32,128]{2,1,0:T(8,128)(2,1)}), bf16[32,32,128]{2,1,0:T(8,128)(2,1)S(1)}, u32[]{:S(2)}, u32[]{:S(2)}) %all-to-all-start.2) | async-done | bytes 262176 | tf_op jit(solution)/shard_map/all_to_all | solution.py:202
  84.1 0.0 copy-done.2
  84.1 1.0 %finish.1 = f32[4,64,256]{2,1,0:T(8,128)S(1)} custom-call(s32[2]{0:T(128)S(1)} %copy-done.4, s32[64,1]{1,0:T(8,128)S(1)} %copy.8.user_ref, bf16[32,32,128]{2,1,0:T(8,128)(2,1)S(1)} %all-to-all-done.2.partial_ref, bf16[64,256]{1,0:T(8,128)(2,1)S(1)} %get-tuple-element.16.gate_ref, bf16[256,1024]{1,0:T(8,128)(2,1)S(1)} %copy-done.2), custom_call_target="tpu_custom_call" | custom-call | tf_op jit(solution)/shard_map/finish/pallas_call | solution.py:203
  85.1 9.8 %all_to_all.20 = f32[4,64,256]{2,1,0:T(8,128)S(1)} all-to-all(f32[4,64,256]{2,1,0:T(8,128)S(1)} %finish.1), channel_id=1, replica_groups=mesh['seq'=32,'head'=4,'user'=4] {'head'}, dimensions={0} | all-to-all | bytes 524288 | tf_op jit(solution)/shard_map/all_to_all | solution.py:211
  95.0 0.0 copy-start.6
  95.0 0.7 copy-done.6
  95.7 0.6 add_convert_fusion
  (1 shorter events, 0.0 us)
Async XLA Ops:
  1.4 22.5 %all-to-all-start = ((bf16[4,64,256]{2,1,0:T(8,128)(2,1)}), bf16[4,64,256]{2,1,0:T(8,128)(2,1)S(1)}, u32[]{:S(2)}, u32[]{:S(2)}) async-start(bf16[4,64,256]{2,1,0:T(8,128)(2,1)} %broadcast_in_dim.2), calls=%async_computation | async-start | bytes 262144 | tf_op jit(solution)/shard_map/all_to_all | solution.py:173
  10.6 1.2 %copy-start = (bf16[2,1024,256]{2,1,0:T(8,128)(2,1)S(1)}, bf16[2,1024,256]{2,1,0:T(8,128)(2,1)}, u32[]{:S(2)}) copy-start(bf16[2,1024,256]{2,1,0:T(8,128)(2,1)} %key_ref.1) | copy-start | bytes 3145732
  11.8 1.2 %copy-start.1 = (bf16[2,1024,256]{2,1,0:T(8,128)(2,1)S(1)}, bf16[2,1024,256]{2,1,0:T(8,128)(2,1)}, u32[]{:S(2)}) copy-start(bf16[2,1024,256]{2,1,0:T(8,128)(2,1)} %value_ref.1) | copy-start | bytes 3145732
  13.1 10.6 %copy-start.5 = (bf16[1024,2,256]{2,1,0:T(2,128)(2,1)S(1)}, bf16[1024,2,256]{2,1,0:T(2,128)(2,1)}, u32[]{:S(2)}) copy-start(bf16[1024,2,256]{2,1,0:T(2,128)(2,1)} %param.8) | copy-start | bytes 3145732
  14.4 20.7 %collective-permute-start = (bf16[2,1024,128]{2,1,0:T(8,128)(2,1)}, bf16[2,1024,128]{2,1,0:T(8,128)(2,1)S(1)}, u32[]{:S(2)}, u32[]{:S(2)}) collective-permute-start(bf16[2,1024,128]{2,1,0:T(8,128)(2,1)} %get-tuple-element.13), channel_id=1, source_target_pairs={{0,64},{16,80},{32,96},{48,112},{64,0},{80,16},{96,32},{112,48},{1... | collective-permute-start | bytes 1572872 | tf_op jit(solution)/shard_map/ppermute | solution.py:168
  16.3 18.8 %collective-permute-start.1 = (bf16[2,1024,128]{2,1,0:T(8,128)(2,1)}, bf16[2,1024,128]{2,1,0:T(8,128)(2,1)S(1)}, u32[]{:S(2)}, u32[]{:S(2)}) collective-permute-start(bf16[2,1024,128]{2,1,0:T(8,128)(2,1)} %get-tuple-element.14), channel_id=1, source_target_pairs={{0,16},{16,0},{32,48},{48,32},{64,80},{80,64},{96,112},{112,96},{1... | collective-permute-start | bytes 1572872 | tf_op jit(solution)/shard_map/ppermute | solution.py:168
  18.2 24.7 %collective-permute-start.2 = (bf16[2,1024,128]{2,1,0:T(8,128)(2,1)}, bf16[2,1024,128]{2,1,0:T(8,128)(2,1)S(1)}, u32[]{:S(2)}, u32[]{:S(2)}) collective-permute-start(bf16[2,1024,128]{2,1,0:T(8,128)(2,1)} %get-tuple-element.15), channel_id=1, source_target_pairs={{0,80},{16,64},{32,112},{48,96},{64,16},{80,0},{96,48},{112,32},{1... | collective-permute-start | bytes 1572872 | tf_op jit(solution)/shard_map/ppermute | solution.py:168
  23.9 0.7 copy-start.3
  25.7 30.2 %all-to-all-start.1 = ((bf16[32,32,128]{2,1,0:T(8,128)(2,1)}), bf16[32,32,128]{2,1,0:T(8,128)(2,1)S(1)}, u32[]{:S(2)}, u32[]{:S(2)}) async-start(bf16[32,32,128]{2,1,0:T(8,128)(2,1)} %get-tuple-element.11), calls=%async_computation.1 | async-start | bytes 524288 | tf_op jit(solution)/shard_map/all_to_all | solution.py:189
  35.1 20.9 %copy-start.4 = (s32[2]{0:T(128)S(1)}, s32[2]{0:T(128)}, u32[]{:S(2)}) copy-start(s32[2]{0:T(128)} %length_ref.3) | copy-start | bytes 28
  66.8 17.3 %copy-start.2 = (bf16[256,1024]{1,0:T(8,128)(2,1)S(1)}, bf16[256,1024]{1,0:T(8,128)(2,1)}, u32[]{:S(2)}) copy-start(bf16[256,1024]{1,0:T(8,128)(2,1)} %weight_ref.1) | copy-start | bytes 1572868
  66.8 17.3 %all-to-all-start.2 = ((bf16[32,32,128]{2,1,0:T(8,128)(2,1)}), bf16[32,32,128]{2,1,0:T(8,128)(2,1)S(1)}, u32[]{:S(2)}, u32[]{:S(2)}) async-start(bf16[32,32,128]{2,1,0:T(8,128)(2,1)} %attend.1), calls=%async_computation.2 | async-start | bytes 524288 | tf_op jit(solution)/shard_map/all_to_all | solution.py:202
  95.0 0.8 copy-start.6

commit v3 on v2

--- a/solution.py
+++ b/solution.py
@@ -11,6 +11,7 @@
 USERS = 2
 VMEM = pl.BlockSpec(memory_space=pltpu.VMEM)
 SMEM = pl.BlockSpec(memory_space=pltpu.SMEM)
+HBM = pl.BlockSpec(memory_space=pltpu.HBM)
 PARAMS = pltpu.CompilerParams(vmem_limit_bytes=48 * 2**20)
 
 
@@ -26,7 +27,21 @@
     return (lane >= head * HEAD_DIM) & (lane < (head + 1) * HEAD_DIM)
 
 
-def project_kernel(user_ref, cand_ref, weight_ref, query_ref, gate_ref):
+def orders_of(users, rows):
+    first = lax.broadcasted_iota(jnp.int32, (rows, rows), 0)
+    second = lax.broadcasted_iota(jnp.int32, (rows, rows), 1)
+    users = jnp.broadcast_to(users, (rows, rows))
+    before = jnp.dot(
+        users.astype(jnp.bfloat16),
+        (first < second).astype(jnp.bfloat16),
+        preferred_element_type=jnp.float32,
+    ).astype(jnp.int32)
+    target = jnp.where(users > 0, rows // USERS + before, second - before)
+    order = (target == first).astype(jnp.float32)
+    return order.astype(jnp.bfloat16), order.T.astype(jnp.bfloat16)
+
+
+def project_kernel(place_ref, cand_ref, weight_ref, query_ref, gate_ref):
     slices, rows, depth = cand_ref.shape
     width = weight_ref.shape[1] // 2
     total = jnp.zeros((rows, 2 * width), jnp.float32)
@@ -37,16 +52,8 @@
             preferred_element_type=jnp.float32,
         )
     projected = total / (1.0 + jnp.exp(-total))
-    first = lax.broadcasted_iota(jnp.int32, (rows, rows), 0)
-    second = lax.broadcasted_iota(jnp.int32, (rows, rows), 1)
-    users = jnp.broadcast_to(user_ref[...], (rows, rows)).astype(jnp.bfloat16)
-    before = jnp.dot(
-        users, (first < second).astype(jnp.bfloat16), preferred_element_type=jnp.float32
-    ).astype(jnp.int32)
-    target = jnp.where(users > 0, rows // USERS + before, second - before)
-    place = (target == first).astype(jnp.bfloat16)
     ordered = jnp.dot(
-        place, projected.astype(jnp.bfloat16), preferred_element_type=jnp.float32
+        place_ref[...], projected.astype(jnp.bfloat16), preferred_element_type=jnp.float32
     )
     query = (ordered[:, :width] * (0.5 * HEAD_DIM**-0.5)).astype(jnp.bfloat16)
     _, block_rows, lanes = query_ref.shape
@@ -58,13 +65,31 @@
     gate_ref[...] = ordered[:, width:].astype(jnp.bfloat16)
 
 
-def share_kernel(place_ref, key_ref, value_ref, *out_refs):
+def share_kernel(
+    place_ref, user_ref, cand_ref, key_ref, value_ref, *rest
+):
+    out_refs, (copy_ref, order_ref, back_ref, sems) = rest[: len(SQUARE)], rest[len(SQUARE) :]
     lanes = out_refs[0].shape[2]
-    for out_ref, offset in zip(out_refs, SQUARE):
+    copies = []
+    for index, (out_ref, offset) in enumerate(zip(out_refs, SQUARE)):
         user, half = role(place_ref[0] ^ offset)
         here = pl.ds(pl.multiple_of(half * lanes, lanes), lanes)
-        out_ref[0] = key_ref[user, :, here]
-        out_ref[1] = value_ref[user, :, here]
+        for kind, history_ref in enumerate((key_ref, value_ref)):
+            copies.append(
+                pltpu.make_async_copy(
+                    history_ref.at[user, :, here], out_ref.at[kind], sems.at[index, kind]
+                )
+            )
+    for copy in copies:
+        copy.start()
+    cand = cand_ref[...]
+    for group in range(copy_ref.shape[0]):
+        copy_ref[group] = cand
+    order, back = orders_of(user_ref[...], cand.shape[0])
+    order_ref[...] = order
+    back_ref[...] = back
+    for copy in copies:
+        copy.wait()
 
 
 def attend_kernel(
@@ -109,7 +134,7 @@
     lax.fori_loop(0, blocks // step_blocks, step, 0)
 
 
-def finish_kernel(length_ref, user_ref, partial_ref, gate_ref, weight_ref, out_ref):
+def finish_kernel(length_ref, back_ref, partial_ref, gate_ref, weight_ref, out_ref):
     rows, width = gate_ref.shape
     sums = {}
     for block in range(partial_ref.shape[0]):
@@ -129,22 +154,21 @@
         summed = jnp.sum(jnp.where(mask, square, 0.0), axis=1, keepdims=True)
         mean = jnp.where(mask, summed * (1.0 / HEAD_DIM), mean)
     normed = attn * lax.rsqrt(mean + 1e-06)
-    gated = (normed * gate_ref[...].astype(jnp.float32)).astype(jnp.bfloat16)
-    first = lax.broadcasted_iota(jnp.int32, (rows, rows), 0)
-    second = lax.broadcasted_iota(jnp.int32, (rows, rows), 1)
-    users = jnp.broadcast_to(user_ref[...], (rows, rows)).astype(jnp.bfloat16)
-    before = jnp.dot(
-        (second < first).astype(jnp.bfloat16), users, preferred_element_type=jnp.float32
-    ).astype(jnp.int32)
-    target = jnp.where(users > 0, rows // USERS + before, first - before)
-    back = (target == second).astype(jnp.bfloat16)
-    gated = jnp.dot(back, gated, preferred_element_type=jnp.float32).astype(jnp.bfloat16)
+    gated = (normed * gate_ref[...]).astype(jnp.bfloat16)
+    gated = jnp.dot(back_ref[...], gated, preferred_element_type=jnp.float32).astype(jnp.bfloat16)
     for part in range(out_ref.shape[0]):
         out_ref[part] = jnp.dot(
             gated,
             weight_ref[:, part * width : (part + 1) * width],
             preferred_element_type=jnp.float32,
-        )
+        ).astype(out_ref.dtype)
+
+
+def add_kernel(cand_ref, term_ref, out_ref):
+    total = cand_ref[...]
+    for group in range(term_ref.shape[0]):
+        total += term_ref[group].astype(jnp.float32)
+    out_ref[...] = total.astype(out_ref.dtype)
 
 
 def local(cand_rows, qu_weight, out_weight, keys, values, lengths, cand_user):
@@ -156,20 +180,25 @@
     place = jnp.reshape(lax.axis_index("seq"), (1,)).astype(jnp.int32)
     block_rows, lanes = rows // USERS, width // 2
 
-    shares = pl.pallas_call(
+    *shares, copies, order, back = pl.pallas_call(
         share_kernel,
-        out_shape=[jax.ShapeDtypeStruct((2, positions, lanes), jnp.bfloat16) for _ in SQUARE],
-        in_specs=[SMEM, VMEM, VMEM],
-        out_specs=[VMEM for _ in SQUARE],
-        compiler_params=PARAMS,
+        out_shape=[jax.ShapeDtypeStruct((2, positions, lanes), jnp.bfloat16) for _ in SQUARE]
+        + [
+            jax.ShapeDtypeStruct((groups, rows, depth), jnp.bfloat16),
+            jax.ShapeDtypeStruct((rows, rows), jnp.bfloat16),
+            jax.ShapeDtypeStruct((rows, rows), jnp.bfloat16),
+        ],
+        in_specs=[SMEM, VMEM, VMEM, HBM, HBM],
+        out_specs=[HBM] * len(SQUARE) + [VMEM] * 3,
+        scratch_shapes=[pltpu.SemaphoreType.DMA((len(SQUARE), 2))],
+        compiler_params=pltpu.CompilerParams(vmem_limit_bytes=60 * 2**20),
         name="share",
-    )(place, keys, values)
+    )(place, cand_user.reshape(1, rows), cand_rows, keys, values)
     history = [
         lax.ppermute(share, "seq", [(s, s ^ offset) for s in range(owners)]) if offset else share
         for share, offset in zip(shares, SQUARE)
     ]
 
-    copies = jnp.broadcast_to(cand_rows[None], (groups, rows, depth))
     cand_parts = lax.all_to_all(copies, "head", 0, 0, tiled=True)
     queries, gates = pl.pallas_call(
         project_kernel,
@@ -182,7 +211,7 @@
         compiler_params=PARAMS,
         name="project",
     )(
-        cand_user.reshape(1, rows),
+        order,
         cand_parts,
         qu_weight.reshape(qu_weight.shape[0], 2 * width),
     )
@@ -202,14 +231,21 @@
     totals = lax.all_to_all(totals, "seq", 0, 0, tiled=True)
     terms = pl.pallas_call(
         finish_kernel,
-        out_shape=jax.ShapeDtypeStruct((groups, rows, depth), jnp.float32),
+        out_shape=jax.ShapeDtypeStruct((groups, rows, depth), jnp.bfloat16),
         in_specs=[SMEM] + [VMEM] * 4,
         out_specs=VMEM,
         compiler_params=PARAMS,
         name="finish",
-    )(lengths, cand_user.reshape(rows, 1), totals, gates, out_weight)
+    )(lengths, back, totals, gates.astype(jnp.float32), out_weight)
     terms = lax.all_to_all(terms, "head", 0, 0, tiled=True)
-    return (cand_rows.astype(jnp.float32) + jnp.sum(terms, axis=0)).astype(jnp.bfloat16)
+    return pl.pallas_call(
+        add_kernel,
+        out_shape=jax.ShapeDtypeStruct((rows, depth), cand_rows.dtype),
+        in_specs=[VMEM, VMEM],
+        out_specs=VMEM,
+        compiler_params=PARAMS,
+        name="add",
+    )(cand_rows.astype(jnp.float32), terms)
 
 
 def solution(mesh):

time: 97 us -> 158 us (1.63)
  Pallas kernels: 14.4 us -> 80.5 us
  blocking collectives: 9.82 us -> 0 us
  starting transfers between devices: 33.1 us -> 38.5 us
  local copies, waits for them, and re-layouts: 5.58 us -> 1.48 us
  waiting for transfers between devices: 32.7 us -> 36.5 us
    pallas_call x1, Pallas kernels: 1.34 us -> 66.1 us  [local(): pl.pallas_call(share_kernel, out_shape=[jax.ShapeDtypeStruct((2, position...]
    all_to_all x1 -> x0, blocking collectives: 9.82 us -> none  [local(): terms = lax.all_to_all(terms, 'head', 0, 0, tiled=True)]
    all_to_all x0 -> x1, starting transfers between devices: none -> 4.94 us  [local(): terms = lax.all_to_all(terms, 'head', 0, 0, tiled=True)]
    all_to_all x0 -> x1, waiting for transfers between devices: none -> 4.51 us  [local(): terms = lax.all_to_all(terms, 'head', 0, 0, tiled=True)]
    unnamed x15 -> x13, local copies, waits for them, and re-layouts: 4.08 us -> 1.48 us
  transfers between devices with their start and end apart: 6 -> 7, of which waited for: 3 -> 4; matrix products, arithmetic and copies ran while one was open for 0% -> 1% of each run, Pallas kernels for 3% -> 1%
where the time goes in v3:
time: 158 us; the launch traced here: 157 us
  Pallas kernels  80.5 us (51%)
  starting transfers between devices  38.5 us (24%)
  waiting for transfers between devices  36.5 us (23%)
    pallas_call x1, Pallas kernels, local(): pl.pallas_call(share_kernel, out_shape=[jax.ShapeDtypeStruct((2, position...  66.1 us
    all_to_all x1, waiting for transfers between devices, local(): queries = lax.all_to_all(queries, 'seq', 0, 0, tiled=True)  13.3 us
    all_to_all x1, waiting for transfers between devices, local(): totals = lax.all_to_all(totals, 'seq', 0, 0, tiled=True)  11.9 us
    pallas_call x1, Pallas kernels, local(): pl.pallas_call(functools.partial(attend_kernel, 1024, 256), out_shape=jax...  10.9 us
    all_to_all x1, starting transfers between devices, local(): queries = lax.all_to_all(queries, 'seq', 0, 0, tiled=True)  9.5 us
    all_to_all x1, starting transfers between devices, local(): cand_parts = lax.all_to_all(copies, 'head', 0, 0, tiled=True)  9.21 us
    ppermute x3, starting transfers between devices, local(): lax.ppermute(share, 'seq', [(s, s ^ offset) for s in range(owners)])  9.2 us
    ppermute x3, waiting for transfers between devices, local(): lax.ppermute(share, 'seq', [(s, s ^ offset) for s in range(owners)])  6.79 us
  transfers between devices with their start and end apart: 7, of which 4 were waited for; matrix products, arithmetic and copies ran while one was open for 1% of the time, Pallas kernels for 1%

profile of v3, /device:TPU:2, one launch (start us, length us, event | category | flops | bytes accessed | tf_op | source)
XLA Modules:
  0.0 157.2 jit_solution(2111362852022965043)
XLA Ops:
  0.0 66.1 %share.1 = (bf16[2,1024,128]{2,1,0:T(8,128)(2,1)}, bf16[2,1024,128]{2,1,0:T(8,128)(2,1)}, bf16[2,1024,128]{2,1,0:T(8,128)(2,1)}, bf16[2,1024,128]{2,1,0:T(8,128)...) custom-call(s32[1]{0:T(128)} %bitcast.place_ref, s32[1,64]{1,0:T(1,128)} %bitcast.6, ...), custom_call_target="tpu_custom_call" | custom-call | tf_op jit(solution)/shard_map/share/pallas_call | solution.py:183
  66.2 9.2 %all-to-all-start = ((bf16[4,64,256]{2,1,0:T(8,128)(2,1)}), bf16[4,64,256]{2,1,0:T(8,128)(2,1)S(1)}, u32[]{:S(2)}, u32[]{:S(2)}) async-start(bf16[4,64,256]{2,1,0:T(8,128)(2,1)} %get-tuple-element.16), calls=%async_computation | async-start | bytes 262144 | tf_op jit(solution)/shard_map/all_to_all | solution.py:202
  75.4 1.9 %collective-permute-start = (bf16[2,1024,128]{2,1,0:T(8,128)(2,1)}, bf16[2,1024,128]{2,1,0:T(8,128)(2,1)S(1)}, u32[]{:S(2)}, u32[]{:S(2)}) collective-permute-start(bf16[2,1024,128]{2,1,0:T(8,128)(2,1)} %get-tuple-element.19), channel_id=1, source_target_pairs={{0,64},{16,80},{32,96},{48,112},{64,0},{80,16},{96,32},{112,48},{1... | collective-permute-start | bytes 1572872 | tf_op jit(solution)/shard_map/ppermute | solution.py:198
  77.3 1.9 %collective-permute-start.1 = (bf16[2,1024,128]{2,1,0:T(8,128)(2,1)}, bf16[2,1024,128]{2,1,0:T(8,128)(2,1)S(1)}, u32[]{:S(2)}, u32[]{:S(2)}) collective-permute-start(bf16[2,1024,128]{2,1,0:T(8,128)(2,1)} %get-tuple-element.20), channel_id=1, source_target_pairs={{0,16},{16,0},{32,48},{48,32},{64,80},{80,64},{96,112},{112,96},{1... | collective-permute-start | bytes 1572872 | tf_op jit(solution)/shard_map/ppermute | solution.py:198
  79.2 5.4 %collective-permute-start.2 = (bf16[2,1024,128]{2,1,0:T(8,128)(2,1)}, bf16[2,1024,128]{2,1,0:T(8,128)(2,1)S(1)}, u32[]{:S(2)}, u32[]{:S(2)}) collective-permute-start(bf16[2,1024,128]{2,1,0:T(8,128)(2,1)} %get-tuple-element.21), channel_id=1, source_target_pairs={{0,80},{16,64},{32,112},{48,96},{64,16},{80,0},{96,48},{112,32},{1... | collective-permute-start | bytes 1572872 | tf_op jit(solution)/shard_map/ppermute | solution.py:198
  84.6 0.0 copy-start.3
  84.6 1.5 copy.8
  86.1 0.0 all-to-all-done.cand_ref
  86.1 0.0 copy-done.3
  86.1 1.2 project.1
  87.3 0.0 copy-start
  87.3 9.5 %all-to-all-start.1 = ((bf16[32,32,128]{2,1,0:T(8,128)(2,1)}), bf16[32,32,128]{2,1,0:T(8,128)(2,1)S(1)}, u32[]{:S(2)}, u32[]{:S(2)}) async-start(bf16[32,32,128]{2,1,0:T(8,128)(2,1)} %get-tuple-element.17), calls=%async_computation.1 | async-start | bytes 524288 | tf_op jit(solution)/shard_map/all_to_all | solution.py:218
  96.8 0.0 copy-start.4
  96.8 0.0 collective-permute-done.rest_1_
  96.8 0.0 collective-permute-done.1.rest_2_
  96.8 6.8 %collective-permute-done.2.rest_3_ = bf16[2,1024,128]{2,1,0:T(8,128)(2,1)S(1)} collective-permute-done((bf16[2,1024,128]{2,1,0:T(8,128)(2,1)}, bf16[2,1024,128]{2,1,0:T(8,128)(2,1)S(1)}, u32[]{:S(2)}, u32[]{:S(2)}) %collective-permute-start.2) | collective-permute-done | bytes 524320 | tf_op jit(solution)/shard_map/ppermute | solution.py:198
  103.6 13.3 %all-to-all-done.1.query_ref = bf16[32,32,128]{2,1,0:T(8,128)(2,1)S(1)} async-done(((bf16[32,32,128]{2,1,0:T(8,128)(2,1)}), bf16[32,32,128]{2,1,0:T(8,128)(2,1)S(1)}, u32[]{:S(2)}, u32[]{:S(2)}) %all-to-all-start.1) | async-done | bytes 262176 | tf_op jit(solution)/shard_map/all_to_all | solution.py:218
  116.9 0.0 copy-done
  116.9 0.0 copy-done.4
  116.9 10.9 %attend.1 = bf16[32,32,128]{2,1,0:T(8,128)(2,1)} custom-call(s32[1]{0:T(128)} %bitcast.place_ref, s32[2]{0:T(128)S(1)} %copy-done.4, bf16[32,32,128]{2,1,0:T(8,128)(2,1)S(1)} %all-to-all-done.1.query_ref, bf16[2,1024,128]{2,1,0:T(8,128)(2,1)S(1)} %copy-done, bf16[2,1024,128]{2,1,0:T(8,128)(2,1)S(1)} %collective-permute-done.rest_1_, ...), custom_call_target="tpu_custom_call" | custom-call | tf_op jit(solution)/shard_map/attend/pallas_call | solution.py:219
  127.8 0.0 copy-start.1
  127.8 5.7 %all-to-all-start.2 = ((bf16[32,32,128]{2,1,0:T(8,128)(2,1)}), bf16[32,32,128]{2,1,0:T(8,128)(2,1)S(1)}, u32[]{:S(2)}, u32[]{:S(2)}) async-start(bf16[32,32,128]{2,1,0:T(8,128)(2,1)} %attend.1), calls=%async_computation.2 | async-start | bytes 524288 | tf_op jit(solution)/shard_map/all_to_all | solution.py:231
  133.5 0.0 copy-start.2
  133.5 11.9 %all-to-all-done.2.partial_ref = bf16[32,32,128]{2,1,0:T(8,128)(2,1)S(1)} async-done(((bf16[32,32,128]{2,1,0:T(8,128)(2,1)}), bf16[32,32,128]{2,1,0:T(8,128)(2,1)S(1)}, u32[]{:S(2)}, u32[]{:S(2)}) %all-to-all-start.2) | async-done | bytes 262176 | tf_op jit(solution)/shard_map/all_to_all | solution.py:231
  145.4 0.0 copy-done.1
  145.4 0.0 copy-done.2
  145.4 1.6 %finish.1 = bf16[4,64,256]{2,1,0:T(8,128)(2,1)} custom-call(s32[2]{0:T(128)S(1)} %copy-done.4, bf16[64,64]{1,0:T(8,128)(2,1)S(1)} %copy-done.2, bf16[32,32,128]{2,1,0:T(8,128)(2,1)S(1)} %all-to-all-done.2.partial_ref, f32[64,256]{1,0:T(8,128)S(1)} %convert_element_type.7.gate_ref, bf16[256,1024]{1,0:T(8,128)(2,1)S(1)} %copy-done.1), custom_call_target="tpu_custom_call" | custom-call | tf_op jit(solution)/shard_map/finish/pallas_call | solution.py:232
  147.1 0.0 copy-start.5
  147.1 4.9 %all-to-all-start.3 = ((bf16[4,64,256]{2,1,0:T(8,128)(2,1)}), bf16[4,64,256]{2,1,0:T(8,128)(2,1)S(1)}, u32[]{:S(2)}, u32[]{:S(2)}) async-start(bf16[4,64,256]{2,1,0:T(8,128)(2,1)} %finish.1), calls=%async_computation.3 | async-start | bytes 262144 | tf_op jit(solution)/shard_map/all_to_all | solution.py:240
  152.0 0.0 copy-done.5
  152.0 4.5 %all-to-all-done.3.term_ref = bf16[4,64,256]{2,1,0:T(8,128)(2,1)S(1)} async-done(((bf16[4,64,256]{2,1,0:T(8,128)(2,1)}), bf16[4,64,256]{2,1,0:T(8,128)(2,1)S(1)}, u32[]{:S(2)}, u32[]{:S(2)}) %all-to-all-start.3) | async-done | bytes 131104 | tf_op jit(solution)/shard_map/all_to_all | solution.py:240
  156.5 0.6 add.1
  (2 shorter events, 0.0 us)
Async XLA Ops:
  66.2 19.9 %all-to-all-start = ((bf16[4,64,256]{2,1,0:T(8,128)(2,1)}), bf16[4,64,256]{2,1,0:T(8,128)(2,1)S(1)}, u32[]{:S(2)}, u32[]{:S(2)}) async-start(bf16[4,64,256]{2,1,0:T(8,128)(2,1)} %get-tuple-element.16), calls=%async_computation | async-start | bytes 262144 | tf_op jit(solution)/shard_map/all_to_all | solution.py:202
  75.4 21.4 %collective-permute-start = (bf16[2,1024,128]{2,1,0:T(8,128)(2,1)}, bf16[2,1024,128]{2,1,0:T(8,128)(2,1)S(1)}, u32[]{:S(2)}, u32[]{:S(2)}) collective-permute-start(bf16[2,1024,128]{2,1,0:T(8,128)(2,1)} %get-tuple-element.19), channel_id=1, source_target_pairs={{0,64},{16,80},{32,96},{48,112},{64,0},{80,16},{96,32},{112,48},{1... | collective-permute-start | bytes 1572872 | tf_op jit(solution)/shard_map/ppermute | solution.py:198
  77.3 19.5 %collective-permute-start.1 = (bf16[2,1024,128]{2,1,0:T(8,128)(2,1)}, bf16[2,1024,128]{2,1,0:T(8,128)(2,1)S(1)}, u32[]{:S(2)}, u32[]{:S(2)}) collective-permute-start(bf16[2,1024,128]{2,1,0:T(8,128)(2,1)} %get-tuple-element.20), channel_id=1, source_target_pairs={{0,16},{16,0},{32,48},{48,32},{64,80},{80,64},{96,112},{112,96},{1... | collective-permute-start | bytes 1572872 | tf_op jit(solution)/shard_map/ppermute | solution.py:198
  79.2 24.4 %collective-permute-start.2 = (bf16[2,1024,128]{2,1,0:T(8,128)(2,1)}, bf16[2,1024,128]{2,1,0:T(8,128)(2,1)S(1)}, u32[]{:S(2)}, u32[]{:S(2)}) collective-permute-start(bf16[2,1024,128]{2,1,0:T(8,128)(2,1)} %get-tuple-element.21), channel_id=1, source_target_pairs={{0,80},{16,64},{32,112},{48,96},{64,16},{80,0},{96,48},{112,32},{1... | collective-permute-start | bytes 1572872 | tf_op jit(solution)/shard_map/ppermute | solution.py:198
  84.6 1.5 copy-start.3
  87.3 29.7 %copy-start = (bf16[2,1024,128]{2,1,0:T(8,128)(2,1)S(1)}, bf16[2,1024,128]{2,1,0:T(8,128)(2,1)}, u32[]{:S(2)}) copy-start(bf16[2,1024,128]{2,1,0:T(8,128)(2,1)} %get-tuple-element.18.rest_0_) | copy-start | bytes 1572868
  87.3 29.7 %all-to-all-start.1 = ((bf16[32,32,128]{2,1,0:T(8,128)(2,1)}), bf16[32,32,128]{2,1,0:T(8,128)(2,1)S(1)}, u32[]{:S(2)}, u32[]{:S(2)}) async-start(bf16[32,32,128]{2,1,0:T(8,128)(2,1)} %get-tuple-element.17), calls=%async_computation.1 | async-start | bytes 524288 | tf_op jit(solution)/shard_map/all_to_all | solution.py:218
  96.8 20.2 %copy-start.4 = (s32[2]{0:T(128)S(1)}, s32[2]{0:T(128)}, u32[]{:S(2)}) copy-start(s32[2]{0:T(128)} %length_ref.3) | copy-start | bytes 28
  127.8 17.6 %copy-start.1 = (bf16[256,1024]{1,0:T(8,128)(2,1)S(1)}, bf16[256,1024]{1,0:T(8,128)(2,1)}, u32[]{:S(2)}) copy-start(bf16[256,1024]{1,0:T(8,128)(2,1)} %weight_ref.1) | copy-start | bytes 1572868
  127.8 17.6 %all-to-all-start.2 = ((bf16[32,32,128]{2,1,0:T(8,128)(2,1)}), bf16[32,32,128]{2,1,0:T(8,128)(2,1)S(1)}, u32[]{:S(2)}, u32[]{:S(2)}) async-start(bf16[32,32,128]{2,1,0:T(8,128)(2,1)} %attend.1), calls=%async_computation.2 | async-start | bytes 524288 | tf_op jit(solution)/shard_map/all_to_all | solution.py:231
  133.5 11.9 %copy-start.2 = (bf16[64,64]{1,0:T(8,128)(2,1)S(1)}, bf16[64,64]{1,0:T(8,128)(2,1)}, u32[]{:S(2)}) copy-start(bf16[64,64]{1,0:T(8,128)(2,1)} %get-tuple-element.14.back_ref) | copy-start | bytes 24580
  147.1 4.9 %copy-start.5 = (bf16[64,256]{1,0:T(8,128)(2,1)S(1)}, bf16[64,256]{1,0:T(8,128)(2,1)}, u32[]{:S(2)}) copy-start(bf16[64,256]{1,0:T(8,128)(2,1)} %cand_ref.1) | copy-start | bytes 98308
  147.1 9.5 %all-to-all-start.3 = ((bf16[4,64,256]{2,1,0:T(8,128)(2,1)}), bf16[4,64,256]{2,1,0:T(8,128)(2,1)S(1)}, u32[]{:S(2)}, u32[]{:S(2)}) async-start(bf16[4,64,256]{2,1,0:T(8,128)(2,1)} %finish.1), calls=%async_computation.3 | async-start | bytes 262144 | tf_op jit(solution)/shard_map/all_to_all | solution.py:240

commit v4 on v3

--- a/solution.py
+++ b/solution.py
@@ -15,11 +15,20 @@
 PARAMS = pltpu.CompilerParams(vmem_limit_bytes=48 * 2**20)
 
 
-SQUARE = (0, 4, 1, 5)
+SOURCES = 4
 
 
 def role(place):
-    return (place // 4) % 2, place % 2
+    return (place // 4) % 2, (place // 8 + place) % 2
+
+
+def source(place, index, owners):
+    if index == 0:
+        return place
+    if index == 3:
+        return place + 1 - 2 * (place % 2)
+    step = 4 - 8 * ((place // 4) % 2)
+    return (place + (step if index == 1 else -step) + owners) % owners
 
 
 def head_mask(shape, head):
@@ -66,13 +75,13 @@
 
 
 def share_kernel(
-    place_ref, user_ref, cand_ref, key_ref, value_ref, *rest
+    owners, place_ref, user_ref, cand_ref, key_ref, value_ref, *rest
 ):
-    out_refs, (copy_ref, order_ref, back_ref, sems) = rest[: len(SQUARE)], rest[len(SQUARE) :]
+    out_refs, (copy_ref, order_ref, back_ref, sems) = rest[:SOURCES], rest[SOURCES:]
     lanes = out_refs[0].shape[2]
     copies = []
-    for index, (out_ref, offset) in enumerate(zip(out_refs, SQUARE)):
-        user, half = role(place_ref[0] ^ offset)
+    for index, out_ref in enumerate(out_refs):
+        user, half = role(source(place_ref[0], index, owners))
         here = pl.ds(pl.multiple_of(half * lanes, lanes), lanes)
         for kind, history_ref in enumerate((key_ref, value_ref)):
             copies.append(
@@ -95,17 +104,17 @@
 def attend_kernel(
     rows_now, positions_now, place_ref, length_ref, query_ref, *rest
 ):
-    history_refs, (out_ref, keys, masked) = rest[: len(SQUARE)], rest[len(SQUARE) :]
+    history_refs, (out_ref, keys, masked) = rest[:SOURCES], rest[SOURCES:]
     blocks, block_rows, width = query_ref.shape
     heads = width // HEAD_DIM
     span = history_refs[0].shape[1]
-    positions = span * len(SQUARE)
+    positions = span * SOURCES
     step_blocks = rows_now // block_rows
     user, _ = role(place_ref[0])
     length = length_ref[user]
-    for index, (offset, history_ref) in enumerate(zip(SQUARE, history_refs)):
+    for index, history_ref in enumerate(history_refs):
         at = slice(index * span, (index + 1) * span)
-        live = length - (place_ref[0] ^ offset) * span
+        live = length - source(place_ref[0], index, blocks) * span
         keys[:, at] = history_ref[0].T
         position = lax.broadcasted_iota(jnp.int32, (span, width), 0)
         value = history_ref[1]
@@ -181,22 +190,22 @@
     block_rows, lanes = rows // USERS, width // 2
 
     *shares, copies, order, back = pl.pallas_call(
-        share_kernel,
-        out_shape=[jax.ShapeDtypeStruct((2, positions, lanes), jnp.bfloat16) for _ in SQUARE]
+        functools.partial(share_kernel, owners),
+        out_shape=[jax.ShapeDtypeStruct((2, positions, lanes), jnp.bfloat16)] * SOURCES
         + [
             jax.ShapeDtypeStruct((groups, rows, depth), jnp.bfloat16),
             jax.ShapeDtypeStruct((rows, rows), jnp.bfloat16),
             jax.ShapeDtypeStruct((rows, rows), jnp.bfloat16),
         ],
         in_specs=[SMEM, VMEM, VMEM, HBM, HBM],
-        out_specs=[HBM] * len(SQUARE) + [VMEM] * 3,
-        scratch_shapes=[pltpu.SemaphoreType.DMA((len(SQUARE), 2))],
+        out_specs=[VMEM] * (SOURCES + 3),
+        scratch_shapes=[pltpu.SemaphoreType.DMA((SOURCES, 2))],
         compiler_params=pltpu.CompilerParams(vmem_limit_bytes=60 * 2**20),
         name="share",
     )(place, cand_user.reshape(1, rows), cand_rows, keys, values)
-    history = [
-        lax.ppermute(share, "seq", [(s, s ^ offset) for s in range(owners)]) if offset else share
-        for share, offset in zip(shares, SQUARE)
+    history = shares[:1] + [
+        lax.ppermute(shares[index], "seq", [(s, source(s, index, owners)) for s in range(owners)])
+        for index in range(1, SOURCES)
     ]
 
     cand_parts = lax.all_to_all(copies, "head", 0, 0, tiled=True)
@@ -219,11 +228,11 @@
     totals = pl.pallas_call(
         functools.partial(attend_kernel, 1024, 256),
         out_shape=jax.ShapeDtypeStruct((owners, block_rows, lanes), jnp.bfloat16),
-        in_specs=[SMEM] * 2 + [VMEM] * (1 + len(SQUARE)),
+        in_specs=[SMEM] * 2 + [VMEM] * (1 + SOURCES),
         out_specs=VMEM,
         scratch_shapes=[
-            pltpu.VMEM((lanes, len(SQUARE) * positions), jnp.bfloat16),
-            pltpu.VMEM((lanes // HEAD_DIM, len(SQUARE) * positions, lanes), jnp.bfloat16),
+            pltpu.VMEM((lanes, SOURCES * positions), jnp.bfloat16),
+            pltpu.VMEM((lanes // HEAD_DIM, SOURCES * positions, lanes), jnp.bfloat16),
         ],
         compiler_params=PARAMS,
         name="attend",

time: 158 us -> 86 us (0.54)
  Pallas kernels: 80.5 us -> 18 us
  waiting for transfers between devices: 36.5 us -> 28.4 us
    pallas_call x1, Pallas kernels: 66.1 us -> 3.73 us  [local(): pl.pallas_call(functools.partial(share_kernel, owners), out_shape=[jax.Sh...]
    all_to_all x1, waiting for transfers between devices: 13.3 us -> 8.01 us  [local(): queries = lax.all_to_all(queries, 'seq', 0, 0, tiled=True)]
    ppermute x3, starting transfers between devices: 9.2 us -> 12.5 us  [local(): lax.ppermute(shares[index], 'seq', [(s, source(s, index, owners)) for s i...]
    all_to_all x1, starting transfers between devices: 9.5 us -> 6.2 us  [local(): queries = lax.all_to_all(queries, 'seq', 0, 0, tiled=True)]
    ppermute x3, waiting for transfers between devices: 6.79 us -> 3.91 us  [local(): lax.ppermute(shares[index], 'seq', [(s, source(s, index, owners)) for s i...]
  transfers between devices with their start and end apart: 7 -> 7, of which waited for: 4 -> 4; matrix products, arithmetic and copies ran while one was open for 1% -> 2% of each run, Pallas kernels for 1% -> 1%
where the time goes in v4:
time: 86 us; the launch traced here: 85.3 us
  starting transfers between devices  37.2 us (43%)
  waiting for transfers between devices  28.4 us (33%)
  Pallas kernels  18 us (21%)
  local copies, waits for them, and re-layouts  1.48 us (2%)
    ppermute x3, starting transfers between devices, local(): lax.ppermute(shares[index], 'seq', [(s, source(s, index, owners)) for s i...  12.5 us
    all_to_all x1, waiting for transfers between devices, local(): totals = lax.all_to_all(totals, 'seq', 0, 0, tiled=True)  11.9 us
    pallas_call x1, Pallas kernels, local(): pl.pallas_call(functools.partial(attend_kernel, 1024, 256), out_shape=jax...  10.8 us
    all_to_all x1, starting transfers between devices, local(): cand_parts = lax.all_to_all(copies, 'head', 0, 0, tiled=True)  9.21 us
    all_to_all x1, waiting for transfers between devices, local(): queries = lax.all_to_all(queries, 'seq', 0, 0, tiled=True)  8.01 us
    all_to_all x1, starting transfers between devices, local(): queries = lax.all_to_all(queries, 'seq', 0, 0, tiled=True)  6.2 us
    all_to_all x1, starting transfers between devices, local(): terms = lax.all_to_all(terms, 'head', 0, 0, tiled=True)  4.92 us
    all_to_all x1, waiting for transfers between devices, local(): terms = lax.all_to_all(terms, 'head', 0, 0, tiled=True)  4.51 us
  transfers between devices with their start and end apart: 7, of which 4 were waited for; matrix products, arithmetic and copies ran while one was open for 2% of the time, Pallas kernels for 1%

profile of v4, /device:TPU:2, one launch (start us, length us, event | category | flops | bytes accessed | tf_op | source)
XLA Modules:
  0.0 85.3 jit_solution(6262663412844201005)
XLA Ops:
  0.0 3.7 %share.1 = (bf16[2,1024,128]{2,1,0:T(8,128)(2,1)}, bf16[2,1024,128]{2,1,0:T(8,128)(2,1)}, bf16[2,1024,128]{2,1,0:T(8,128)(2,1)}, bf16[2,1024,128]{2,1,0:T(8,128)...) custom-call(s32[1]{0:T(128)} %bitcast.place_ref, s32[1,64]{1,0:T(1,128)} %bitcast.6, ...), custom_call_target="tpu_custom_call" | custom-call | tf_op jit(solution)/shard_map/share/pallas_call | solution.py:192
  3.7 9.2 %all-to-all-start = ((bf16[4,64,256]{2,1,0:T(8,128)(2,1)}), bf16[4,64,256]{2,1,0:T(8,128)(2,1)S(1)}, u32[]{:S(2)}, u32[]{:S(2)}) async-start(bf16[4,64,256]{2,1,0:T(8,128)(2,1)} %get-tuple-element.16), calls=%async_computation | async-start | bytes 262144 | tf_op jit(solution)/shard_map/all_to_all | solution.py:211
  13.0 1.9 %collective-permute-start = (bf16[2,1024,128]{2,1,0:T(8,128)(2,1)}, bf16[2,1024,128]{2,1,0:T(8,128)(2,1)S(1)}, u32[]{:S(2)}, u32[]{:S(2)}) collective-permute-start(bf16[2,1024,128]{2,1,0:T(8,128)(2,1)} %get-tuple-element.19), channel_id=1, source_target_pairs={{0,64},{16,80},{32,96},{48,112},{64,0},{80,16},{96,32},{112,48},{1... | collective-permute-start | bytes 1572872 | tf_op jit(solution)/shard_map/ppermute | solution.py:207
  14.9 7.1 %collective-permute-start.1 = (bf16[2,1024,128]{2,1,0:T(8,128)(2,1)}, bf16[2,1024,128]{2,1,0:T(8,128)(2,1)S(1)}, u32[]{:S(2)}, u32[]{:S(2)}) collective-permute-start(bf16[2,1024,128]{2,1,0:T(8,128)(2,1)} %get-tuple-element.20), channel_id=1, source_target_pairs={{0,448},{16,464},{32,480},{48,496},{64,128},{80,144},{96,160},{112... | collective-permute-start | bytes 1572872 | tf_op jit(solution)/shard_map/ppermute | solution.py:207
  22.0 3.5 %collective-permute-start.2 = (bf16[2,1024,128]{2,1,0:T(8,128)(2,1)}, bf16[2,1024,128]{2,1,0:T(8,128)(2,1)S(1)}, u32[]{:S(2)}, u32[]{:S(2)}) collective-permute-start(bf16[2,1024,128]{2,1,0:T(8,128)(2,1)} %get-tuple-element.21), channel_id=1, source_target_pairs={{0,16},{16,0},{32,48},{48,32},{64,80},{80,64},{96,112},{112,96},{1... | collective-permute-start | bytes 1572872 | tf_op jit(solution)/shard_map/ppermute | solution.py:207
  25.5 0.0 copy-start.3
  25.5 1.5 %copy.8 = bf16[128,8,2,256]{3,1,2,0:T(8,128)(2,1)S(1)} copy(bf16[128,8,2,256]{3,2,1,0:T(2,128)(2,1)} %bitcast.5) | data formatting | bytes 2097152
  27.0 0.0 all-to-all-done.cand_ref
  27.0 0.0 copy-done.3
  27.0 1.2 %project.1 = (bf16[32,32,128]{2,1,0:T(8,128)(2,1)}, bf16[64,256]{1,0:T(8,128)(2,1)S(1)}) custom-call(bf16[64,64]{1,0:T(8,128)(2,1)S(1)} %copy-done.3, bf16[4,64,256]{2,1,0:T(8,128)(2,1)S(1)} %all-to-all-done.cand_ref, bf16[1024,512]{1,0:T(8,128)(2,1)S(1)} %bitcast.4), custom_call_target="tpu_custom_call" | custom-call | tf_op jit(solution)/shard_map/project/pallas_call | solution.py:212
  28.2 0.0 copy-start
  28.2 6.2 %all-to-all-start.1 = ((bf16[32,32,128]{2,1,0:T(8,128)(2,1)}), bf16[32,32,128]{2,1,0:T(8,128)(2,1)S(1)}, u32[]{:S(2)}, u32[]{:S(2)}) async-start(bf16[32,32,128]{2,1,0:T(8,128)(2,1)} %get-tuple-element.17), calls=%async_computation.1 | async-start | bytes 524288 | tf_op jit(solution)/shard_map/all_to_all | solution.py:227
  34.4 0.0 copy-start.4
  34.4 0.0 collective-permute-done.rest_1_
  34.4 0.0 collective-permute-done.1.rest_2_
  34.4 3.9 %collective-permute-done.2.rest_3_ = bf16[2,1024,128]{2,1,0:T(8,128)(2,1)S(1)} collective-permute-done((bf16[2,1024,128]{2,1,0:T(8,128)(2,1)}, bf16[2,1024,128]{2,1,0:T(8,128)(2,1)S(1)}, u32[]{:S(2)}, u32[]{:S(2)}) %collective-permute-start.2) | collective-permute-done | bytes 524320 | tf_op jit(solution)/shard_map/ppermute | solution.py:207
  38.3 8.0 %all-to-all-done.1.query_ref = bf16[32,32,128]{2,1,0:T(8,128)(2,1)S(1)} async-done(((bf16[32,32,128]{2,1,0:T(8,128)(2,1)}), bf16[32,32,128]{2,1,0:T(8,128)(2,1)S(1)}, u32[]{:S(2)}, u32[]{:S(2)}) %all-to-all-start.1) | async-done | bytes 262176 | tf_op jit(solution)/shard_map/all_to_all | solution.py:227
  46.3 0.0 copy-done
  46.3 0.0 copy-done.4
  46.3 10.8 %attend.1 = bf16[32,32,128]{2,1,0:T(8,128)(2,1)} custom-call(s32[1]{0:T(128)} %bitcast.place_ref, s32[2]{0:T(128)S(1)} %copy-done.4, bf16[32,32,128]{2,1,0:T(8,128)(2,1)S(1)} %all-to-all-done.1.query_ref, bf16[2,1024,128]{2,1,0:T(8,128)(2,1)S(1)} %copy-done, bf16[2,1024,128]{2,1,0:T(8,128)(2,1)S(1)} %collective-permute-done.rest_1_, ...), custom_call_target="tpu_custom_call" | custom-call | tf_op jit(solution)/shard_map/attend/pallas_call | solution.py:228
  57.2 0.0 copy-start.1
  57.2 4.4 %all-to-all-start.2 = ((bf16[32,32,128]{2,1,0:T(8,128)(2,1)}), bf16[32,32,128]{2,1,0:T(8,128)(2,1)S(1)}, u32[]{:S(2)}, u32[]{:S(2)}) async-start(bf16[32,32,128]{2,1,0:T(8,128)(2,1)} %attend.1), calls=%async_computation.2 | async-start | bytes 524288 | tf_op jit(solution)/shard_map/all_to_all | solution.py:240
  61.6 0.0 copy-start.2
  61.6 11.9 %all-to-all-done.2.partial_ref = bf16[32,32,128]{2,1,0:T(8,128)(2,1)S(1)} async-done(((bf16[32,32,128]{2,1,0:T(8,128)(2,1)}), bf16[32,32,128]{2,1,0:T(8,128)(2,1)S(1)}, u32[]{:S(2)}, u32[]{:S(2)}) %all-to-all-start.2) | async-done | bytes 262176 | tf_op jit(solution)/shard_map/all_to_all | solution.py:240
  73.5 0.0 copy-done.1
  73.5 0.0 copy-done.2
  73.5 1.6 %finish.1 = bf16[4,64,256]{2,1,0:T(8,128)(2,1)} custom-call(s32[2]{0:T(128)S(1)} %copy-done.4, bf16[64,64]{1,0:T(8,128)(2,1)S(1)} %copy-done.2, bf16[32,32,128]{2,1,0:T(8,128)(2,1)S(1)} %all-to-all-done.2.partial_ref, f32[64,256]{1,0:T(8,128)S(1)} %convert_element_type.7.gate_ref, bf16[256,1024]{1,0:T(8,128)(2,1)S(1)} %copy-done.1), custom_call_target="tpu_custom_call" | custom-call | tf_op jit(solution)/shard_map/finish/pallas_call | solution.py:241
  75.2 0.0 copy-start.5
  75.2 4.9 %all-to-all-start.3 = ((bf16[4,64,256]{2,1,0:T(8,128)(2,1)}), bf16[4,64,256]{2,1,0:T(8,128)(2,1)S(1)}, u32[]{:S(2)}, u32[]{:S(2)}) async-start(bf16[4,64,256]{2,1,0:T(8,128)(2,1)} %finish.1), calls=%async_computation.3 | async-start | bytes 262144 | tf_op jit(solution)/shard_map/all_to_all | solution.py:249
  80.1 0.0 copy-done.5
  80.1 4.5 %all-to-all-done.3.term_ref = bf16[4,64,256]{2,1,0:T(8,128)(2,1)S(1)} async-done(((bf16[4,64,256]{2,1,0:T(8,128)(2,1)}), bf16[4,64,256]{2,1,0:T(8,128)(2,1)S(1)}, u32[]{:S(2)}, u32[]{:S(2)}) %all-to-all-start.3) | async-done | bytes 131104 | tf_op jit(solution)/shard_map/all_to_all | solution.py:249
  84.6 0.6 add.1
  (2 shorter events, 0.0 us)
Async XLA Ops:
  3.7 23.2 %all-to-all-start = ((bf16[4,64,256]{2,1,0:T(8,128)(2,1)}), bf16[4,64,256]{2,1,0:T(8,128)(2,1)S(1)}, u32[]{:S(2)}, u32[]{:S(2)}) async-start(bf16[4,64,256]{2,1,0:T(8,128)(2,1)} %get-tuple-element.16), calls=%async_computation | async-start | bytes 262144 | tf_op jit(solution)/shard_map/all_to_all | solution.py:211
  13.0 21.4 %collective-permute-start = (bf16[2,1024,128]{2,1,0:T(8,128)(2,1)}, bf16[2,1024,128]{2,1,0:T(8,128)(2,1)S(1)}, u32[]{:S(2)}, u32[]{:S(2)}) collective-permute-start(bf16[2,1024,128]{2,1,0:T(8,128)(2,1)} %get-tuple-element.19), channel_id=1, source_target_pairs={{0,64},{16,80},{32,96},{48,112},{64,0},{80,16},{96,32},{112,48},{1... | collective-permute-start | bytes 1572872 | tf_op jit(solution)/shard_map/ppermute | solution.py:207
  14.9 19.5 %collective-permute-start.1 = (bf16[2,1024,128]{2,1,0:T(8,128)(2,1)}, bf16[2,1024,128]{2,1,0:T(8,128)(2,1)S(1)}, u32[]{:S(2)}, u32[]{:S(2)}) collective-permute-start(bf16[2,1024,128]{2,1,0:T(8,128)(2,1)} %get-tuple-element.20), channel_id=1, source_target_pairs={{0,448},{16,464},{32,480},{48,496},{64,128},{80,144},{96,160},{112... | collective-permute-start | bytes 1572872 | tf_op jit(solution)/shard_map/ppermute | solution.py:207
  22.0 16.3 %collective-permute-start.2 = (bf16[2,1024,128]{2,1,0:T(8,128)(2,1)}, bf16[2,1024,128]{2,1,0:T(8,128)(2,1)S(1)}, u32[]{:S(2)}, u32[]{:S(2)}) collective-permute-start(bf16[2,1024,128]{2,1,0:T(8,128)(2,1)} %get-tuple-element.21), channel_id=1, source_target_pairs={{0,16},{16,0},{32,48},{48,32},{64,80},{80,64},{96,112},{112,96},{1... | collective-permute-start | bytes 1572872 | tf_op jit(solution)/shard_map/ppermute | solution.py:207
  25.5 1.5 %copy-start.3 = (bf16[64,64]{1,0:T(8,128)(2,1)S(1)}, bf16[64,64]{1,0:T(8,128)(2,1)}, u32[]{:S(2)}) copy-start(bf16[64,64]{1,0:T(8,128)(2,1)} %get-tuple-element.15.place_ref) | copy-start | bytes 24580
  28.2 18.2 %copy-start = (bf16[2,1024,128]{2,1,0:T(8,128)(2,1)S(1)}, bf16[2,1024,128]{2,1,0:T(8,128)(2,1)}, u32[]{:S(2)}) copy-start(bf16[2,1024,128]{2,1,0:T(8,128)(2,1)} %get-tuple-element.18.rest_0_) | copy-start | bytes 1572868
  28.2 18.2 %all-to-all-start.1 = ((bf16[32,32,128]{2,1,0:T(8,128)(2,1)}), bf16[32,32,128]{2,1,0:T(8,128)(2,1)S(1)}, u32[]{:S(2)}, u32[]{:S(2)}) async-start(bf16[32,32,128]{2,1,0:T(8,128)(2,1)} %get-tuple-element.17), calls=%async_computation.1 | async-start | bytes 524288 | tf_op jit(solution)/shard_map/all_to_all | solution.py:227
  34.4 12.0 %copy-start.4 = (s32[2]{0:T(128)S(1)}, s32[2]{0:T(128)}, u32[]{:S(2)}) copy-start(s32[2]{0:T(128)} %length_ref.3) | copy-start | bytes 28
  57.2 16.4 %copy-start.1 = (bf16[256,1024]{1,0:T(8,128)(2,1)S(1)}, bf16[256,1024]{1,0:T(8,128)(2,1)}, u32[]{:S(2)}) copy-start(bf16[256,1024]{1,0:T(8,128)(2,1)} %weight_ref.1) | copy-start | bytes 1572868
  57.2 16.4 %all-to-all-start.2 = ((bf16[32,32,128]{2,1,0:T(8,128)(2,1)}), bf16[32,32,128]{2,1,0:T(8,128)(2,1)S(1)}, u32[]{:S(2)}, u32[]{:S(2)}) async-start(bf16[32,32,128]{2,1,0:T(8,128)(2,1)} %attend.1), calls=%async_computation.2 | async-start | bytes 524288 | tf_op jit(solution)/shard_map/all_to_all | solution.py:240
  61.6 12.0 %copy-start.2 = (bf16[64,64]{1,0:T(8,128)(2,1)S(1)}, bf16[64,64]{1,0:T(8,128)(2,1)}, u32[]{:S(2)}) copy-start(bf16[64,64]{1,0:T(8,128)(2,1)} %get-tuple-element.14.back_ref) | copy-start | bytes 24580
  75.2 4.9 %copy-start.5 = (bf16[64,256]{1,0:T(8,128)(2,1)S(1)}, bf16[64,256]{1,0:T(8,128)(2,1)}, u32[]{:S(2)}) copy-start(bf16[64,256]{1,0:T(8,128)(2,1)} %cand_ref.1) | copy-start | bytes 98308
  75.2 9.4 %all-to-all-start.3 = ((bf16[4,64,256]{2,1,0:T(8,128)(2,1)}), bf16[4,64,256]{2,1,0:T(8,128)(2,1)S(1)}, u32[]{:S(2)}, u32[]{:S(2)}) async-start(bf16[4,64,256]{2,1,0:T(8,128)(2,1)} %finish.1), calls=%async_computation.3 | async-start | bytes 262144 | tf_op jit(solution)/shard_map/all_to_all | solution.py:249

commit v5 on v4

--- a/solution.py
+++ b/solution.py
@@ -12,7 +12,8 @@
 VMEM = pl.BlockSpec(memory_space=pltpu.VMEM)
 SMEM = pl.BlockSpec(memory_space=pltpu.SMEM)
 HBM = pl.BlockSpec(memory_space=pltpu.HBM)
-PARAMS = pltpu.CompilerParams(vmem_limit_bytes=48 * 2**20)
+PARAMS = pltpu.CompilerParams(vmem_limit_bytes=16 * 2**20)
+ATTEND_PARAMS = pltpu.CompilerParams(vmem_limit_bytes=32 * 2**20)
 
 
 SOURCES = 4
@@ -75,52 +76,71 @@
 
 
 def share_kernel(
-    owners, place_ref, user_ref, cand_ref, key_ref, value_ref, *rest
+    owners, place_ref, user_ref, cand_ref, weight_ref, key_ref, value_ref, *rest
 ):
-    out_refs, (copy_ref, order_ref, back_ref, sems) = rest[:SOURCES], rest[SOURCES:]
+    out_refs, rest = rest[:SOURCES], rest[SOURCES:]
+    copy_ref, keep_ref, order_ref, back_ref, held_ref, users, parts, sems, own_sems = rest
     lanes = out_refs[0].shape[2]
-    copies = []
-    for index, out_ref in enumerate(out_refs):
+    first = [
+        pltpu.make_async_copy(cand_ref, keep_ref, own_sems.at[0]),
+        pltpu.make_async_copy(user_ref, users, own_sems.at[1]),
+    ]
+    into = []
+    for index in range(SOURCES):
         user, half = role(source(place_ref[0], index, owners))
         here = pl.ds(pl.multiple_of(half * lanes, lanes), lanes)
         for kind, history_ref in enumerate((key_ref, value_ref)):
-            copies.append(
+            into.append(
                 pltpu.make_async_copy(
-                    history_ref.at[user, :, here], out_ref.at[kind], sems.at[index, kind]
+                    history_ref.at[user, :, here], parts.at[index, kind], sems.at[index, kind]
                 )
             )
-    for copy in copies:
+    last = pltpu.make_async_copy(weight_ref, held_ref, own_sems.at[2])
+    for copy in first + into + [last]:
         copy.start()
-    cand = cand_ref[...]
+    for copy in first:
+        copy.wait()
+    cand = keep_ref[...]
     for group in range(copy_ref.shape[0]):
         copy_ref[group] = cand
-    order, back = orders_of(user_ref[...], cand.shape[0])
+    order, back = orders_of(users[...], cand.shape[0])
     order_ref[...] = order
     back_ref[...] = back
-    for copy in copies:
+    out = []
+    for index, out_ref in enumerate(out_refs):
+        for kind in range(2):
+            into[2 * index + kind].wait()
+            out.append(
+                pltpu.make_async_copy(
+                    parts.at[index, kind], out_ref.at[kind], sems.at[index, kind]
+                )
+            )
+            out[-1].start()
+    last.wait()
+    for copy in out:
         copy.wait()
 
 
-def attend_kernel(
-    rows_now, positions_now, place_ref, length_ref, query_ref, *rest
-):
-    history_refs, (out_ref, keys, masked) = rest[:SOURCES], rest[SOURCES:]
-    blocks, block_rows, width = query_ref.shape
-    heads = width // HEAD_DIM
-    span = history_refs[0].shape[1]
-    positions = span * SOURCES
-    step_blocks = rows_now // block_rows
+def prepare_kernel(owners, place_ref, length_ref, *rest):
+    history_refs, (key_ref, value_ref) = rest[:SOURCES], rest[SOURCES:]
+    _, span, width = history_refs[0].shape
     user, _ = role(place_ref[0])
     length = length_ref[user]
+    position = lax.broadcasted_iota(jnp.int32, (span, width), 0)
     for index, history_ref in enumerate(history_refs):
         at = slice(index * span, (index + 1) * span)
-        live = length - source(place_ref[0], index, blocks) * span
-        keys[:, at] = history_ref[0].T
-        position = lax.broadcasted_iota(jnp.int32, (span, width), 0)
+        live = length - source(place_ref[0], index, owners) * span
+        key_ref[:, at] = history_ref[0].T
         value = history_ref[1]
-        for head in range(heads):
+        for head in range(width // HEAD_DIM):
             keep = (position < live) & head_mask((span, width), head)
-            masked[head, at, :] = jnp.where(keep, value, jnp.zeros_like(value))
+            value_ref[head, at, :] = jnp.where(keep, value, jnp.zeros_like(value))
+
+
+def attend_kernel(rows_now, positions_now, query_ref, keys, masked, out_ref):
+    blocks, block_rows, width = query_ref.shape
+    heads, positions, _ = masked.shape
+    step_blocks = rows_now // block_rows
 
     def step(index, carry):
         here = pl.ds(index * step_blocks, step_blocks)
@@ -143,8 +163,12 @@
     lax.fori_loop(0, blocks // step_blocks, step, 0)
 
 
-def finish_kernel(length_ref, back_ref, partial_ref, gate_ref, weight_ref, out_ref):
+def finish_kernel(
+    length_ref, back_ref, partial_ref, gate_ref, source_ref, out_ref, weight_ref, sem
+):
     rows, width = gate_ref.shape
+    fetch = pltpu.make_async_copy(source_ref, weight_ref, sem)
+    fetch.start()
     sums = {}
     for block in range(partial_ref.shape[0]):
         term = partial_ref[block].astype(jnp.float32)
@@ -165,6 +189,7 @@
     normed = attn * lax.rsqrt(mean + 1e-06)
     gated = (normed * gate_ref[...]).astype(jnp.bfloat16)
     gated = jnp.dot(back_ref[...], gated, preferred_element_type=jnp.float32).astype(jnp.bfloat16)
+    fetch.wait()
     for part in range(out_ref.shape[0]):
         out_ref[part] = jnp.dot(
             gated,
@@ -174,10 +199,14 @@
 
 
 def add_kernel(cand_ref, term_ref, out_ref):
-    total = cand_ref[...]
+    total = cand_ref[...].astype(jnp.float32)
     for group in range(term_ref.shape[0]):
         total += term_ref[group].astype(jnp.float32)
     out_ref[...] = total.astype(out_ref.dtype)
+
+
+def in_hbm(array):
+    return pltpu.with_memory_space_constraint(array, pltpu.HBM)
 
 
 def local(cand_rows, qu_weight, out_weight, keys, values, lengths, cand_user):
@@ -189,20 +218,27 @@
     place = jnp.reshape(lax.axis_index("seq"), (1,)).astype(jnp.int32)
     block_rows, lanes = rows // USERS, width // 2
 
-    *shares, copies, order, back = pl.pallas_call(
+    *shares, copies, kept, order, back, weight = pl.pallas_call(
         functools.partial(share_kernel, owners),
-        out_shape=[jax.ShapeDtypeStruct((2, positions, lanes), jnp.bfloat16)] * SOURCES
+        out_shape=[pltpu.HBM((2, positions, lanes), jnp.bfloat16)] * SOURCES
         + [
             jax.ShapeDtypeStruct((groups, rows, depth), jnp.bfloat16),
-            jax.ShapeDtypeStruct((rows, rows), jnp.bfloat16),
-            jax.ShapeDtypeStruct((rows, rows), jnp.bfloat16),
+            pltpu.VMEM((rows, depth), jnp.bfloat16),
+            pltpu.VMEM((rows, rows), jnp.bfloat16),
+            pltpu.VMEM((rows, rows), jnp.bfloat16),
+            pltpu.VMEM(qu_weight.shape, jnp.bfloat16),
         ],
-        in_specs=[SMEM, VMEM, VMEM, HBM, HBM],
-        out_specs=[VMEM] * (SOURCES + 3),
-        scratch_shapes=[pltpu.SemaphoreType.DMA((SOURCES, 2))],
-        compiler_params=pltpu.CompilerParams(vmem_limit_bytes=60 * 2**20),
+        in_specs=[SMEM] + [HBM] * 5,
+        out_specs=[HBM] * SOURCES + [VMEM] * 5,
+        scratch_shapes=[
+            pltpu.VMEM((1, rows), jnp.int32),
+            pltpu.VMEM((SOURCES, 2, positions, lanes), jnp.bfloat16),
+            pltpu.SemaphoreType.DMA((SOURCES, 2)),
+            pltpu.SemaphoreType.DMA((3,)),
+        ],
+        compiler_params=PARAMS,
         name="share",
-    )(place, cand_user.reshape(1, rows), cand_rows, keys, values)
+    )(place, *map(in_hbm, (cand_user.reshape(1, rows), cand_rows, qu_weight, keys, values)))
     history = shares[:1] + [
         lax.ppermute(shares[index], "seq", [(s, source(s, index, owners)) for s in range(owners)])
         for index in range(1, SOURCES)
@@ -222,30 +258,40 @@
     )(
         order,
         cand_parts,
-        qu_weight.reshape(qu_weight.shape[0], 2 * width),
+        weight.reshape(qu_weight.shape[0], 2 * width),
     )
     queries = lax.all_to_all(queries, "seq", 0, 0, tiled=True)
+    turned, masked = pl.pallas_call(
+        functools.partial(prepare_kernel, owners),
+        out_shape=(
+            jax.ShapeDtypeStruct((lanes, SOURCES * positions), jnp.bfloat16),
+            jax.ShapeDtypeStruct(
+                (lanes // HEAD_DIM, SOURCES * positions, lanes), jnp.bfloat16
+            ),
+        ),
+        in_specs=[SMEM] * 2 + [VMEM] * SOURCES,
+        out_specs=(VMEM, VMEM),
+        compiler_params=PARAMS,
+        name="prepare",
+    )(place, lengths, *map(in_hbm, history))
     totals = pl.pallas_call(
         functools.partial(attend_kernel, 1024, 256),
         out_shape=jax.ShapeDtypeStruct((owners, block_rows, lanes), jnp.bfloat16),
-        in_specs=[SMEM] * 2 + [VMEM] * (1 + SOURCES),
+        in_specs=[VMEM] * 3,
         out_specs=VMEM,
-        scratch_shapes=[
-            pltpu.VMEM((lanes, SOURCES * positions), jnp.bfloat16),
-            pltpu.VMEM((lanes // HEAD_DIM, SOURCES * positions, lanes), jnp.bfloat16),
-        ],
-        compiler_params=PARAMS,
+        compiler_params=ATTEND_PARAMS,
         name="attend",
-    )(place, lengths, queries, *history)
+    )(queries, turned, masked)
     totals = lax.all_to_all(totals, "seq", 0, 0, tiled=True)
     terms = pl.pallas_call(
         finish_kernel,
         out_shape=jax.ShapeDtypeStruct((groups, rows, depth), jnp.bfloat16),
-        in_specs=[SMEM] + [VMEM] * 4,
+        in_specs=[SMEM] + [VMEM] * 3 + [HBM],
         out_specs=VMEM,
+        scratch_shapes=[pltpu.VMEM(out_weight.shape, jnp.bfloat16), pltpu.SemaphoreType.DMA],
         compiler_params=PARAMS,
         name="finish",
-    )(lengths, back, totals, gates.astype(jnp.float32), out_weight)
+    )(lengths, back, totals, gates.astype(jnp.float32), in_hbm(out_weight))
     terms = lax.all_to_all(terms, "head", 0, 0, tiled=True)
     return pl.pallas_call(
         add_kernel,
@@ -254,7 +300,7 @@
         out_specs=VMEM,
         compiler_params=PARAMS,
         name="add",
-    )(cand_rows.astype(jnp.float32), terms)
+    )(kept, terms)
 
 
 def solution(mesh):

time: 86 us -> 84 us (0.977)
  blocking collectives: 0 us -> 9.11 us
  waiting for transfers between devices: 28.4 us -> 20.7 us
  starting transfers between devices: 37.2 us -> 33.4 us
  Pallas kernels: 18 us -> 19.9 us
  local copies, waits for them, and re-layouts: 1.48 us -> 0.24 us
    all_to_all x0 -> x1, blocking collectives: none -> 9.11 us  [local(): terms = lax.all_to_all(terms, 'head', 0, 0, tiled=True)]
    all_to_all x1, waiting for transfers between devices: 8.01 us -> 2.55 us  [local(): queries = lax.all_to_all(queries, 'seq', 0, 0, tiled=True)]
    all_to_all x1 -> x0, starting transfers between devices: 4.92 us -> none  [local(): terms = lax.all_to_all(terms, 'head', 0, 0, tiled=True)]
    all_to_all x1 -> x0, waiting for transfers between devices: 4.51 us -> none  [local(): terms = lax.all_to_all(terms, 'head', 0, 0, tiled=True)]
    pallas_call x1 -> x2, Pallas kernels: 3.73 us -> 6.58 us  [the longest x1 3.43 us: local(): pl.pallas_call(functools.partial(share_kernel, owners), out_shape=[pltpu....]
    ppermute x3, waiting for transfers between devices: 3.91 us -> 6.2 us  [local(): lax.ppermute(shares[index], 'seq', [(s, source(s, index, owners)) for s i...]
    unnamed x13 -> x7, local copies, waits for them, and re-layouts: 1.48 us -> 0.24 us
    all_to_all x1, starting transfers between devices: 4.39 us -> 5.58 us  [local(): totals = lax.all_to_all(totals, 'seq', 0, 0, tiled=True)]
  transfers between devices with their start and end apart: 7 -> 6, of which waited for: 4 -> 4; matrix products, arithmetic and copies ran while one was open for 2% -> 0% of each run, Pallas kernels for 1% -> 5%
where the time goes in v5:
time: 84 us; the launch traced here: 83.5 us
  starting transfers between devices  33.4 us (40%)
  waiting for transfers between devices  20.7 us (25%)
  Pallas kernels  19.9 us (24%)
  blocking collectives  9.11 us (11%)
    ppermute x3, starting transfers between devices, local(): lax.ppermute(shares[index], 'seq', [(s, source(s, index, owners)) for s i...  12.5 us
    all_to_all x1, waiting for transfers between devices, local(): totals = lax.all_to_all(totals, 'seq', 0, 0, tiled=True)  11.9 us
    pallas_call x1, Pallas kernels, local(): pl.pallas_call(functools.partial(attend_kernel, 1024, 256), out_shape=jax...  9.73 us
    all_to_all x1, starting transfers between devices, local(): cand_parts = lax.all_to_all(copies, 'head', 0, 0, tiled=True)  9.21 us
    all_to_all x1, blocking collectives, local(): terms = lax.all_to_all(terms, 'head', 0, 0, tiled=True)  9.11 us
    ppermute x3, waiting for transfers between devices, local(): lax.ppermute(shares[index], 'seq', [(s, source(s, index, owners)) for s i...  6.2 us
    all_to_all x1, starting transfers between devices, local(): queries = lax.all_to_all(queries, 'seq', 0, 0, tiled=True)  6.06 us
    all_to_all x1, starting transfers between devices, local(): totals = lax.all_to_all(totals, 'seq', 0, 0, tiled=True)  5.58 us
  transfers between devices with their start and end apart: 6, of which 4 were waited for; matrix products, arithmetic and copies ran while one was open for 0% of the time, Pallas kernels for 5%

profile of v5, /device:TPU:2, one launch (start us, length us, event | category | flops | bytes accessed | tf_op | source)
XLA Modules:
  0.0 83.5 jit_solution(3559274189306719898)
XLA Ops:
  0.0 3.4 %share.1 = (bf16[2,1024,128]{2,1,0:T(8,128)(2,1)}, bf16[2,1024,128]{2,1,0:T(8,128)(2,1)}, bf16[2,1024,128]{2,1,0:T(8,128)(2,1)}, bf16[2,1024,128]{2,1,0:T(8,128)...) custom-call(s32[1]{0:T(128)} %bitcast.place_ref, ...), custom_call_target="tpu_custom_call" | custom-call | tf_op jit(solution)/shard_map/share/pallas_call | solution.py:221
  3.4 0.0 copy-start
  3.4 9.2 %all-to-all-start = ((bf16[4,64,256]{2,1,0:T(8,128)(2,1)}), bf16[4,64,256]{2,1,0:T(8,128)(2,1)S(1)}, u32[]{:S(2)}, u32[]{:S(2)}) async-start(bf16[4,64,256]{2,1,0:T(8,128)(2,1)} %get-tuple-element.21), calls=%async_computation | async-start | bytes 262144 | tf_op jit(solution)/shard_map/all_to_all | solution.py:247
  12.7 1.9 %collective-permute-start = (bf16[2,1024,128]{2,1,0:T(8,128)(2,1)}, bf16[2,1024,128]{2,1,0:T(8,128)(2,1)S(1)}, u32[]{:S(2)}, u32[]{:S(2)}) collective-permute-start(bf16[2,1024,128]{2,1,0:T(8,128)(2,1)} %get-tuple-element.25), channel_id=1, source_target_pairs={{0,64},{16,80},{32,96},{48,112},{64,0},{80,16},{96,32},{112,48},{1... | collective-permute-start | bytes 1572872 | tf_op jit(solution)/shard_map/ppermute | solution.py:243
  14.6 7.1 %collective-permute-start.1 = (bf16[2,1024,128]{2,1,0:T(8,128)(2,1)}, bf16[2,1024,128]{2,1,0:T(8,128)(2,1)S(1)}, u32[]{:S(2)}, u32[]{:S(2)}) collective-permute-start(bf16[2,1024,128]{2,1,0:T(8,128)(2,1)} %get-tuple-element.26), channel_id=1, source_target_pairs={{0,448},{16,464},{32,480},{48,496},{64,128},{80,144},{96,160},{112... | collective-permute-start | bytes 1572872 | tf_op jit(solution)/shard_map/ppermute | solution.py:243
  21.7 3.5 %collective-permute-start.2 = (bf16[2,1024,128]{2,1,0:T(8,128)(2,1)}, bf16[2,1024,128]{2,1,0:T(8,128)(2,1)}, u32[]{:S(2)}, u32[]{:S(2)}) collective-permute-start(bf16[2,1024,128]{2,1,0:T(8,128)(2,1)} %get-tuple-element.27), channel_id=1, source_target_pairs={{0,16},{16,0},{32,48},{48,32},{64,80},{80,64},{96,112},{112,96},{1... | collective-permute-start | bytes 1572872 | tf_op jit(solution)/shard_map/ppermute | solution.py:243
  25.2 0.2 copy.8
  25.4 0.0 all-to-all-done.cand_ref
  25.4 1.2 %project.1 = (bf16[32,32,128]{2,1,0:T(8,128)(2,1)}, bf16[64,256]{1,0:T(8,128)(2,1)S(1)}) custom-call(bf16[64,64]{1,0:T(8,128)(2,1)S(1)} %get-tuple-element.20.place_ref, bf16[4,64,256]{2,1,0:T(8,128)(2,1)S(1)} %all-to-all-done.cand_ref, bf16[1024,512]{1,0:T(8,128)(2,1)S(1)} %bitcast.4), custom_call_target="tpu_custom_call" | custom-call | tf_op jit(solution)/shard_map/project/pallas_call | solution.py:248
  26.6 6.1 %all-to-all-start.1 = ((bf16[32,32,128]{2,1,0:T(8,128)(2,1)}), bf16[32,32,128]{2,1,0:T(8,128)(2,1)S(1)}, u32[]{:S(2)}, u32[]{:S(2)}) async-start(bf16[32,32,128]{2,1,0:T(8,128)(2,1)} %get-tuple-element.23), calls=%async_computation.1 | async-start | bytes 524288 | tf_op jit(solution)/shard_map/all_to_all | solution.py:263
  32.7 0.0 collective-permute-done.rest_1_
  32.7 0.0 copy-start.1
  32.7 0.3 collective-permute-done.1.rest_2_
  33.0 0.0 copy-start.2
  33.0 5.9 %collective-permute-done.2.rest_3_ = bf16[2,1024,128]{2,1,0:T(8,128)(2,1)} collective-permute-done((bf16[2,1024,128]{2,1,0:T(8,128)(2,1)}, bf16[2,1024,128]{2,1,0:T(8,128)(2,1)}, u32[]{:S(2)}, u32[]{:S(2)}) %collective-permute-start.2) | collective-permute-done | bytes 524320 | tf_op jit(solution)/shard_map/ppermute | solution.py:243
  38.9 0.0 copy-done.1
  38.9 0.0 copy-done.2
  38.9 0.0 copy-done
  38.9 3.2 %prepare.1 = (bf16[128,4096]{1,0:T(8,128)(2,1)S(1)}, bf16[2,4096,128]{2,1,0:T(8,128)(2,1)S(1)}) custom-call(s32[1]{0:T(128)} %bitcast.place_ref, s32[2]{0:T(128)S(1)} %copy-done, bf16[2,1024,128]{2,1,0:T(8,128)(2,1)} %get-tuple-element.24.rest_0_, bf16[2,1024,128]{2,1,0:T(8,128)(2,1)} %copy-done.1, bf16[2,1024,128]{2,1,0:T(8,128)(2,1)} %copy-done.2, ...), custom_call_target="tpu_custom_call" | custom-call | tf_op jit(solution)/shard_map/prepare/pallas_call | solution.py:264
  42.1 2.6 %all-to-all-done.1.query_ref = bf16[32,32,128]{2,1,0:T(8,128)(2,1)S(1)} async-done(((bf16[32,32,128]{2,1,0:T(8,128)(2,1)}), bf16[32,32,128]{2,1,0:T(8,128)(2,1)S(1)}, u32[]{:S(2)}, u32[]{:S(2)}) %all-to-all-start.1) | async-done | bytes 262176 | tf_op jit(solution)/shard_map/all_to_all | solution.py:263
  44.6 9.7 %attend.1 = bf16[32,32,128]{2,1,0:T(8,128)(2,1)} custom-call(bf16[32,32,128]{2,1,0:T(8,128)(2,1)S(1)} %all-to-all-done.1.query_ref, bf16[128,4096]{1,0:T(8,128)(2,1)S(1)} %get-tuple-element.28.keys, bf16[2,4096,128]{2,1,0:T(8,128)(2,1)S(1)} %get-tuple-element.29.masked), custom_call_target="tpu_custom_call" | custom-call | tf_op jit(solution)/shard_map/attend/pallas_call | solution.py:277
  54.4 5.6 %all-to-all-start.2 = ((bf16[32,32,128]{2,1,0:T(8,128)(2,1)}), bf16[32,32,128]{2,1,0:T(8,128)(2,1)S(1)}, u32[]{:S(2)}, u32[]{:S(2)}) async-start(bf16[32,32,128]{2,1,0:T(8,128)(2,1)} %attend.1), calls=%async_computation.2 | async-start | bytes 524288 | tf_op jit(solution)/shard_map/all_to_all | solution.py:285
  60.0 11.9 %all-to-all-done.2.partial_ref = bf16[32,32,128]{2,1,0:T(8,128)(2,1)S(1)} async-done(((bf16[32,32,128]{2,1,0:T(8,128)(2,1)}), bf16[32,32,128]{2,1,0:T(8,128)(2,1)S(1)}, u32[]{:S(2)}, u32[]{:S(2)}) %all-to-all-start.2) | async-done | bytes 262176 | tf_op jit(solution)/shard_map/all_to_all | solution.py:285
  71.9 1.8 %finish.1 = bf16[4,64,256]{2,1,0:T(8,128)(2,1)S(1)} custom-call(s32[2]{0:T(128)S(1)} %copy-done, bf16[64,64]{1,0:T(8,128)(2,1)S(1)} %get-tuple-element.19.back_ref, bf16[32,32,128]{2,1,0:T(8,128)(2,1)S(1)} %all-to-all-done.2.partial_ref, f32[64,256]{1,0:T(8,128)S(1)} %convert_element_type.3.gate_ref, bf16[256,1024]{1,0:T(8,128)(2,1)} %source_ref.1), custom_call_target="tpu_custom_call" | custom-call | tf_op jit(solution)/shard_map/finish/pallas_call | solution.py:286
  73.7 9.1 %all_to_all.20.term_ref = bf16[4,64,256]{2,1,0:T(8,128)(2,1)S(1)} all-to-all(bf16[4,64,256]{2,1,0:T(8,128)(2,1)S(1)} %finish.1), channel_id=1, replica_groups=mesh['seq'=32,'head'=4,'user'=4] {'head'}, dimensions={0} | all-to-all | bytes 262144 | tf_op jit(solution)/shard_map/all_to_all | solution.py:295
  82.8 0.6 add.1
  (1 shorter events, 0.0 us)
Async XLA Ops:
  3.4 35.5 %copy-start = (s32[2]{0:T(128)S(1)}, s32[2]{0:T(128)}, u32[]{:S(2)}) copy-start(s32[2]{0:T(128)} %length_ref.3) | copy-start | bytes 28
  3.4 22.0 %all-to-all-start = ((bf16[4,64,256]{2,1,0:T(8,128)(2,1)}), bf16[4,64,256]{2,1,0:T(8,128)(2,1)S(1)}, u32[]{:S(2)}, u32[]{:S(2)}) async-start(bf16[4,64,256]{2,1,0:T(8,128)(2,1)} %get-tuple-element.21), calls=%async_computation | async-start | bytes 262144 | tf_op jit(solution)/shard_map/all_to_all | solution.py:247
  12.7 20.0 %collective-permute-start = (bf16[2,1024,128]{2,1,0:T(8,128)(2,1)}, bf16[2,1024,128]{2,1,0:T(8,128)(2,1)S(1)}, u32[]{:S(2)}, u32[]{:S(2)}) collective-permute-start(bf16[2,1024,128]{2,1,0:T(8,128)(2,1)} %get-tuple-element.25), channel_id=1, source_target_pairs={{0,64},{16,80},{32,96},{48,112},{64,0},{80,16},{96,32},{112,48},{1... | collective-permute-start | bytes 1572872 | tf_op jit(solution)/shard_map/ppermute | solution.py:243
  14.6 18.4 %collective-permute-start.1 = (bf16[2,1024,128]{2,1,0:T(8,128)(2,1)}, bf16[2,1024,128]{2,1,0:T(8,128)(2,1)S(1)}, u32[]{:S(2)}, u32[]{:S(2)}) collective-permute-start(bf16[2,1024,128]{2,1,0:T(8,128)(2,1)} %get-tuple-element.26), channel_id=1, source_target_pairs={{0,448},{16,464},{32,480},{48,496},{64,128},{80,144},{96,160},{112... | collective-permute-start | bytes 1572872 | tf_op jit(solution)/shard_map/ppermute | solution.py:243
  21.7 17.2 %collective-permute-start.2 = (bf16[2,1024,128]{2,1,0:T(8,128)(2,1)}, bf16[2,1024,128]{2,1,0:T(8,128)(2,1)}, u32[]{:S(2)}, u32[]{:S(2)}) collective-permute-start(bf16[2,1024,128]{2,1,0:T(8,128)(2,1)} %get-tuple-element.27), channel_id=1, source_target_pairs={{0,16},{16,0},{32,48},{48,32},{64,80},{80,64},{96,112},{112,96},{1... | collective-permute-start | bytes 1572872 | tf_op jit(solution)/shard_map/ppermute | solution.py:243
  26.6 18.0 %all-to-all-start.1 = ((bf16[32,32,128]{2,1,0:T(8,128)(2,1)}), bf16[32,32,128]{2,1,0:T(8,128)(2,1)S(1)}, u32[]{:S(2)}, u32[]{:S(2)}) async-start(bf16[32,32,128]{2,1,0:T(8,128)(2,1)} %get-tuple-element.23), calls=%async_computation.1 | async-start | bytes 524288 | tf_op jit(solution)/shard_map/all_to_all | solution.py:263
  32.7 6.2 %copy-start.1 = (bf16[2,1024,128]{2,1,0:T(8,128)(2,1)}, bf16[2,1024,128]{2,1,0:T(8,128)(2,1)S(1)}, u32[]{:S(2)}) copy-start(bf16[2,1024,128]{2,1,0:T(8,128)(2,1)S(1)} %collective-permute-done.rest_1_) | copy-start | bytes 1572868
  33.0 5.9 %copy-start.2 = (bf16[2,1024,128]{2,1,0:T(8,128)(2,1)}, bf16[2,1024,128]{2,1,0:T(8,128)(2,1)S(1)}, u32[]{:S(2)}) copy-start(bf16[2,1024,128]{2,1,0:T(8,128)(2,1)S(1)} %collective-permute-done.1.rest_2_) | copy-start | bytes 1572868
  54.4 17.5 %all-to-all-start.2 = ((bf16[32,32,128]{2,1,0:T(8,128)(2,1)}), bf16[32,32,128]{2,1,0:T(8,128)(2,1)S(1)}, u32[]{:S(2)}, u32[]{:S(2)}) async-start(bf16[32,32,128]{2,1,0:T(8,128)(2,1)} %attend.1), calls=%async_computation.2 | async-start | bytes 524288 | tf_op jit(solution)/shard_map/all_to_all | solution.py:285

commit v6 on v5

--- a/solution.py
+++ b/solution.py
@@ -121,15 +121,19 @@
         copy.wait()
 
 
-def prepare_kernel(owners, place_ref, length_ref, *rest):
-    history_refs, (key_ref, value_ref) = rest[:SOURCES], rest[SOURCES:]
+def after_kernel(*refs):
+    pass
+
+
+def prepare_kernel(owners, first_source, place_ref, length_ref, *rest):
+    history_refs, (key_ref, value_ref) = rest[:-2], rest[-2:]
     _, span, width = history_refs[0].shape
     user, _ = role(place_ref[0])
     length = length_ref[user]
     position = lax.broadcasted_iota(jnp.int32, (span, width), 0)
     for index, history_ref in enumerate(history_refs):
         at = slice(index * span, (index + 1) * span)
-        live = length - source(place_ref[0], index, owners) * span
+        live = length - source(place_ref[0], first_source + index, owners) * span
         key_ref[:, at] = history_ref[0].T
         value = history_ref[1]
         for head in range(width // HEAD_DIM):
@@ -137,7 +141,8 @@
             value_ref[head, at, :] = jnp.where(keep, value, jnp.zeros_like(value))
 
 
-def attend_kernel(rows_now, positions_now, query_ref, keys, masked, out_ref):
+def attend_kernel(rows_now, positions_now, query_ref, keys, masked, *rest):
+    *begun_refs, out_ref = rest
     blocks, block_rows, width = query_ref.shape
     heads, positions, _ = masked.shape
     step_blocks = rows_now // block_rows
@@ -145,7 +150,10 @@
     def step(index, carry):
         here = pl.ds(index * step_blocks, step_blocks)
         query = query_ref[here].reshape(rows_now, width)
-        total = jnp.zeros((rows_now, width), jnp.float32)
+        if begun_refs:
+            total = begun_refs[0][here].reshape(rows_now, width)
+        else:
+            total = jnp.zeros((rows_now, width), jnp.float32)
         for start in range(0, positions, positions_now):
             at = slice(start, start + positions_now)
             for head in range(heads):
@@ -157,7 +165,7 @@
                 total += jnp.dot(
                     weight, masked[head, at, :], preferred_element_type=jnp.float32
                 )
-        out_ref[here] = total.astype(jnp.bfloat16).reshape(step_blocks, block_rows, width)
+        out_ref[here] = total.astype(out_ref.dtype).reshape(step_blocks, block_rows, width)
         return carry
 
     lax.fori_loop(0, blocks // step_blocks, step, 0)
@@ -239,11 +247,12 @@
         compiler_params=PARAMS,
         name="share",
     )(place, *map(in_hbm, (cand_user.reshape(1, rows), cand_rows, qu_weight, keys, values)))
-    history = shares[:1] + [
-        lax.ppermute(shares[index], "seq", [(s, source(s, index, owners)) for s in range(owners)])
-        for index in range(1, SOURCES)
-    ]
-
+    def from_source(index, share):
+        return lax.ppermute(
+            share, "seq", [(s, source(s, index, owners)) for s in range(owners)]
+        )
+
+    early = [shares[0], from_source(1, shares[1])]
     cand_parts = lax.all_to_all(copies, "head", 0, 0, tiled=True)
     queries, gates = pl.pallas_call(
         project_kernel,
@@ -260,28 +269,50 @@
         cand_parts,
         weight.reshape(qu_weight.shape[0], 2 * width),
     )
-    queries = lax.all_to_all(queries, "seq", 0, 0, tiled=True)
-    turned, masked = pl.pallas_call(
-        functools.partial(prepare_kernel, owners),
-        out_shape=(
-            jax.ShapeDtypeStruct((lanes, SOURCES * positions), jnp.bfloat16),
-            jax.ShapeDtypeStruct(
-                (lanes // HEAD_DIM, SOURCES * positions, lanes), jnp.bfloat16
+    sent = queries
+    queries = lax.all_to_all(sent, "seq", 0, 0, tiled=True)
+    held = pl.pallas_call(
+        after_kernel,
+        out_shape=[pltpu.HBM(share.shape, share.dtype) for share in shares[2:]],
+        in_specs=[HBM] * (SOURCES - 1),
+        out_specs=[HBM] * (SOURCES - 2),
+        input_output_aliases={0: 0, 1: 1},
+        compiler_params=PARAMS,
+        name="after",
+    )(*map(in_hbm, shares[2:]), in_hbm(sent))
+    late = [from_source(2 + index, share) for index, share in enumerate(held)]
+
+    def prepare(first_source, history):
+        count = len(history) * positions
+        return pl.pallas_call(
+            functools.partial(prepare_kernel, owners, first_source),
+            out_shape=(
+                jax.ShapeDtypeStruct((lanes, count), jnp.bfloat16),
+                jax.ShapeDtypeStruct((lanes // HEAD_DIM, count, lanes), jnp.bfloat16),
             ),
-        ),
-        in_specs=[SMEM] * 2 + [VMEM] * SOURCES,
-        out_specs=(VMEM, VMEM),
-        compiler_params=PARAMS,
-        name="prepare",
-    )(place, lengths, *map(in_hbm, history))
-    totals = pl.pallas_call(
-        functools.partial(attend_kernel, 1024, 256),
-        out_shape=jax.ShapeDtypeStruct((owners, block_rows, lanes), jnp.bfloat16),
-        in_specs=[VMEM] * 3,
-        out_specs=VMEM,
-        compiler_params=ATTEND_PARAMS,
-        name="attend",
-    )(queries, turned, masked)
+            in_specs=[SMEM] * 2 + [VMEM] * len(history),
+            out_specs=(VMEM, VMEM),
+            compiler_params=PARAMS,
+            name="prepare",
+        )(place, lengths, *map(in_hbm, history))
+
+    def attend(dtype, *operands):
+        return pl.pallas_call(
+            functools.partial(attend_kernel, 1024, 256),
+            out_shape=jax.ShapeDtypeStruct((owners, block_rows, lanes), dtype),
+            in_specs=[VMEM] * len(operands),
+            out_specs=VMEM,
+            compiler_params=ATTEND_PARAMS,
+            cost_estimate=pl.CostEstimate(
+                flops=8 * owners * block_rows * lanes * 2 * positions,
+                bytes_accessed=0,
+                transcendentals=0,
+            ),
+            name="attend",
+        )(*operands)
+
+    begun = attend(jnp.float32, queries, *prepare(0, early))
+    totals = attend(jnp.bfloat16, queries, *prepare(2, late), begun)
     totals = lax.all_to_all(totals, "seq", 0, 0, tiled=True)
     terms = pl.pallas_call(
         finish_kernel,

time: 84 us -> 86.9 us (1.035)
  the two profiles are of different devices: /device:TPU:2 before, /device:TPU:8 now
where the time goes in v6:
time: 86.9 us; the launch traced here: 86.3 us
  starting transfers between devices  36.7 us (42%)
  Pallas kernels  21.1 us (24%)
  waiting for transfers between devices  17.5 us (20%)
  blocking collectives  9.06 us (10%)
  local copies, waits for them, and re-layouts  1.84 us (2%)
    all_to_all x1, starting transfers between devices, local(): queries = lax.all_to_all(sent, 'seq', 0, 0, tiled=True)  14 us
    all_to_all x1, waiting for transfers between devices, local(): totals = lax.all_to_all(totals, 'seq', 0, 0, tiled=True)  11.4 us
    ppermute x3, starting transfers between devices, from_source(): lax.ppermute(share, 'seq', [(s, source(s, index, owners)) for s in range(...  11.4 us
    pallas_call x2, Pallas kernels, attend(): pl.pallas_call(functools.partial(attend_kernel, 1024, 256), out_shape=jax...  9.98 us
    all_to_all x1, blocking collectives, local(): terms = lax.all_to_all(terms, 'head', 0, 0, tiled=True)  9.06 us
    all_to_all x1, starting transfers between devices, local(): totals = lax.all_to_all(totals, 'seq', 0, 0, tiled=True)  7.02 us
    ppermute x3, waiting for transfers between devices, from_source(): lax.ppermute(share, 'seq', [(s, source(s, index, owners)) for s in range(...  4.6 us
    all_to_all x1, starting transfers between devices, local(): cand_parts = lax.all_to_all(copies, 'head', 0, 0, tiled=True)  4.3 us
  transfers between devices with their start and end apart: 6, of which 3 were waited for; matrix products, arithmetic and copies ran while one was open for 0% of the time, Pallas kernels for 9%

profile of v6, /device:TPU:8, one launch (start us, length us, event | category | flops | bytes accessed | tf_op | source)
XLA Modules:
  0.0 86.3 jit_solution(12586779976357710615)
XLA Ops:
  0.0 3.5 %share.1 = (bf16[2,1024,128]{2,1,0:T(8,128)(2,1)}, bf16[2,1024,128]{2,1,0:T(8,128)(2,1)}, bf16[2,1024,128]{2,1,0:T(8,128)(2,1)}, bf16[2,1024,128]{2,1,0:T(8,128)...) custom-call(s32[1]{0:T(128)} %bitcast.place_ref, ...), custom_call_target="tpu_custom_call" | custom-call | tf_op jit(solution)/shard_map/share/pallas_call | solution.py:229
  3.5 4.3 %all-to-all-start = ((bf16[4,64,256]{2,1,0:T(8,128)(2,1)}), bf16[4,64,256]{2,1,0:T(8,128)(2,1)S(1)}, u32[]{:S(2)}, u32[]{:S(2)}) async-start(bf16[4,64,256]{2,1,0:T(8,128)(2,1)} %get-tuple-element.25), calls=%async_computation | async-start | bytes 262144 | tf_op jit(solution)/shard_map/all_to_all | solution.py:256
  7.8 4.3 %collective-permute-start.2 = (bf16[2,1024,128]{2,1,0:T(8,128)(2,1)}, bf16[2,1024,128]{2,1,0:T(8,128)(2,1)S(1)}, u32[]{:S(2)}, u32[]{:S(2)}) collective-permute-start(bf16[2,1024,128]{2,1,0:T(8,128)(2,1)} %get-tuple-element.35), channel_id=1, source_target_pairs={{0,64},{16,80},{32,96},{48,112},{64,0},{80,16},{96,32},{112,48},{1... | collective-permute-start | bytes 1572872 | tf_op jit(solution)/shard_map/ppermute | solution.py:251
  12.0 0.2 copy.10
  12.3 1.5 %all-to-all-done.cand_ref = bf16[4,64,256]{2,1,0:T(8,128)(2,1)S(1)} async-done(((bf16[4,64,256]{2,1,0:T(8,128)(2,1)}), bf16[4,64,256]{2,1,0:T(8,128)(2,1)S(1)}, u32[]{:S(2)}, u32[]{:S(2)}) %all-to-all-start) | async-done | bytes 131104 | tf_op jit(solution)/shard_map/all_to_all | solution.py:256
  13.8 1.2 %project.1 = (bf16[32,32,128]{2,1,0:T(8,128)(2,1)}, bf16[64,256]{1,0:T(8,128)(2,1)S(1)}) custom-call(bf16[64,64]{1,0:T(8,128)(2,1)S(1)} %get-tuple-element.24.place_ref, bf16[4,64,256]{2,1,0:T(8,128)(2,1)S(1)} %all-to-all-done.cand_ref, bf16[1024,512]{1,0:T(8,128)(2,1)S(1)} %bitcast.4), custom_call_target="tpu_custom_call" | custom-call | tf_op jit(solution)/shard_map/project/pallas_call | solution.py:257
  15.0 14.0 %all-to-all-start.1 = ((bf16[32,32,128]{2,1,0:T(8,128)(2,1)}), bf16[32,32,128]{2,1,0:T(8,128)(2,1)S(1)}, u32[]{:S(2)}, u32[]{:S(2)}) async-start(bf16[32,32,128]{2,1,0:T(8,128)(2,1)} %get-tuple-element.27.refs_2_), calls=%async_computation.1 | async-start | bytes 524288 | tf_op jit(solution)/shard_map/all_to_all | solution.py:273
  28.9 4.7 %collective-permute-start = (bf16[2,1024,128]{2,1,0:T(8,128)(2,1)}, bf16[2,1024,128]{2,1,0:T(8,128)(2,1)S(1)}, u32[]{:S(2)}, u32[]{:S(2)}) collective-permute-start(bf16[2,1024,128]{2,1,0:T(8,128)(2,1)} %get-tuple-element.30), channel_id=1, source_target_pairs={{0,448},{16,464},{32,480},{48,496},{64,128},{80,144},{96,160},{112... | collective-permute-start | bytes 1572872 | tf_op jit(solution)/shard_map/ppermute | solution.py:251
  33.6 0.0 copy-start
  33.6 2.5 %collective-permute-start.1 = (bf16[2,1024,128]{2,1,0:T(8,128)(2,1)}, bf16[2,1024,128]{2,1,0:T(8,128)(2,1)}, u32[]{:S(2)}, u32[]{:S(2)}) collective-permute-start(bf16[2,1024,128]{2,1,0:T(8,128)(2,1)} %get-tuple-element.31), channel_id=1, source_target_pairs={{0,16},{16,0},{32,48},{48,32},{64,80},{80,64},{96,112},{112,96},{1... | collective-permute-start | bytes 1572872 | tf_op jit(solution)/shard_map/ppermute | solution.py:251
  36.1 0.0 collective-permute-done.2.rest_1_
  36.1 0.0 copy-start.1
  36.1 0.8 copy-done.1
  36.9 0.0 copy-done
  36.9 2.0 %prepare.3 = (bf16[128,2048]{1,0:T(8,128)(2,1)S(1)}, bf16[2,2048,128]{2,1,0:T(8,128)(2,1)S(1)}) custom-call(s32[1]{0:T(128)} %bitcast.place_ref, s32[2]{0:T(128)S(1)} %copy-done, bf16[2,1024,128]{2,1,0:T(8,128)(2,1)} %get-tuple-element.34.rest_0_, bf16[2,1024,128]{2,1,0:T(8,128)(2,1)} %copy-done.1), custom_call_target="tpu_custom_call" | custom-call | tf_op jit(solution)/shard_map/prepare/pallas_call | solution.py:287
  38.9 0.0 all-to-all-done.1.query_ref
  38.9 4.7 %attend.2.rest_0_ = f32[32,32,128]{2,1,0:T(8,128)S(1)} custom-call(bf16[32,32,128]{2,1,0:T(8,128)(2,1)S(1)} %all-to-all-done.1.query_ref, bf16[128,2048]{1,0:T(8,128)(2,1)S(1)} %get-tuple-element.36.keys, bf16[2,2048,128]{2,1,0:T(8,128)(2,1)S(1)} %get-tuple-element.37.masked), custom_call_target="tpu_custom_call" | custom-call | flops 2147483648 | tf_op jit(solution)/shard_map/attend/pallas_call | solution.py:300
  43.6 4.6 %collective-permute-done.rest_0_ = bf16[2,1024,128]{2,1,0:T(8,128)(2,1)S(1)} collective-permute-done((bf16[2,1024,128]{2,1,0:T(8,128)(2,1)}, bf16[2,1024,128]{2,1,0:T(8,128)(2,1)S(1)}, u32[]{:S(2)}, u32[]{:S(2)}) %collective-permute-start) | collective-permute-done | bytes 524320 | tf_op jit(solution)/shard_map/ppermute | solution.py:251
  48.2 0.0 copy-start.2
  48.2 0.0 collective-permute-done.1.rest_1_
  48.2 0.8 copy-done.2
  49.0 2.0 %prepare.2 = (bf16[128,2048]{1,0:T(8,128)(2,1)S(1)}, bf16[2,2048,128]{2,1,0:T(8,128)(2,1)S(1)}) custom-call(s32[1]{0:T(128)} %bitcast.place_ref, s32[2]{0:T(128)S(1)} %copy-done, bf16[2,1024,128]{2,1,0:T(8,128)(2,1)} %copy-done.2, bf16[2,1024,128]{2,1,0:T(8,128)(2,1)} %collective-permute-done.1.rest_1_), custom_call_target="tpu_custom_call" | custom-call | tf_op jit(solution)/shard_map/prepare/pallas_call | solution.py:287
  51.0 5.3 %attend.3 = bf16[32,32,128]{2,1,0:T(8,128)(2,1)} custom-call(bf16[32,32,128]{2,1,0:T(8,128)(2,1)S(1)} %all-to-all-done.1.query_ref, bf16[128,2048]{1,0:T(8,128)(2,1)S(1)} %get-tuple-element.32.keys, bf16[2,2048,128]{2,1,0:T(8,128)(2,1)S(1)} %get-tuple-element.33.masked, f32[32,32,128]{2,1,0:T(8,128)S(1)} %attend.2.rest_0_), custom_call_target="tpu_custom_call" | custom-call | flops 2147483648 | tf_op jit(solution)/shard_map/attend/pallas_call | solution.py:300
  56.4 7.0 %all-to-all-start.2 = ((bf16[32,32,128]{2,1,0:T(8,128)(2,1)}), bf16[32,32,128]{2,1,0:T(8,128)(2,1)S(1)}, u32[]{:S(2)}, u32[]{:S(2)}) async-start(bf16[32,32,128]{2,1,0:T(8,128)(2,1)} %attend.3), calls=%async_computation.2 | async-start | bytes 524288 | tf_op jit(solution)/shard_map/all_to_all | solution.py:316
  63.4 11.4 %all-to-all-done.2.partial_ref = bf16[32,32,128]{2,1,0:T(8,128)(2,1)S(1)} async-done(((bf16[32,32,128]{2,1,0:T(8,128)(2,1)}), bf16[32,32,128]{2,1,0:T(8,128)(2,1)S(1)}, u32[]{:S(2)}, u32[]{:S(2)}) %all-to-all-start.2) | async-done | bytes 262176 | tf_op jit(solution)/shard_map/all_to_all | solution.py:316
  74.8 1.8 %finish.1 = bf16[4,64,256]{2,1,0:T(8,128)(2,1)S(1)} custom-call(s32[2]{0:T(128)S(1)} %copy-done, bf16[64,64]{1,0:T(8,128)(2,1)S(1)} %get-tuple-element.23.back_ref, bf16[32,32,128]{2,1,0:T(8,128)(2,1)S(1)} %all-to-all-done.2.partial_ref, f32[64,256]{1,0:T(8,128)S(1)} %convert_element_type.3.gate_ref, bf16[256,1024]{1,0:T(8,128)(2,1)} %source_ref.1), custom_call_target="tpu_custom_call" | custom-call | tf_op jit(solution)/shard_map/finish/pallas_call | solution.py:317
  76.6 9.1 %all_to_all.20.term_ref = bf16[4,64,256]{2,1,0:T(8,128)(2,1)S(1)} all-to-all(bf16[4,64,256]{2,1,0:T(8,128)(2,1)S(1)} %finish.1), channel_id=1, replica_groups=mesh['seq'=32,'head'=4,'user'=4] {'head'}, dimensions={0} | all-to-all | bytes 262144 | tf_op jit(solution)/shard_map/all_to_all | solution.py:326
  85.7 0.6 add.1
  (2 shorter events, 0.0 us)
Async XLA Ops:
  3.5 10.3 %all-to-all-start = ((bf16[4,64,256]{2,1,0:T(8,128)(2,1)}), bf16[4,64,256]{2,1,0:T(8,128)(2,1)S(1)}, u32[]{:S(2)}, u32[]{:S(2)}) async-start(bf16[4,64,256]{2,1,0:T(8,128)(2,1)} %get-tuple-element.25), calls=%async_computation | async-start | bytes 262144 | tf_op jit(solution)/shard_map/all_to_all | solution.py:256
  7.8 28.3 %collective-permute-start.2 = (bf16[2,1024,128]{2,1,0:T(8,128)(2,1)}, bf16[2,1024,128]{2,1,0:T(8,128)(2,1)S(1)}, u32[]{:S(2)}, u32[]{:S(2)}) collective-permute-start(bf16[2,1024,128]{2,1,0:T(8,128)(2,1)} %get-tuple-element.35), channel_id=1, source_target_pairs={{0,64},{16,80},{32,96},{48,112},{64,0},{80,16},{96,32},{112,48},{1... | collective-permute-start | bytes 1572872 | tf_op jit(solution)/shard_map/ppermute | solution.py:251
  15.0 24.0 %all-to-all-start.1 = ((bf16[32,32,128]{2,1,0:T(8,128)(2,1)}), bf16[32,32,128]{2,1,0:T(8,128)(2,1)S(1)}, u32[]{:S(2)}, u32[]{:S(2)}) async-start(bf16[32,32,128]{2,1,0:T(8,128)(2,1)} %get-tuple-element.27.refs_2_), calls=%async_computation.1 | async-start | bytes 524288 | tf_op jit(solution)/shard_map/all_to_all | solution.py:273
  28.9 19.2 %collective-permute-start = (bf16[2,1024,128]{2,1,0:T(8,128)(2,1)}, bf16[2,1024,128]{2,1,0:T(8,128)(2,1)S(1)}, u32[]{:S(2)}, u32[]{:S(2)}) collective-permute-start(bf16[2,1024,128]{2,1,0:T(8,128)(2,1)} %get-tuple-element.30), channel_id=1, source_target_pairs={{0,448},{16,464},{32,480},{48,496},{64,128},{80,144},{96,160},{112... | collective-permute-start | bytes 1572872 | tf_op jit(solution)/shard_map/ppermute | solution.py:251
  33.6 3.3 %copy-start = (s32[2]{0:T(128)S(1)}, s32[2]{0:T(128)}, u32[]{:S(2)}) copy-start(s32[2]{0:T(128)} %length_ref.5) | copy-start | bytes 28
  33.6 14.6 %collective-permute-start.1 = (bf16[2,1024,128]{2,1,0:T(8,128)(2,1)}, bf16[2,1024,128]{2,1,0:T(8,128)(2,1)}, u32[]{:S(2)}, u32[]{:S(2)}) collective-permute-start(bf16[2,1024,128]{2,1,0:T(8,128)(2,1)} %get-tuple-element.31), channel_id=1, source_target_pairs={{0,16},{16,0},{32,48},{48,32},{64,80},{80,64},{96,112},{112,96},{1... | collective-permute-start | bytes 1572872 | tf_op jit(solution)/shard_map/ppermute | solution.py:251
  36.1 0.8 copy-start.1
  48.2 0.8 copy-start.2
  56.4 18.5 %all-to-all-start.2 = ((bf16[32,32,128]{2,1,0:T(8,128)(2,1)}), bf16[32,32,128]{2,1,0:T(8,128)(2,1)S(1)}, u32[]{:S(2)}, u32[]{:S(2)}) async-start(bf16[32,32,128]{2,1,0:T(8,128)(2,1)} %attend.3), calls=%async_computation.2 | async-start | bytes 524288 | tf_op jit(solution)/shard_map/all_to_all | solution.py:316

commit v7 on v5

--- a/solution.py
+++ b/solution.py
@@ -13,7 +13,7 @@
 SMEM = pl.BlockSpec(memory_space=pltpu.SMEM)
 HBM = pl.BlockSpec(memory_space=pltpu.HBM)
 PARAMS = pltpu.CompilerParams(vmem_limit_bytes=16 * 2**20)
-ATTEND_PARAMS = pltpu.CompilerParams(vmem_limit_bytes=32 * 2**20)
+ATTEND_PARAMS = pltpu.CompilerParams(vmem_limit_bytes=24 * 2**20)
 
 
 SOURCES = 4
@@ -51,7 +51,7 @@
     return order.astype(jnp.bfloat16), order.T.astype(jnp.bfloat16)
 
 
-def project_kernel(place_ref, cand_ref, weight_ref, query_ref, gate_ref):
+def project_kernel(cand_ref, weight_ref, query_ref, gate_ref):
     slices, rows, depth = cand_ref.shape
     width = weight_ref.shape[1] // 2
     total = jnp.zeros((rows, 2 * width), jnp.float32)
@@ -61,38 +61,42 @@
             weight_ref[part * depth : (part + 1) * depth, :],
             preferred_element_type=jnp.float32,
         )
-    projected = total / (1.0 + jnp.exp(-total))
-    ordered = jnp.dot(
-        place_ref[...], projected.astype(jnp.bfloat16), preferred_element_type=jnp.float32
-    )
-    query = (ordered[:, :width] * (0.5 * HEAD_DIM**-0.5)).astype(jnp.bfloat16)
+    projected = (total / (1.0 + jnp.exp(-total))).astype(jnp.bfloat16)
+    query = (projected[:, :width].astype(jnp.float32) * (0.5 * HEAD_DIM**-0.5)).astype(
+        jnp.bfloat16
+    )
     _, block_rows, lanes = query_ref.shape
     for owner in range(query_ref.shape[0]):
         user, half = role(owner)
         query_ref[owner] = query[
             user * block_rows : (user + 1) * block_rows, half * lanes : (half + 1) * lanes
         ]
-    gate_ref[...] = ordered[:, width:].astype(jnp.bfloat16)
+    gate_ref[...] = projected[:, width:]
+
+
+def part_of(history_ref, user, half, lanes):
+    return history_ref.at[user, :, pl.ds(pl.multiple_of(half * lanes, lanes), lanes)]
 
 
 def share_kernel(
     owners, place_ref, user_ref, cand_ref, weight_ref, key_ref, value_ref, *rest
 ):
-    out_refs, rest = rest[:SOURCES], rest[SOURCES:]
-    copy_ref, keep_ref, order_ref, back_ref, held_ref, users, parts, sems, own_sems = rest
+    out_refs, rest = rest[: SOURCES - 1], rest[SOURCES - 1 :]
+    copy_ref, keep_ref, held_ref, users, rows, parts, sems, copy_sems, own_sems = rest
     lanes = out_refs[0].shape[2]
     first = [
         pltpu.make_async_copy(cand_ref, keep_ref, own_sems.at[0]),
         pltpu.make_async_copy(user_ref, users, own_sems.at[1]),
     ]
     into = []
-    for index in range(SOURCES):
-        user, half = role(source(place_ref[0], index, owners))
-        here = pl.ds(pl.multiple_of(half * lanes, lanes), lanes)
+    for index in range(SOURCES - 1):
+        user, half = role(source(place_ref[0], index + 1, owners))
         for kind, history_ref in enumerate((key_ref, value_ref)):
             into.append(
                 pltpu.make_async_copy(
-                    history_ref.at[user, :, here], parts.at[index, kind], sems.at[index, kind]
+                    part_of(history_ref, user, half, lanes),
+                    parts.at[index, kind],
+                    sems.at[index, kind],
                 )
             )
     last = pltpu.make_async_copy(weight_ref, held_ref, own_sems.at[2])
@@ -100,13 +104,14 @@
         copy.start()
     for copy in first:
         copy.wait()
-    cand = keep_ref[...]
+    order, _ = orders_of(users[...], rows.shape[0])
+    rows[...] = jnp.dot(order, keep_ref[...], preferred_element_type=jnp.float32).astype(
+        rows.dtype
+    )
+    out = []
     for group in range(copy_ref.shape[0]):
-        copy_ref[group] = cand
-    order, back = orders_of(users[...], cand.shape[0])
-    order_ref[...] = order
-    back_ref[...] = back
-    out = []
+        out.append(pltpu.make_async_copy(rows, copy_ref.at[group], copy_sems.at[group]))
+        out[-1].start()
     for index, out_ref in enumerate(out_refs):
         for kind in range(2):
             into[2 * index + kind].wait()
@@ -121,20 +126,35 @@
         copy.wait()
 
 
-def prepare_kernel(owners, place_ref, length_ref, *rest):
-    history_refs, (key_ref, value_ref) = rest[:SOURCES], rest[SOURCES:]
-    _, span, width = history_refs[0].shape
-    user, _ = role(place_ref[0])
+def prepare_kernel(
+    owners, place_ref, length_ref, user_ref, key_ref, value_ref, *rest
+):
+    history_refs, rest = rest[: SOURCES - 1], rest[SOURCES - 1 :]
+    turned_ref, masked_ref, back_ref, own, sems = rest
+    _, span, width = own.shape
+    user, half = role(place_ref[0])
+    copies = [
+        pltpu.make_async_copy(part_of(history_ref, user, half, width), own.at[kind], sems.at[kind])
+        for kind, history_ref in enumerate((key_ref, value_ref))
+    ]
+    for copy in copies:
+        copy.start()
+    _, back = orders_of(user_ref[...], back_ref.shape[0])
+    back_ref[...] = back
     length = length_ref[user]
     position = lax.broadcasted_iota(jnp.int32, (span, width), 0)
-    for index, history_ref in enumerate(history_refs):
+    for index in reversed(range(SOURCES)):
+        if index == 0:
+            for copy in copies:
+                copy.wait()
+        history_ref = history_refs[index - 1] if index else own
         at = slice(index * span, (index + 1) * span)
         live = length - source(place_ref[0], index, owners) * span
-        key_ref[:, at] = history_ref[0].T
+        turned_ref[:, at] = history_ref[0].T
         value = history_ref[1]
         for head in range(width // HEAD_DIM):
             keep = (position < live) & head_mask((span, width), head)
-            value_ref[head, at, :] = jnp.where(keep, value, jnp.zeros_like(value))
+            masked_ref[head, at, :] = jnp.where(keep, value, jnp.zeros_like(value))
 
 
 def attend_kernel(rows_now, positions_now, query_ref, keys, masked, out_ref):
@@ -163,12 +183,8 @@
     lax.fori_loop(0, blocks // step_blocks, step, 0)
 
 
-def finish_kernel(
-    length_ref, back_ref, partial_ref, gate_ref, source_ref, out_ref, weight_ref, sem
-):
+def finish_kernel(length_ref, back_ref, partial_ref, gate_ref, weight_ref, out_ref):
     rows, width = gate_ref.shape
-    fetch = pltpu.make_async_copy(source_ref, weight_ref, sem)
-    fetch.start()
     sums = {}
     for block in range(partial_ref.shape[0]):
         term = partial_ref[block].astype(jnp.float32)
@@ -189,11 +205,10 @@
     normed = attn * lax.rsqrt(mean + 1e-06)
     gated = (normed * gate_ref[...]).astype(jnp.bfloat16)
     gated = jnp.dot(back_ref[...], gated, preferred_element_type=jnp.float32).astype(jnp.bfloat16)
-    fetch.wait()
     for part in range(out_ref.shape[0]):
         out_ref[part] = jnp.dot(
             gated,
-            weight_ref[:, part * width : (part + 1) * width],
+            weight_ref[part],
             preferred_element_type=jnp.float32,
         ).astype(out_ref.dtype)
 
@@ -218,30 +233,31 @@
     place = jnp.reshape(lax.axis_index("seq"), (1,)).astype(jnp.int32)
     block_rows, lanes = rows // USERS, width // 2
 
-    *shares, copies, kept, order, back, weight = pl.pallas_call(
+    users = cand_user.reshape(1, rows)
+    *shares, copies, kept, weight = pl.pallas_call(
         functools.partial(share_kernel, owners),
-        out_shape=[pltpu.HBM((2, positions, lanes), jnp.bfloat16)] * SOURCES
+        out_shape=[pltpu.HBM((2, positions, lanes), jnp.bfloat16)] * (SOURCES - 1)
         + [
-            jax.ShapeDtypeStruct((groups, rows, depth), jnp.bfloat16),
+            pltpu.HBM((groups, rows, depth), jnp.bfloat16),
             pltpu.VMEM((rows, depth), jnp.bfloat16),
-            pltpu.VMEM((rows, rows), jnp.bfloat16),
-            pltpu.VMEM((rows, rows), jnp.bfloat16),
             pltpu.VMEM(qu_weight.shape, jnp.bfloat16),
         ],
         in_specs=[SMEM] + [HBM] * 5,
-        out_specs=[HBM] * SOURCES + [VMEM] * 5,
+        out_specs=[HBM] * SOURCES + [VMEM] * 2,
         scratch_shapes=[
             pltpu.VMEM((1, rows), jnp.int32),
-            pltpu.VMEM((SOURCES, 2, positions, lanes), jnp.bfloat16),
-            pltpu.SemaphoreType.DMA((SOURCES, 2)),
+            pltpu.VMEM((rows, depth), jnp.bfloat16),
+            pltpu.VMEM((SOURCES - 1, 2, positions, lanes), jnp.bfloat16),
+            pltpu.SemaphoreType.DMA((SOURCES - 1, 2)),
+            pltpu.SemaphoreType.DMA((groups,)),
             pltpu.SemaphoreType.DMA((3,)),
         ],
         compiler_params=PARAMS,
         name="share",
-    )(place, *map(in_hbm, (cand_user.reshape(1, rows), cand_rows, qu_weight, keys, values)))
-    history = shares[:1] + [
-        lax.ppermute(shares[index], "seq", [(s, source(s, index, owners)) for s in range(owners)])
-        for index in range(1, SOURCES)
+    )(place, *map(in_hbm, (users, cand_rows, qu_weight, keys, values)))
+    history = [
+        lax.ppermute(share, "seq", [(s, source(s, index + 1, owners)) for s in range(owners)])
+        for index, share in enumerate(shares)
     ]
 
     cand_parts = lax.all_to_all(copies, "head", 0, 0, tiled=True)
@@ -251,29 +267,33 @@
             jax.ShapeDtypeStruct((owners, block_rows, lanes), jnp.bfloat16),
             jax.ShapeDtypeStruct((rows, width), jnp.bfloat16),
         ),
-        in_specs=[VMEM] * 3,
+        in_specs=[VMEM] * 2,
         out_specs=(VMEM, VMEM),
         compiler_params=PARAMS,
         name="project",
     )(
-        order,
         cand_parts,
         weight.reshape(qu_weight.shape[0], 2 * width),
     )
     queries = lax.all_to_all(queries, "seq", 0, 0, tiled=True)
-    turned, masked = pl.pallas_call(
+    turned, masked, back = pl.pallas_call(
         functools.partial(prepare_kernel, owners),
         out_shape=(
             jax.ShapeDtypeStruct((lanes, SOURCES * positions), jnp.bfloat16),
             jax.ShapeDtypeStruct(
                 (lanes // HEAD_DIM, SOURCES * positions, lanes), jnp.bfloat16
             ),
+            pltpu.VMEM((rows, rows), jnp.bfloat16),
         ),
-        in_specs=[SMEM] * 2 + [VMEM] * SOURCES,
-        out_specs=(VMEM, VMEM),
+        in_specs=[SMEM] * 2 + [VMEM] + [HBM] * 2 + [VMEM] * (SOURCES - 1),
+        out_specs=(VMEM,) * 3,
+        scratch_shapes=[
+            pltpu.VMEM((2, positions, lanes), jnp.bfloat16),
+            pltpu.SemaphoreType.DMA((2,)),
+        ],
         compiler_params=PARAMS,
         name="prepare",
-    )(place, lengths, *map(in_hbm, history))
+    )(place, lengths, *map(in_hbm, (users, keys, values, *history)))
     totals = pl.pallas_call(
         functools.partial(attend_kernel, 1024, 256),
         out_shape=jax.ShapeDtypeStruct((owners, block_rows, lanes), jnp.bfloat16),
@@ -283,15 +303,15 @@
         name="attend",
     )(queries, turned, masked)
     totals = lax.all_to_all(totals, "seq", 0, 0, tiled=True)
+    blocks = jnp.transpose(out_weight.reshape(width, groups, depth), (1, 0, 2))
     terms = pl.pallas_call(
         finish_kernel,
         out_shape=jax.ShapeDtypeStruct((groups, rows, depth), jnp.bfloat16),
-        in_specs=[SMEM] + [VMEM] * 3 + [HBM],
+        in_specs=[SMEM] + [VMEM] * 4,
         out_specs=VMEM,
-        scratch_shapes=[pltpu.VMEM(out_weight.shape, jnp.bfloat16), pltpu.SemaphoreType.DMA],
         compiler_params=PARAMS,
         name="finish",
-    )(lengths, back, totals, gates.astype(jnp.float32), in_hbm(out_weight))
+    )(lengths, back, totals, gates.astype(jnp.float32), blocks)
     terms = lax.all_to_all(terms, "head", 0, 0, tiled=True)
     return pl.pallas_call(
         add_kernel,

time: 84 us -> 82.3 us (0.980)
  local copies, waits for them, and re-layouts: 0.24 us -> 2.92 us
  waiting for transfers between devices: 20.7 us -> 18.1 us
  Pallas kernels: 19.9 us -> 18 us
    unnamed x7 -> x8, local copies, waits for them, and re-layouts: 0.24 us -> 2.72 us
    all_to_all x1, waiting for transfers between devices: 11.9 us -> 10.5 us  [local(): totals = lax.all_to_all(totals, 'seq', 0, 0, tiled=True)]
    ppermute x3, waiting for transfers between devices: 6.2 us -> 5.1 us  [local(): lax.ppermute(share, 'seq', [(s, source(s, index + 1, owners)) for s in ra...]
    pallas_call x1, Pallas kernels: 3.43 us -> 2.51 us  [local(): pl.pallas_call(functools.partial(share_kernel, owners), out_shape=[pltpu....]
  transfers between devices with their start and end apart: 6 -> 6, of which waited for: 4 -> 4; matrix products, arithmetic and copies ran while one was open for 0% -> 2% of each run, Pallas kernels for 5% -> 5%
where the time goes in v7:
time: 82.3 us; the launch traced here: 81.7 us
  starting transfers between devices  33.5 us (41%)
  waiting for transfers between devices  18.1 us (22%)
  Pallas kernels  18 us (22%)
  blocking collectives  9.12 us (11%)
  local copies, waits for them, and re-layouts  2.92 us (4%)
    ppermute x3, starting transfers between devices, local(): lax.ppermute(share, 'seq', [(s, source(s, index + 1, owners)) for s in ra...  12.5 us
    all_to_all x1, waiting for transfers between devices, local(): totals = lax.all_to_all(totals, 'seq', 0, 0, tiled=True)  10.5 us
    pallas_call x1, Pallas kernels, local(): pl.pallas_call(functools.partial(attend_kernel, 1024, 256), out_shape=jax...  9.74 us
    all_to_all x1, starting transfers between devices, local(): cand_parts = lax.all_to_all(copies, 'head', 0, 0, tiled=True)  9.21 us
    all_to_all x1, blocking collectives, local(): terms = lax.all_to_all(terms, 'head', 0, 0, tiled=True)  9.12 us
    all_to_all x1, starting transfers between devices, local(): queries = lax.all_to_all(queries, 'seq', 0, 0, tiled=True)  6.06 us
    all_to_all x1, starting transfers between devices, local(): totals = lax.all_to_all(totals, 'seq', 0, 0, tiled=True)  5.68 us
    ppermute x3, waiting for transfers between devices, local(): lax.ppermute(share, 'seq', [(s, source(s, index + 1, owners)) for s in ra...  5.1 us
  transfers between devices with their start and end apart: 6, of which 4 were waited for; matrix products, arithmetic and copies ran while one was open for 2% of the time, Pallas kernels for 5%

profile of v7, /device:TPU:2, one launch (start us, length us, event | category | flops | bytes accessed | tf_op | source)
XLA Modules:
  0.0 81.7 jit_solution(6650500088494095076)
XLA Ops:
  0.0 2.5 %share.1 = (bf16[2,1024,128]{2,1,0:T(8,128)(2,1)}, bf16[2,1024,128]{2,1,0:T(8,128)(2,1)}, bf16[2,1024,128]{2,1,0:T(8,128)(2,1)}, bf16[4,64,256]{2,1,0:T(8,128)(2...) custom-call(s32[1]{0:T(128)} %bitcast.place_ref, s32[1,64]{1,0:T(1,128)} %bitcast.10, ...), custom_call_target="tpu_custom_call" | custom-call | tf_op jit(solution)/shard_map/share/pallas_call | solution.py:237
  2.5 0.0 copy-start
  2.5 9.2 %all-to-all-start = ((bf16[4,64,256]{2,1,0:T(8,128)(2,1)}), bf16[4,64,256]{2,1,0:T(8,128)(2,1)S(1)}, u32[]{:S(2)}, u32[]{:S(2)}) async-start(bf16[4,64,256]{2,1,0:T(8,128)(2,1)} %get-tuple-element.21), calls=%async_computation | async-start | bytes 262144 | tf_op jit(solution)/shard_map/all_to_all | solution.py:263
  11.7 1.9 %collective-permute-start = (bf16[2,1024,128]{2,1,0:T(8,128)(2,1)}, bf16[2,1024,128]{2,1,0:T(8,128)(2,1)S(1)}, u32[]{:S(2)}, u32[]{:S(2)}) collective-permute-start(bf16[2,1024,128]{2,1,0:T(8,128)(2,1)} %get-tuple-element.17), channel_id=1, source_target_pairs={{0,64},{16,80},{32,96},{48,112},{64,0},{80,16},{96,32},{112,48},{1... | collective-permute-start | bytes 1572872 | tf_op jit(solution)/shard_map/ppermute | solution.py:259
  13.7 7.1 %collective-permute-start.1 = (bf16[2,1024,128]{2,1,0:T(8,128)(2,1)}, bf16[2,1024,128]{2,1,0:T(8,128)(2,1)S(1)}, u32[]{:S(2)}, u32[]{:S(2)}) collective-permute-start(bf16[2,1024,128]{2,1,0:T(8,128)(2,1)} %get-tuple-element.18), channel_id=1, source_target_pairs={{0,448},{16,464},{32,480},{48,496},{64,128},{80,144},{96,160},{112... | collective-permute-start | bytes 1572872 | tf_op jit(solution)/shard_map/ppermute | solution.py:259
  20.8 3.5 %collective-permute-start.2 = (bf16[2,1024,128]{2,1,0:T(8,128)(2,1)}, bf16[2,1024,128]{2,1,0:T(8,128)(2,1)}, u32[]{:S(2)}, u32[]{:S(2)}) collective-permute-start(bf16[2,1024,128]{2,1,0:T(8,128)(2,1)} %get-tuple-element.19), channel_id=1, source_target_pairs={{0,16},{16,0},{32,48},{48,32},{64,80},{80,64},{96,112},{112,96},{1... | collective-permute-start | bytes 1572872 | tf_op jit(solution)/shard_map/ppermute | solution.py:259
  24.3 0.2 copy.10
  24.5 0.0 all-to-all-done.cand_ref
  24.5 1.0 %project.1 = (bf16[32,32,128]{2,1,0:T(8,128)(2,1)}, bf16[64,256]{1,0:T(8,128)(2,1)S(1)}) custom-call(bf16[4,64,256]{2,1,0:T(8,128)(2,1)S(1)} %all-to-all-done.cand_ref, bf16[1024,512]{1,0:T(8,128)(2,1)S(1)} %bitcast.6), custom_call_target="tpu_custom_call" | custom-call | tf_op jit(solution)/shard_map/project/pallas_call | solution.py:264
  25.6 6.1 %all-to-all-start.1 = ((bf16[32,32,128]{2,1,0:T(8,128)(2,1)}), bf16[32,32,128]{2,1,0:T(8,128)(2,1)S(1)}, u32[]{:S(2)}, u32[]{:S(2)}) async-start(bf16[32,32,128]{2,1,0:T(8,128)(2,1)} %get-tuple-element.23), calls=%async_computation.1 | async-start | bytes 524288 | tf_op jit(solution)/shard_map/all_to_all | solution.py:278
  31.6 0.0 collective-permute-done.rest_0_
  31.7 0.0 copy-start.1
  31.7 0.4 collective-permute-done.1.rest_1_
  32.1 0.4 copy-done.1
  32.5 0.0 copy-start.2
  32.5 0.8 %copy-done.2 = bf16[2,1024,128]{2,1,0:T(8,128)(2,1)} copy-done((bf16[2,1024,128]{2,1,0:T(8,128)(2,1)}, bf16[2,1024,128]{2,1,0:T(8,128)(2,1)S(1)}, u32[]{:S(2)}) %copy-start.2) | copy-done | bytes 524312
  33.3 4.7 %collective-permute-done.2.rest_2_ = bf16[2,1024,128]{2,1,0:T(8,128)(2,1)} collective-permute-done((bf16[2,1024,128]{2,1,0:T(8,128)(2,1)}, bf16[2,1024,128]{2,1,0:T(8,128)(2,1)}, u32[]{:S(2)}, u32[]{:S(2)}) %collective-permute-start.2) | collective-permute-done | bytes 524320 | tf_op jit(solution)/shard_map/ppermute | solution.py:259
  38.0 0.0 copy-done
  38.0 3.1 %prepare.1 = (bf16[128,4096]{1,0:T(8,128)(2,1)S(1)}, bf16[2,4096,128]{2,1,0:T(8,128)(2,1)S(1)}, bf16[64,64]{1,0:T(8,128)(2,1)S(1)}) custom-call(s32[1]{0:T(128)} %bitcast.place_ref, s32[2]{0:T(128)S(1)} %copy-done, s32[1,64]{1,0:T(1,128)} %bitcast.11, bf16[2,1024,256]{2,1,0:T(8,128)(2,1)} %key_ref.3, bf16[2,1024,256]{2,1,0:T(8,128)(2,1)} %value_ref.3, ...), custom_call_target="tpu_custom_call" | custom-call | tf_op jit(solution)/shard_map/prepare/pallas_call | solution.py:279
  41.1 2.5 %all-to-all-done.1.query_ref = bf16[32,32,128]{2,1,0:T(8,128)(2,1)S(1)} async-done(((bf16[32,32,128]{2,1,0:T(8,128)(2,1)}), bf16[32,32,128]{2,1,0:T(8,128)(2,1)S(1)}, u32[]{:S(2)}, u32[]{:S(2)}) %all-to-all-start.1) | async-done | bytes 262176 | tf_op jit(solution)/shard_map/all_to_all | solution.py:278
  43.6 9.7 %attend.1 = bf16[32,32,128]{2,1,0:T(8,128)(2,1)} custom-call(bf16[32,32,128]{2,1,0:T(8,128)(2,1)S(1)} %all-to-all-done.1.query_ref, bf16[128,4096]{1,0:T(8,128)(2,1)S(1)} %get-tuple-element.24.keys, bf16[2,4096,128]{2,1,0:T(8,128)(2,1)S(1)} %get-tuple-element.25.masked), custom_call_target="tpu_custom_call" | custom-call | tf_op jit(solution)/shard_map/attend/pallas_call | solution.py:297
  53.3 5.7 %all-to-all-start.2 = ((bf16[32,32,128]{2,1,0:T(8,128)(2,1)}), bf16[32,32,128]{2,1,0:T(8,128)(2,1)S(1)}, u32[]{:S(2)}, u32[]{:S(2)}) async-start(bf16[32,32,128]{2,1,0:T(8,128)(2,1)} %attend.1), calls=%async_computation.2 | async-start | bytes 524288 | tf_op jit(solution)/shard_map/all_to_all | solution.py:305
  59.0 1.2 %copy.8 = bf16[256,1024]{0,1:T(8,128)(2,1)S(1)} copy(bf16[256,1024]{1,0:T(8,128)(2,1)} %param.9) | data formatting | bytes 1048576 | tf_op args[2]
  60.3 0.2 copy.9
  60.5 10.5 %all-to-all-done.2.partial_ref = bf16[32,32,128]{2,1,0:T(8,128)(2,1)S(1)} async-done(((bf16[32,32,128]{2,1,0:T(8,128)(2,1)}), bf16[32,32,128]{2,1,0:T(8,128)(2,1)S(1)}, u32[]{:S(2)}, u32[]{:S(2)}) %all-to-all-start.2) | async-done | bytes 262176 | tf_op jit(solution)/shard_map/all_to_all | solution.py:305
  71.0 1.0 %finish.1 = bf16[4,64,256]{2,1,0:T(8,128)(2,1)S(1)} custom-call(s32[2]{0:T(128)S(1)} %copy-done, bf16[64,64]{1,0:T(8,128)(2,1)S(1)} %get-tuple-element.20.back_ref, bf16[32,32,128]{2,1,0:T(8,128)(2,1)S(1)} %all-to-all-done.2.partial_ref, f32[64,256]{1,0:T(8,128)S(1)} %convert_element_type.3.gate_ref, bf16[4,256,256]{2,1,0:T(8,128)(2,1)S(1)} %bitcast.7), custom_call_target="tpu_custom_call" | custom-call | tf_op jit(solution)/shard_map/finish/pallas_call | solution.py:307
  71.9 9.1 %all_to_all.20.term_ref = bf16[4,64,256]{2,1,0:T(8,128)(2,1)S(1)} all-to-all(bf16[4,64,256]{2,1,0:T(8,128)(2,1)S(1)} %finish.1), channel_id=1, replica_groups=mesh['seq'=32,'head'=4,'user'=4] {'head'}, dimensions={0} | all-to-all | bytes 262144 | tf_op jit(solution)/shard_map/all_to_all | solution.py:315
  81.1 0.6 add.1
  (1 shorter events, 0.0 us)
Async XLA Ops:
  2.5 35.5 %copy-start = (s32[2]{0:T(128)S(1)}, s32[2]{0:T(128)}, u32[]{:S(2)}) copy-start(s32[2]{0:T(128)} %length_ref.3) | copy-start | bytes 28
  2.5 22.0 %all-to-all-start = ((bf16[4,64,256]{2,1,0:T(8,128)(2,1)}), bf16[4,64,256]{2,1,0:T(8,128)(2,1)S(1)}, u32[]{:S(2)}, u32[]{:S(2)}) async-start(bf16[4,64,256]{2,1,0:T(8,128)(2,1)} %get-tuple-element.21), calls=%async_computation | async-start | bytes 262144 | tf_op jit(solution)/shard_map/all_to_all | solution.py:263
  11.7 19.9 %collective-permute-start = (bf16[2,1024,128]{2,1,0:T(8,128)(2,1)}, bf16[2,1024,128]{2,1,0:T(8,128)(2,1)S(1)}, u32[]{:S(2)}, u32[]{:S(2)}) collective-permute-start(bf16[2,1024,128]{2,1,0:T(8,128)(2,1)} %get-tuple-element.17), channel_id=1, source_target_pairs={{0,64},{16,80},{32,96},{48,112},{64,0},{80,16},{96,32},{112,48},{1... | collective-permute-start | bytes 1572872 | tf_op jit(solution)/shard_map/ppermute | solution.py:259
  13.7 18.4 %collective-permute-start.1 = (bf16[2,1024,128]{2,1,0:T(8,128)(2,1)}, bf16[2,1024,128]{2,1,0:T(8,128)(2,1)S(1)}, u32[]{:S(2)}, u32[]{:S(2)}) collective-permute-start(bf16[2,1024,128]{2,1,0:T(8,128)(2,1)} %get-tuple-element.18), channel_id=1, source_target_pairs={{0,448},{16,464},{32,480},{48,496},{64,128},{80,144},{96,160},{112... | collective-permute-start | bytes 1572872 | tf_op jit(solution)/shard_map/ppermute | solution.py:259
  20.8 17.2 %collective-permute-start.2 = (bf16[2,1024,128]{2,1,0:T(8,128)(2,1)}, bf16[2,1024,128]{2,1,0:T(8,128)(2,1)}, u32[]{:S(2)}, u32[]{:S(2)}) collective-permute-start(bf16[2,1024,128]{2,1,0:T(8,128)(2,1)} %get-tuple-element.19), channel_id=1, source_target_pairs={{0,16},{16,0},{32,48},{48,32},{64,80},{80,64},{96,112},{112,96},{1... | collective-permute-start | bytes 1572872 | tf_op jit(solution)/shard_map/ppermute | solution.py:259
  25.6 18.0 %all-to-all-start.1 = ((bf16[32,32,128]{2,1,0:T(8,128)(2,1)}), bf16[32,32,128]{2,1,0:T(8,128)(2,1)S(1)}, u32[]{:S(2)}, u32[]{:S(2)}) async-start(bf16[32,32,128]{2,1,0:T(8,128)(2,1)} %get-tuple-element.23), calls=%async_computation.1 | async-start | bytes 524288 | tf_op jit(solution)/shard_map/all_to_all | solution.py:278
  31.7 0.8 copy-start.1
  32.5 0.8 %copy-start.2 = (bf16[2,1024,128]{2,1,0:T(8,128)(2,1)}, bf16[2,1024,128]{2,1,0:T(8,128)(2,1)S(1)}, u32[]{:S(2)}) copy-start(bf16[2,1024,128]{2,1,0:T(8,128)(2,1)S(1)} %collective-permute-done.1.rest_1_) | copy-start | bytes 1572868
  53.3 17.6 %all-to-all-start.2 = ((bf16[32,32,128]{2,1,0:T(8,128)(2,1)}), bf16[32,32,128]{2,1,0:T(8,128)(2,1)S(1)}, u32[]{:S(2)}, u32[]{:S(2)}) async-start(bf16[32,32,128]{2,1,0:T(8,128)(2,1)} %attend.1), calls=%async_computation.2 | async-start | bytes 524288 | tf_op jit(solution)/shard_map/all_to_all | solution.py:305

commit v8 on v7

--- a/solution.py
+++ b/solution.py
@@ -17,6 +17,7 @@
 
 
 SOURCES = 4
+ATTEND_TILE = (1024, 256)
 
 
 def role(place):
@@ -126,11 +127,23 @@
         copy.wait()
 
 
+def after_kernel(*refs):
+    pass
+
+
+def prepare_source(index, owners, place, length, history_ref, at, turned_ref, live_ref):
+    _, span, width = history_ref.shape
+    position = lax.broadcasted_iota(jnp.int32, (span, width), 0)
+    live = length - source(place, index, owners) * span
+    turned_ref[:, at] = history_ref[0].T
+    value = history_ref[1]
+    live_ref[at, :] = jnp.where(position < live, value, jnp.zeros_like(value))
+
+
 def prepare_kernel(
     owners, place_ref, length_ref, user_ref, key_ref, value_ref, *rest
 ):
-    history_refs, rest = rest[: SOURCES - 1], rest[SOURCES - 1 :]
-    turned_ref, masked_ref, back_ref, own, sems = rest
+    *history_refs, turned_ref, live_ref, back_ref, own, sems = rest
     _, span, width = own.shape
     user, half = role(place_ref[0])
     copies = [
@@ -141,46 +154,73 @@
         copy.start()
     _, back = orders_of(user_ref[...], back_ref.shape[0])
     back_ref[...] = back
-    length = length_ref[user]
-    position = lax.broadcasted_iota(jnp.int32, (span, width), 0)
-    for index in reversed(range(SOURCES)):
+    for index in reversed(range(SOURCES - 1)):
         if index == 0:
             for copy in copies:
                 copy.wait()
-        history_ref = history_refs[index - 1] if index else own
-        at = slice(index * span, (index + 1) * span)
-        live = length - source(place_ref[0], index, owners) * span
-        turned_ref[:, at] = history_ref[0].T
-        value = history_ref[1]
-        for head in range(width // HEAD_DIM):
-            keep = (position < live) & head_mask((span, width), head)
-            masked_ref[head, at, :] = jnp.where(keep, value, jnp.zeros_like(value))
-
-
-def attend_kernel(rows_now, positions_now, query_ref, keys, masked, out_ref):
+        prepare_source(
+            index,
+            owners,
+            place_ref[0],
+            length_ref[user],
+            history_refs[index - 1] if index else own,
+            slice(index * span, (index + 1) * span),
+            turned_ref,
+            live_ref,
+        )
+
+
+def attend_rows(rows_now, positions_now, query_ref, keys, values, begun_ref, out_ref):
     blocks, block_rows, width = query_ref.shape
-    heads, positions, _ = masked.shape
+    positions = values.shape[0]
     step_blocks = rows_now // block_rows
+
+    def of_head(array, head):
+        return jnp.where(head_mask(array.shape, head), array, jnp.zeros_like(array))
 
     def step(index, carry):
         here = pl.ds(index * step_blocks, step_blocks)
         query = query_ref[here].reshape(rows_now, width)
-        total = jnp.zeros((rows_now, width), jnp.float32)
+        if begun_ref is None:
+            total = jnp.zeros((rows_now, width), jnp.float32)
+        else:
+            total = begun_ref[here].reshape(rows_now, width)
         for start in range(0, positions, positions_now):
             at = slice(start, start + positions_now)
-            for head in range(heads):
-                own = jnp.where(
-                    head_mask((rows_now, width), head), query, jnp.zeros_like(query)
+            for head in range(width // HEAD_DIM):
+                half = jnp.dot(
+                    of_head(query, head), keys[:, at], preferred_element_type=jnp.float32
                 )
-                half = jnp.dot(own, keys[:, at], preferred_element_type=jnp.float32)
                 weight = (half + half * jnp.tanh(half)).astype(jnp.bfloat16)
                 total += jnp.dot(
-                    weight, masked[head, at, :], preferred_element_type=jnp.float32
+                    weight, of_head(values[at, :], head), preferred_element_type=jnp.float32
                 )
-        out_ref[here] = total.astype(jnp.bfloat16).reshape(step_blocks, block_rows, width)
+        out_ref[here] = total.astype(out_ref.dtype).reshape(step_blocks, block_rows, width)
         return carry
 
     lax.fori_loop(0, blocks // step_blocks, step, 0)
+
+
+def begin_kernel(query_ref, keys, values, out_ref):
+    attend_rows(*ATTEND_TILE, query_ref, keys, values, None, out_ref)
+
+
+def end_kernel(
+    owners, place_ref, length_ref, query_ref, history_ref, begun_ref, out_ref, keys, values
+):
+    user, _ = role(place_ref[0])
+    span = history_ref.shape[1]
+    prepare_source(
+        SOURCES - 1,
+        owners,
+        place_ref[0],
+        length_ref[user],
+        history_ref,
+        slice(0, span),
+        keys,
+        values,
+    )
+    attend_rows(*ATTEND_TILE, query_ref, keys, values, begun_ref, out_ref)
 
 
 def finish_kernel(length_ref, back_ref, partial_ref, gate_ref, weight_ref, out_ref):
@@ -255,16 +295,18 @@
         compiler_params=PARAMS,
         name="share",
     )(place, *map(in_hbm, (users, cand_rows, qu_weight, keys, values)))
-    history = [
-        lax.ppermute(share, "seq", [(s, source(s, index + 1, owners)) for s in range(owners)])
-        for index, share in enumerate(shares)
-    ]
+    def from_source(index, share):
+        return lax.ppermute(
+            share, "seq", [(s, source(s, index, owners)) for s in range(owners)]
+        )
+
+    along_z = [from_source(index + 1, share) for index, share in enumerate(shares[:-1])]
 
     cand_parts = lax.all_to_all(copies, "head", 0, 0, tiled=True)
     queries, gates = pl.pallas_call(
         project_kernel,
         out_shape=(
-            jax.ShapeDtypeStruct((owners, block_rows, lanes), jnp.bfloat16),
+            pltpu.HBM((owners, block_rows, lanes), jnp.bfloat16),
             jax.ShapeDtypeStruct((rows, width), jnp.bfloat16),
         ),
         in_specs=[VMEM] * 2,
@@ -275,17 +317,26 @@
         cand_parts,
         weight.reshape(qu_weight.shape[0], 2 * width),
     )
+    share = pl.pallas_call(
+        after_kernel,
+        out_shape=pltpu.HBM(shares[-1].shape, shares[-1].dtype),
+        in_specs=[HBM] * 2,
+        out_specs=HBM,
+        input_output_aliases={0: 0},
+        compiler_params=PARAMS,
+        name="after",
+    )(in_hbm(shares[-1]), in_hbm(queries))
+    along_y = from_source(SOURCES - 1, share)
     queries = lax.all_to_all(queries, "seq", 0, 0, tiled=True)
-    turned, masked, back = pl.pallas_call(
+    count = (SOURCES - 1) * positions
+    turned, live, back = pl.pallas_call(
         functools.partial(prepare_kernel, owners),
         out_shape=(
-            jax.ShapeDtypeStruct((lanes, SOURCES * positions), jnp.bfloat16),
-            jax.ShapeDtypeStruct(
-                (lanes // HEAD_DIM, SOURCES * positions, lanes), jnp.bfloat16
-            ),
+            jax.ShapeDtypeStruct((lanes, count), jnp.bfloat16),
+            jax.ShapeDtypeStruct((count, lanes), jnp.bfloat16),
             pltpu.VMEM((rows, rows), jnp.bfloat16),
         ),
-        in_specs=[SMEM] * 2 + [VMEM] + [HBM] * 2 + [VMEM] * (SOURCES - 1),
+        in_specs=[SMEM] * 2 + [VMEM] + [HBM] * 2 + [VMEM] * (SOURCES - 2),
         out_specs=(VMEM,) * 3,
         scratch_shapes=[
             pltpu.VMEM((2, positions, lanes), jnp.bfloat16),
@@ -293,15 +344,33 @@
         ],
         compiler_params=PARAMS,
         name="prepare",
-    )(place, lengths, *map(in_hbm, (users, keys, values, *history)))
-    totals = pl.pallas_call(
-        functools.partial(attend_kernel, 1024, 256),
-        out_shape=jax.ShapeDtypeStruct((owners, block_rows, lanes), jnp.bfloat16),
+    )(place, lengths, *map(in_hbm, (users, keys, values, *along_z)))
+    begun = pl.pallas_call(
+        begin_kernel,
+        out_shape=jax.ShapeDtypeStruct((owners, block_rows, lanes), jnp.float32),
         in_specs=[VMEM] * 3,
         out_specs=VMEM,
         compiler_params=ATTEND_PARAMS,
-        name="attend",
-    )(queries, turned, masked)
+        cost_estimate=pl.CostEstimate(
+            flops=8 * owners * block_rows * lanes * count, bytes_accessed=0, transcendentals=0
+        ),
+        name="begin",
+    )(queries, turned, live)
+    totals = pl.pallas_call(
+        functools.partial(end_kernel, owners),
+        out_shape=jax.ShapeDtypeStruct((owners, block_rows, lanes), jnp.bfloat16),
+        in_specs=[SMEM] * 2 + [VMEM] * 3,
+        out_specs=VMEM,
+        scratch_shapes=[
+            pltpu.VMEM((lanes, positions), jnp.bfloat16),
+            pltpu.VMEM((positions, lanes), jnp.bfloat16),
+        ],
+        compiler_params=ATTEND_PARAMS,
+        cost_estimate=pl.CostEstimate(
+            flops=8 * owners * block_rows * lanes * positions, bytes_accessed=0, transcendentals=0
+        ),
+        name="end",
+    )(place, lengths, queries, along_y, begun)
     totals = lax.all_to_all(totals, "seq", 0, 0, tiled=True)
     blocks = jnp.transpose(out_weight.reshape(width, groups, depth), (1, 0, 2))
     terms = pl.pallas_call(

time: 82.3 us -> 83.2 us (1.011)
  starting transfers between devices: 33.5 us -> 35.4 us
  local copies, waits for them, and re-layouts: 2.92 us -> 1.44 us
    ppermute x3, waiting for transfers between devices: 5.1 us -> 3.14 us  [from_source(): lax.ppermute(share, 'seq', [(s, source(s, index, owners)) for s in range(...]
    unnamed x8 -> x10, local copies, waits for them, and re-layouts: 2.72 us -> 1.24 us
    all_to_all x1, waiting for transfers between devices: 2.55 us -> 3.62 us  [local(): queries = lax.all_to_all(queries, 'seq', 0, 0, tiled=True)]
    all_to_all x1, waiting for transfers between devices: 10.5 us -> 11.5 us  [local(): totals = lax.all_to_all(totals, 'seq', 0, 0, tiled=True)]
    all_to_all x1, starting transfers between devices: 6.06 us -> 7.08 us  [local(): queries = lax.all_to_all(queries, 'seq', 0, 0, tiled=True)]
    pallas_call x2 -> x4, Pallas kernels: 10.8 us -> 11.7 us  [the longest x1 6.84 us: local(): pl.pallas_call(begin_kernel, out_shape=jax.ShapeDtypeStruct((owners, bloc...]
  transfers between devices with their start and end apart: 6 -> 6, of which waited for: 4 -> 3; matrix products, arithmetic and copies ran while one was open for 2% -> 1% of each run, Pallas kernels for 5% -> 12%
where the time goes in v8:
time: 83.2 us; the launch traced here: 82.7 us
  starting transfers between devices  35.4 us (43%)
  Pallas kernels  18.3 us (22%)
  waiting for transfers between devices  18.3 us (22%)
  blocking collectives  9.12 us (11%)
  local copies, waits for them, and re-layouts  1.44 us (2%)
    ppermute x3, starting transfers between devices, from_source(): lax.ppermute(share, 'seq', [(s, source(s, index, owners)) for s in range(...  12.7 us
    all_to_all x1, waiting for transfers between devices, local(): totals = lax.all_to_all(totals, 'seq', 0, 0, tiled=True)  11.5 us
    all_to_all x1, starting transfers between devices, local(): cand_parts = lax.all_to_all(copies, 'head', 0, 0, tiled=True)  9.21 us
    all_to_all x1, blocking collectives, local(): terms = lax.all_to_all(terms, 'head', 0, 0, tiled=True)  9.12 us
    all_to_all x1, starting transfers between devices, local(): queries = lax.all_to_all(queries, 'seq', 0, 0, tiled=True)  7.08 us
    pallas_call x1, Pallas kernels, local(): pl.pallas_call(begin_kernel, out_shape=jax.ShapeDtypeStruct((owners, bloc...  6.84 us
    all_to_all x1, starting transfers between devices, local(): totals = lax.all_to_all(totals, 'seq', 0, 0, tiled=True)  6.43 us
    pallas_call x1, Pallas kernels, local(): pl.pallas_call(functools.partial(end_kernel, owners), out_shape=jax.Shape...  3.8 us
  transfers between devices with their start and end apart: 6, of which 3 were waited for; matrix products, arithmetic and copies ran while one was open for 1% of the time, Pallas kernels for 12%

profile of v8, /device:TPU:2, one launch (start us, length us, event | category | flops | bytes accessed | tf_op | source)
XLA Modules:
  0.0 82.7 jit_solution(16240590266355651759)
XLA Ops:
  0.0 2.6 %share.1 = (bf16[2,1024,128]{2,1,0:T(8,128)(2,1)}, bf16[2,1024,128]{2,1,0:T(8,128)(2,1)}, bf16[2,1024,128]{2,1,0:T(8,128)(2,1)}, bf16[4,64,256]{2,1,0:T(8,128)(2...) custom-call(s32[1]{0:T(128)} %bitcast.place_ref, s32[1,64]{1,0:T(1,128)} %bitcast.10, ...), custom_call_target="tpu_custom_call" | custom-call | tf_op jit(solution)/shard_map/share/pallas_call | solution.py:277
  2.6 9.2 %all-to-all-start = ((bf16[4,64,256]{2,1,0:T(8,128)(2,1)}), bf16[4,64,256]{2,1,0:T(8,128)(2,1)S(1)}, u32[]{:S(2)}, u32[]{:S(2)}) async-start(bf16[4,64,256]{2,1,0:T(8,128)(2,1)} %get-tuple-element.20), calls=%async_computation | async-start | bytes 262144 | tf_op jit(solution)/shard_map/all_to_all | solution.py:305
  11.8 1.9 %collective-permute-start = (bf16[2,1024,128]{2,1,0:T(8,128)(2,1)}, bf16[2,1024,128]{2,1,0:T(8,128)(2,1)S(1)}, u32[]{:S(2)}, u32[]{:S(2)}) collective-permute-start(bf16[2,1024,128]{2,1,0:T(8,128)(2,1)} %get-tuple-element.17), channel_id=1, source_target_pairs={{0,64},{16,80},{32,96},{48,112},{64,0},{80,16},{96,32},{112,48},{1... | collective-permute-start | bytes 1572872 | tf_op jit(solution)/shard_map/ppermute | solution.py:299
  13.7 7.1 %collective-permute-start.1 = (bf16[2,1024,128]{2,1,0:T(8,128)(2,1)}, bf16[2,1024,128]{2,1,0:T(8,128)(2,1)S(1)}, u32[]{:S(2)}, u32[]{:S(2)}) collective-permute-start(bf16[2,1024,128]{2,1,0:T(8,128)(2,1)} %get-tuple-element.18), channel_id=1, source_target_pairs={{0,448},{16,464},{32,480},{48,496},{64,128},{80,144},{96,160},{112... | collective-permute-start | bytes 1572872 | tf_op jit(solution)/shard_map/ppermute | solution.py:299
  20.8 0.2 copy.11
  21.1 0.0 all-to-all-done.cand_ref
  21.1 1.0 %project.1 = (bf16[32,32,128]{2,1,0:T(8,128)(2,1)}, bf16[64,256]{1,0:T(8,128)(2,1)S(1)}) custom-call(bf16[4,64,256]{2,1,0:T(8,128)(2,1)S(1)} %all-to-all-done.cand_ref, bf16[1024,512]{1,0:T(8,128)(2,1)S(1)} %bitcast.6), custom_call_target="tpu_custom_call" | custom-call | tf_op jit(solution)/shard_map/project/pallas_call | solution.py:306
  22.1 7.1 %all-to-all-start.1 = ((bf16[32,32,128]{2,1,0:T(8,128)(2,1)}), bf16[32,32,128]{2,1,0:T(8,128)(2,1)S(1)}, u32[]{:S(2)}, u32[]{:S(2)}) async-start(bf16[32,32,128]{2,1,0:T(8,128)(2,1)} %get-tuple-element.22.refs_1_), calls=%async_computation.1 | async-start | bytes 524288 | tf_op jit(solution)/shard_map/all_to_all | solution.py:330
  29.2 0.0 copy-start
  29.2 3.7 %collective-permute-start.2 = (bf16[2,1024,128]{2,1,0:T(8,128)(2,1)}, bf16[2,1024,128]{2,1,0:T(8,128)(2,1)S(1)}, u32[]{:S(2)}, u32[]{:S(2)}) collective-permute-start(bf16[2,1024,128]{2,1,0:T(8,128)(2,1)} %after.1), channel_id=1, source_target_pairs={{0,16},{16,0},{32,48},{48,32},{64,80},{80,64},{96,112},{112,96},{1... | collective-permute-start | bytes 1572872 | tf_op jit(solution)/shard_map/ppermute | solution.py:299
  32.9 0.0 collective-permute-done.rest_0_
  32.9 0.0 copy-start.1
  32.9 3.1 %collective-permute-done.1.rest_1_ = bf16[2,1024,128]{2,1,0:T(8,128)(2,1)S(1)} collective-permute-done((bf16[2,1024,128]{2,1,0:T(8,128)(2,1)}, bf16[2,1024,128]{2,1,0:T(8,128)(2,1)S(1)}, u32[]{:S(2)}, u32[]{:S(2)}) %collective-permute-start.1) | collective-permute-done | bytes 524320 | tf_op jit(solution)/shard_map/ppermute | solution.py:299
  36.1 0.0 copy-done.1
  36.1 0.0 copy-start.2
  36.1 0.8 copy-done.2
  36.9 0.0 copy-done
  36.9 2.4 %prepare.1 = (bf16[128,3072]{1,0:T(8,128)(2,1)S(1)}, bf16[3072,128]{1,0:T(8,128)(2,1)S(1)}, bf16[64,64]{1,0:T(8,128)(2,1)S(1)}) custom-call(s32[1]{0:T(128)} %bitcast.place_ref, s32[2]{0:T(128)S(1)} %copy-done, s32[1,64]{1,0:T(1,128)} %bitcast.11, bf16[2,1024,256]{2,1,0:T(8,128)(2,1)} %key_ref.3, bf16[2,1024,256]{2,1,0:T(8,128)(2,1)} %value_ref.3, ...), custom_call_target="tpu_custom_call" | custom-call | tf_op jit(solution)/shard_map/prepare/pallas_call | solution.py:332
  39.3 3.6 %all-to-all-done.1.query_ref = bf16[32,32,128]{2,1,0:T(8,128)(2,1)S(1)} async-done(((bf16[32,32,128]{2,1,0:T(8,128)(2,1)}), bf16[32,32,128]{2,1,0:T(8,128)(2,1)S(1)}, u32[]{:S(2)}, u32[]{:S(2)}) %all-to-all-start.1) | async-done | bytes 262176 | tf_op jit(solution)/shard_map/all_to_all | solution.py:330
  42.9 6.8 %begin.1.begun_ref = f32[32,32,128]{2,1,0:T(8,128)S(1)} custom-call(bf16[32,32,128]{2,1,0:T(8,128)(2,1)S(1)} %all-to-all-done.1.query_ref, bf16[128,3072]{1,0:T(8,128)(2,1)S(1)} %get-tuple-element.24.keys, bf16[3072,128]{1,0:T(8,128)(2,1)S(1)} %get-tuple-element.25.values), custom_call_target="tpu_custom_call" | custom-call | flops 3221225472 | tf_op jit(solution)/shard_map/begin/pallas_call | solution.py:348
  49.8 0.0 collective-permute-done.2.history_ref
  49.8 3.8 %end.1 = bf16[32,32,128]{2,1,0:T(8,128)(2,1)} custom-call(s32[1]{0:T(128)} %bitcast.place_ref, s32[2]{0:T(128)S(1)} %copy-done, bf16[32,32,128]{2,1,0:T(8,128)(2,1)S(1)} %all-to-all-done.1.query_ref, bf16[2,1024,128]{2,1,0:T(8,128)(2,1)S(1)} %collective-permute-done.2.history_ref, f32[32,32,128]{2,1,0:T(8,128)S(1)} %begin.1.begun_ref), custom_call_target="tpu_custom_call" | custom-call | flops 1073741824 | tf_op jit(solution)/shard_map/end/pallas_call | solution.py:359
  53.6 0.0 copy-start.3
  53.6 6.4 %all-to-all-start.2 = ((bf16[32,32,128]{2,1,0:T(8,128)(2,1)}), bf16[32,32,128]{2,1,0:T(8,128)(2,1)S(1)}, u32[]{:S(2)}, u32[]{:S(2)}) async-start(bf16[32,32,128]{2,1,0:T(8,128)(2,1)} %end.1), calls=%async_computation.2 | async-start | bytes 524288 | tf_op jit(solution)/shard_map/all_to_all | solution.py:374
  60.0 0.0 copy-done.3
  60.0 0.2 copy.9
  60.2 0.2 copy.10
  60.5 11.5 %all-to-all-done.2.partial_ref = bf16[32,32,128]{2,1,0:T(8,128)(2,1)S(1)} async-done(((bf16[32,32,128]{2,1,0:T(8,128)(2,1)}), bf16[32,32,128]{2,1,0:T(8,128)(2,1)S(1)}, u32[]{:S(2)}, u32[]{:S(2)}) %all-to-all-start.2) | async-done | bytes 262176 | tf_op jit(solution)/shard_map/all_to_all | solution.py:374
  72.0 1.0 %finish.1 = bf16[4,64,256]{2,1,0:T(8,128)(2,1)S(1)} custom-call(s32[2]{0:T(128)S(1)} %copy-done, bf16[64,64]{1,0:T(8,128)(2,1)S(1)} %get-tuple-element.19.back_ref, bf16[32,32,128]{2,1,0:T(8,128)(2,1)S(1)} %all-to-all-done.2.partial_ref, f32[64,256]{1,0:T(8,128)S(1)} %convert_element_type.3.gate_ref, bf16[4,256,256]{2,1,0:T(8,128)(2,1)S(1)} %bitcast.7), custom_call_target="tpu_custom_call" | custom-call | tf_op jit(solution)/shard_map/finish/pallas_call | solution.py:376
  72.9 9.1 %all_to_all.20.term_ref = bf16[4,64,256]{2,1,0:T(8,128)(2,1)S(1)} all-to-all(bf16[4,64,256]{2,1,0:T(8,128)(2,1)S(1)} %finish.1), channel_id=1, replica_groups=mesh['seq'=32,'head'=4,'user'=4] {'head'}, dimensions={0} | all-to-all | bytes 262144 | tf_op jit(solution)/shard_map/all_to_all | solution.py:384
  82.0 0.6 add.1
  (2 shorter events, 0.0 us)
Async XLA Ops:
  2.6 18.5 %all-to-all-start = ((bf16[4,64,256]{2,1,0:T(8,128)(2,1)}), bf16[4,64,256]{2,1,0:T(8,128)(2,1)S(1)}, u32[]{:S(2)}, u32[]{:S(2)}) async-start(bf16[4,64,256]{2,1,0:T(8,128)(2,1)} %get-tuple-element.20), calls=%async_computation | async-start | bytes 262144 | tf_op jit(solution)/shard_map/all_to_all | solution.py:305
  11.8 21.2 %collective-permute-start = (bf16[2,1024,128]{2,1,0:T(8,128)(2,1)}, bf16[2,1024,128]{2,1,0:T(8,128)(2,1)S(1)}, u32[]{:S(2)}, u32[]{:S(2)}) collective-permute-start(bf16[2,1024,128]{2,1,0:T(8,128)(2,1)} %get-tuple-element.17), channel_id=1, source_target_pairs={{0,64},{16,80},{32,96},{48,112},{64,0},{80,16},{96,32},{112,48},{1... | collective-permute-start | bytes 1572872 | tf_op jit(solution)/shard_map/ppermute | solution.py:299
  13.7 22.4 %collective-permute-start.1 = (bf16[2,1024,128]{2,1,0:T(8,128)(2,1)}, bf16[2,1024,128]{2,1,0:T(8,128)(2,1)S(1)}, u32[]{:S(2)}, u32[]{:S(2)}) collective-permute-start(bf16[2,1024,128]{2,1,0:T(8,128)(2,1)} %get-tuple-element.18), channel_id=1, source_target_pairs={{0,448},{16,464},{32,480},{48,496},{64,128},{80,144},{96,160},{112... | collective-permute-start | bytes 1572872 | tf_op jit(solution)/shard_map/ppermute | solution.py:299
  22.1 20.8 %all-to-all-start.1 = ((bf16[32,32,128]{2,1,0:T(8,128)(2,1)}), bf16[32,32,128]{2,1,0:T(8,128)(2,1)S(1)}, u32[]{:S(2)}, u32[]{:S(2)}) async-start(bf16[32,32,128]{2,1,0:T(8,128)(2,1)} %get-tuple-element.22.refs_1_), calls=%async_computation.1 | async-start | bytes 524288 | tf_op jit(solution)/shard_map/all_to_all | solution.py:330
  29.2 7.7 %copy-start = (s32[2]{0:T(128)S(1)}, s32[2]{0:T(128)}, u32[]{:S(2)}) copy-start(s32[2]{0:T(128)} %length_ref.5) | copy-start | bytes 28
  29.2 20.5 %collective-permute-start.2 = (bf16[2,1024,128]{2,1,0:T(8,128)(2,1)}, bf16[2,1024,128]{2,1,0:T(8,128)(2,1)S(1)}, u32[]{:S(2)}, u32[]{:S(2)}) collective-permute-start(bf16[2,1024,128]{2,1,0:T(8,128)(2,1)} %after.1), channel_id=1, source_target_pairs={{0,16},{16,0},{32,48},{48,32},{64,80},{80,64},{96,112},{112,96},{1... | collective-permute-start | bytes 1572872 | tf_op jit(solution)/shard_map/ppermute | solution.py:299
  32.9 3.1 %copy-start.1 = (bf16[2,1024,128]{2,1,0:T(8,128)(2,1)}, bf16[2,1024,128]{2,1,0:T(8,128)(2,1)S(1)}, u32[]{:S(2)}) copy-start(bf16[2,1024,128]{2,1,0:T(8,128)(2,1)S(1)} %collective-permute-done.rest_0_) | copy-start | bytes 1572868
  36.1 0.8 copy-start.2
  53.6 6.4 %copy-start.3 = (bf16[256,1024]{1,0:T(8,128)(2,1)S(1)}, bf16[256,1024]{1,0:T(8,128)(2,1)}, u32[]{:S(2)}) copy-start(bf16[256,1024]{1,0:T(8,128)(2,1)} %param.9) | copy-start | bytes 1572868
  53.6 18.4 %all-to-all-start.2 = ((bf16[32,32,128]{2,1,0:T(8,128)(2,1)}), bf16[32,32,128]{2,1,0:T(8,128)(2,1)S(1)}, u32[]{:S(2)}, u32[]{:S(2)}) async-start(bf16[32,32,128]{2,1,0:T(8,128)(2,1)} %end.1), calls=%async_computation.2 | async-start | bytes 524288 | tf_op jit(solution)/shard_map/all_to_all | solution.py:374

commit v9 on v7

--- a/solution.py
+++ b/solution.py
@@ -130,7 +130,7 @@
     owners, place_ref, length_ref, user_ref, key_ref, value_ref, *rest
 ):
     history_refs, rest = rest[: SOURCES - 1], rest[SOURCES - 1 :]
-    turned_ref, masked_ref, back_ref, own, sems = rest
+    turned_ref, live_ref, back_ref, own, sems = rest
     _, span, width = own.shape
     user, half = role(place_ref[0])
     copies = [
@@ -152,15 +152,16 @@
         live = length - source(place_ref[0], index, owners) * span
         turned_ref[:, at] = history_ref[0].T
         value = history_ref[1]
-        for head in range(width // HEAD_DIM):
-            keep = (position < live) & head_mask((span, width), head)
-            masked_ref[head, at, :] = jnp.where(keep, value, jnp.zeros_like(value))
-
-
-def attend_kernel(rows_now, positions_now, query_ref, keys, masked, out_ref):
+        live_ref[at, :] = jnp.where(position < live, value, jnp.zeros_like(value))
+
+
+def attend_kernel(rows_now, positions_now, query_ref, keys, values, out_ref):
     blocks, block_rows, width = query_ref.shape
-    heads, positions, _ = masked.shape
+    positions = values.shape[0]
     step_blocks = rows_now // block_rows
+
+    def of_head(array, head):
+        return jnp.where(head_mask(array.shape, head), array, jnp.zeros_like(array))
 
     def step(index, carry):
         here = pl.ds(index * step_blocks, step_blocks)
@@ -168,14 +169,13 @@
         total = jnp.zeros((rows_now, width), jnp.float32)
         for start in range(0, positions, positions_now):
             at = slice(start, start + positions_now)
-            for head in range(heads):
-                own = jnp.where(
-                    head_mask((rows_now, width), head), query, jnp.zeros_like(query)
+            for head in range(width // HEAD_DIM):
+                half = jnp.dot(
+                    of_head(query, head), keys[:, at], preferred_element_type=jnp.float32
                 )
-                half = jnp.dot(own, keys[:, at], preferred_element_type=jnp.float32)
                 weight = (half + half * jnp.tanh(half)).astype(jnp.bfloat16)
                 total += jnp.dot(
-                    weight, masked[head, at, :], preferred_element_type=jnp.float32
+                    weight, of_head(values[at, :], head), preferred_element_type=jnp.float32
                 )
         out_ref[here] = total.astype(jnp.bfloat16).reshape(step_blocks, block_rows, width)
         return carry
@@ -203,12 +203,12 @@
         summed = jnp.sum(jnp.where(mask, square, 0.0), axis=1, keepdims=True)
         mean = jnp.where(mask, summed * (1.0 / HEAD_DIM), mean)
     normed = attn * lax.rsqrt(mean + 1e-06)
-    gated = (normed * gate_ref[...]).astype(jnp.bfloat16)
+    gated = (normed * gate_ref[...].astype(jnp.float32)).astype(jnp.bfloat16)
     gated = jnp.dot(back_ref[...], gated, preferred_element_type=jnp.float32).astype(jnp.bfloat16)
     for part in range(out_ref.shape[0]):
         out_ref[part] = jnp.dot(
             gated,
-            weight_ref[part],
+            weight_ref[:, part * width : (part + 1) * width],
             preferred_element_type=jnp.float32,
         ).astype(out_ref.dtype)
 
@@ -276,13 +276,11 @@
         weight.reshape(qu_weight.shape[0], 2 * width),
     )
     queries = lax.all_to_all(queries, "seq", 0, 0, tiled=True)
-    turned, masked, back = pl.pallas_call(
+    turned, live, back = pl.pallas_call(
         functools.partial(prepare_kernel, owners),
         out_shape=(
             jax.ShapeDtypeStruct((lanes, SOURCES * positions), jnp.bfloat16),
-            jax.ShapeDtypeStruct(
-                (lanes // HEAD_DIM, SOURCES * positions, lanes), jnp.bfloat16
-            ),
+            jax.ShapeDtypeStruct((SOURCES * positions, lanes), jnp.bfloat16),
             pltpu.VMEM((rows, rows), jnp.bfloat16),
         ),
         in_specs=[SMEM] * 2 + [VMEM] + [HBM] * 2 + [VMEM] * (SOURCES - 1),
@@ -301,9 +299,8 @@
         out_specs=VMEM,
         compiler_params=ATTEND_PARAMS,
         name="attend",
-    )(queries, turned, masked)
+    )(queries, turned, live)
     totals = lax.all_to_all(totals, "seq", 0, 0, tiled=True)
-    blocks = jnp.transpose(out_weight.reshape(width, groups, depth), (1, 0, 2))
     terms = pl.pallas_call(
         finish_kernel,
         out_shape=jax.ShapeDtypeStruct((groups, rows, depth), jnp.bfloat16),
@@ -311,7 +308,7 @@
         out_specs=VMEM,
         compiler_params=PARAMS,
         name="finish",
-    )(lengths, back, totals, gates.astype(jnp.float32), blocks)
+    )(lengths, back, totals, gates, out_weight)
     terms = lax.all_to_all(terms, "head", 0, 0, tiled=True)
     return pl.pallas_call(
         add_kernel,

time: 82.3 us -> 81.4 us (0.989)
  blocking collectives: 9.12 us -> 26.6 us
  waiting for transfers between devices: 18.1 us -> 9.12 us
  starting transfers between devices: 33.5 us -> 27.9 us
  local copies, waits for them, and re-layouts: 2.92 us -> 0.24 us
  Pallas kernels: 18 us -> 17 us
    all_to_all x0 -> x1, blocking collectives: none -> 17.5 us  [local(): totals = lax.all_to_all(totals, 'seq', 0, 0, tiled=True)]
    all_to_all x1 -> x0, waiting for transfers between devices: 10.5 us -> none  [local(): totals = lax.all_to_all(totals, 'seq', 0, 0, tiled=True)]
    all_to_all x1 -> x0, starting transfers between devices: 5.68 us -> none  [local(): totals = lax.all_to_all(totals, 'seq', 0, 0, tiled=True)]
    unnamed x8 -> x9, local copies, waits for them, and re-layouts: 2.72 us -> 0.24 us
    ppermute x3, waiting for transfers between devices: 5.1 us -> 6.22 us  [local(): lax.ppermute(share, 'seq', [(s, source(s, index + 1, owners)) for s in ra...]
  transfers between devices with their start and end apart: 6 -> 5, of which waited for: 4 -> 3; matrix products, arithmetic and copies ran while one was open for 2% -> 0% of each run, Pallas kernels for 5% -> 5%
where the time goes in v9:
time: 81.4 us; the launch traced here: 80.9 us
  starting transfers between devices  27.9 us (34%)
  blocking collectives  26.6 us (33%)
  Pallas kernels  17 us (21%)
  waiting for transfers between devices  9.12 us (11%)
    all_to_all x1, blocking collectives, local(): totals = lax.all_to_all(totals, 'seq', 0, 0, tiled=True)  17.5 us
    ppermute x3, starting transfers between devices, local(): lax.ppermute(share, 'seq', [(s, source(s, index + 1, owners)) for s in ra...  12.5 us
    all_to_all x1, starting transfers between devices, local(): cand_parts = lax.all_to_all(copies, 'head', 0, 0, tiled=True)  9.21 us
    all_to_all x1, blocking collectives, local(): terms = lax.all_to_all(terms, 'head', 0, 0, tiled=True)  9.12 us
    pallas_call x1, Pallas kernels, local(): pl.pallas_call(functools.partial(attend_kernel, 1024, 256), out_shape=jax...  9.02 us
    ppermute x3, waiting for transfers between devices, local(): lax.ppermute(share, 'seq', [(s, source(s, index + 1, owners)) for s in ra...  6.22 us
    all_to_all x1, starting transfers between devices, local(): queries = lax.all_to_all(queries, 'seq', 0, 0, tiled=True)  6.19 us
    all_to_all x1, waiting for transfers between devices, local(): queries = lax.all_to_all(queries, 'seq', 0, 0, tiled=True)  2.89 us
  transfers between devices with their start and end apart: 5, of which 3 were waited for; matrix products, arithmetic and copies ran while one was open for 0% of the time, Pallas kernels for 5%

profile of v9, /device:TPU:2, one launch (start us, length us, event | category | flops | bytes accessed | tf_op | source)
XLA Modules:
  0.0 80.9 jit_solution(16513638487340067844)
XLA Ops:
  0.0 2.5 %share.1 = (bf16[2,1024,128]{2,1,0:T(8,128)(2,1)}, bf16[2,1024,128]{2,1,0:T(8,128)(2,1)}, bf16[2,1024,128]{2,1,0:T(8,128)(2,1)}, bf16[4,64,256]{2,1,0:T(8,128)(2...) custom-call(s32[1]{0:T(128)} %bitcast.place_ref, s32[1,64]{1,0:T(1,128)} %bitcast.6, ...), custom_call_target="tpu_custom_call" | custom-call | tf_op jit(solution)/shard_map/share/pallas_call | solution.py:237
  2.5 9.2 %all-to-all-start = ((bf16[4,64,256]{2,1,0:T(8,128)(2,1)}), bf16[4,64,256]{2,1,0:T(8,128)(2,1)S(1)}, u32[]{:S(2)}, u32[]{:S(2)}) async-start(bf16[4,64,256]{2,1,0:T(8,128)(2,1)} %get-tuple-element.21), calls=%async_computation | async-start | bytes 262144 | tf_op jit(solution)/shard_map/all_to_all | solution.py:263
  11.7 1.9 %collective-permute-start = (bf16[2,1024,128]{2,1,0:T(8,128)(2,1)}, bf16[2,1024,128]{2,1,0:T(8,128)(2,1)S(1)}, u32[]{:S(2)}, u32[]{:S(2)}) collective-permute-start(bf16[2,1024,128]{2,1,0:T(8,128)(2,1)} %get-tuple-element.17), channel_id=1, source_target_pairs={{0,64},{16,80},{32,96},{48,112},{64,0},{80,16},{96,32},{112,48},{1... | collective-permute-start | bytes 1572872 | tf_op jit(solution)/shard_map/ppermute | solution.py:259
  13.7 7.1 %collective-permute-start.1 = (bf16[2,1024,128]{2,1,0:T(8,128)(2,1)}, bf16[2,1024,128]{2,1,0:T(8,128)(2,1)S(1)}, u32[]{:S(2)}, u32[]{:S(2)}) collective-permute-start(bf16[2,1024,128]{2,1,0:T(8,128)(2,1)} %get-tuple-element.18), channel_id=1, source_target_pairs={{0,448},{16,464},{32,480},{48,496},{64,128},{80,144},{96,160},{112... | collective-permute-start | bytes 1572872 | tf_op jit(solution)/shard_map/ppermute | solution.py:259
  20.8 3.5 %collective-permute-start.2 = (bf16[2,1024,128]{2,1,0:T(8,128)(2,1)}, bf16[2,1024,128]{2,1,0:T(8,128)(2,1)}, u32[]{:S(2)}, u32[]{:S(2)}) collective-permute-start(bf16[2,1024,128]{2,1,0:T(8,128)(2,1)} %get-tuple-element.19), channel_id=1, source_target_pairs={{0,16},{16,0},{32,48},{48,32},{64,80},{80,64},{96,112},{112,96},{1... | collective-permute-start | bytes 1572872 | tf_op jit(solution)/shard_map/ppermute | solution.py:259
  24.3 0.2 copy.8
  24.5 0.0 all-to-all-done.cand_ref
  24.5 1.0 %project.1 = (bf16[32,32,128]{2,1,0:T(8,128)(2,1)}, bf16[64,256]{1,0:T(8,128)(2,1)S(1)}) custom-call(bf16[4,64,256]{2,1,0:T(8,128)(2,1)S(1)} %all-to-all-done.cand_ref, bf16[1024,512]{1,0:T(8,128)(2,1)S(1)} %bitcast.4), custom_call_target="tpu_custom_call" | custom-call | tf_op jit(solution)/shard_map/project/pallas_call | solution.py:264
  25.5 0.0 copy-start.1
  25.6 6.2 %all-to-all-start.1 = ((bf16[32,32,128]{2,1,0:T(8,128)(2,1)}), bf16[32,32,128]{2,1,0:T(8,128)(2,1)S(1)}, u32[]{:S(2)}, u32[]{:S(2)}) async-start(bf16[32,32,128]{2,1,0:T(8,128)(2,1)} %get-tuple-element.23), calls=%async_computation.1 | async-start | bytes 524288 | tf_op jit(solution)/shard_map/all_to_all | solution.py:278
  31.8 0.0 collective-permute-done.rest_0_
  31.8 0.0 copy-start.2
  31.8 0.3 collective-permute-done.1.rest_1_
  32.1 0.0 copy-start.3
  32.1 5.9 %collective-permute-done.2.rest_2_ = bf16[2,1024,128]{2,1,0:T(8,128)(2,1)} collective-permute-done((bf16[2,1024,128]{2,1,0:T(8,128)(2,1)}, bf16[2,1024,128]{2,1,0:T(8,128)(2,1)}, u32[]{:S(2)}, u32[]{:S(2)}) %collective-permute-start.2) | collective-permute-done | bytes 524320 | tf_op jit(solution)/shard_map/ppermute | solution.py:259
  38.0 0.0 copy-done.2
  38.0 0.0 copy-done.3
  38.0 0.0 copy-done.1
  38.0 2.8 %prepare.1 = (bf16[128,4096]{1,0:T(8,128)(2,1)S(1)}, bf16[4096,128]{1,0:T(8,128)(2,1)S(1)}, bf16[64,64]{1,0:T(8,128)(2,1)S(1)}) custom-call(s32[1]{0:T(128)} %bitcast.place_ref, s32[2]{0:T(128)S(1)} %copy-done.1, s32[1,64]{1,0:T(1,128)} %bitcast.7, bf16[2,1024,256]{2,1,0:T(8,128)(2,1)} %key_ref.3, bf16[2,1024,256]{2,1,0:T(8,128)(2,1)} %value_ref.3, ...), custom_call_target="tpu_custom_call" | custom-call | tf_op jit(solution)/shard_map/prepare/pallas_call | solution.py:279
  40.8 2.9 %all-to-all-done.1.query_ref = bf16[32,32,128]{2,1,0:T(8,128)(2,1)S(1)} async-done(((bf16[32,32,128]{2,1,0:T(8,128)(2,1)}), bf16[32,32,128]{2,1,0:T(8,128)(2,1)S(1)}, u32[]{:S(2)}, u32[]{:S(2)}) %all-to-all-start.1) | async-done | bytes 262176 | tf_op jit(solution)/shard_map/all_to_all | solution.py:278
  43.7 9.0 %attend.1 = bf16[32,32,128]{2,1,0:T(8,128)(2,1)S(1)} custom-call(bf16[32,32,128]{2,1,0:T(8,128)(2,1)S(1)} %all-to-all-done.1.query_ref, bf16[128,4096]{1,0:T(8,128)(2,1)S(1)} %get-tuple-element.24.keys, bf16[4096,128]{1,0:T(8,128)(2,1)S(1)} %get-tuple-element.25.values), custom_call_target="tpu_custom_call" | custom-call | tf_op jit(solution)/shard_map/attend/pallas_call | solution.py:295
  52.7 0.0 copy-start
  52.7 17.5 %all_to_all.20.partial_ref = bf16[32,32,128]{2,1,0:T(8,128)(2,1)S(1)} all-to-all(bf16[32,32,128]{2,1,0:T(8,128)(2,1)S(1)} %attend.1), channel_id=1, replica_groups=mesh['seq'=32,'head'=4,'user'=4] {'seq'}, dimensions={0} | all-to-all | bytes 524288 | tf_op jit(solution)/shard_map/all_to_all | solution.py:303
  70.2 0.0 copy-done
  70.2 1.0 %finish.1 = bf16[4,64,256]{2,1,0:T(8,128)(2,1)S(1)} custom-call(s32[2]{0:T(128)S(1)} %copy-done.1, bf16[64,64]{1,0:T(8,128)(2,1)S(1)} %get-tuple-element.20.back_ref, bf16[32,32,128]{2,1,0:T(8,128)(2,1)S(1)} %all_to_all.20.partial_ref, bf16[64,256]{1,0:T(8,128)(2,1)S(1)} %get-tuple-element.26.gate_ref, bf16[256,1024]{1,0:T(8,128)(2,1)S(1)} %copy-done), custom_call_target="tpu_custom_call" | custom-call | tf_op jit(solution)/shard_map/finish/pallas_call | solution.py:304
  71.2 9.1 %all_to_all.21.term_ref = bf16[4,64,256]{2,1,0:T(8,128)(2,1)S(1)} all-to-all(bf16[4,64,256]{2,1,0:T(8,128)(2,1)S(1)} %finish.1), channel_id=1, replica_groups=mesh['seq'=32,'head'=4,'user'=4] {'head'}, dimensions={0} | all-to-all | bytes 262144 | tf_op jit(solution)/shard_map/all_to_all | solution.py:312
  80.3 0.6 add.1
Async XLA Ops:
  2.5 22.0 %all-to-all-start = ((bf16[4,64,256]{2,1,0:T(8,128)(2,1)}), bf16[4,64,256]{2,1,0:T(8,128)(2,1)S(1)}, u32[]{:S(2)}, u32[]{:S(2)}) async-start(bf16[4,64,256]{2,1,0:T(8,128)(2,1)} %get-tuple-element.21), calls=%async_computation | async-start | bytes 262144 | tf_op jit(solution)/shard_map/all_to_all | solution.py:263
  11.7 20.0 %collective-permute-start = (bf16[2,1024,128]{2,1,0:T(8,128)(2,1)}, bf16[2,1024,128]{2,1,0:T(8,128)(2,1)S(1)}, u32[]{:S(2)}, u32[]{:S(2)}) collective-permute-start(bf16[2,1024,128]{2,1,0:T(8,128)(2,1)} %get-tuple-element.17), channel_id=1, source_target_pairs={{0,64},{16,80},{32,96},{48,112},{64,0},{80,16},{96,32},{112,48},{1... | collective-permute-start | bytes 1572872 | tf_op jit(solution)/shard_map/ppermute | solution.py:259
  13.7 18.4 %collective-permute-start.1 = (bf16[2,1024,128]{2,1,0:T(8,128)(2,1)}, bf16[2,1024,128]{2,1,0:T(8,128)(2,1)S(1)}, u32[]{:S(2)}, u32[]{:S(2)}) collective-permute-start(bf16[2,1024,128]{2,1,0:T(8,128)(2,1)} %get-tuple-element.18), channel_id=1, source_target_pairs={{0,448},{16,464},{32,480},{48,496},{64,128},{80,144},{96,160},{112... | collective-permute-start | bytes 1572872 | tf_op jit(solution)/shard_map/ppermute | solution.py:259
  20.8 17.2 %collective-permute-start.2 = (bf16[2,1024,128]{2,1,0:T(8,128)(2,1)}, bf16[2,1024,128]{2,1,0:T(8,128)(2,1)}, u32[]{:S(2)}, u32[]{:S(2)}) collective-permute-start(bf16[2,1024,128]{2,1,0:T(8,128)(2,1)} %get-tuple-element.19), channel_id=1, source_target_pairs={{0,16},{16,0},{32,48},{48,32},{64,80},{80,64},{96,112},{112,96},{1... | collective-permute-start | bytes 1572872 | tf_op jit(solution)/shard_map/ppermute | solution.py:259
  25.5 12.5 %copy-start.1 = (s32[2]{0:T(128)S(1)}, s32[2]{0:T(128)}, u32[]{:S(2)}) copy-start(s32[2]{0:T(128)} %length_ref.3) | copy-start | bytes 28
  25.6 18.1 %all-to-all-start.1 = ((bf16[32,32,128]{2,1,0:T(8,128)(2,1)}), bf16[32,32,128]{2,1,0:T(8,128)(2,1)S(1)}, u32[]{:S(2)}, u32[]{:S(2)}) async-start(bf16[32,32,128]{2,1,0:T(8,128)(2,1)} %get-tuple-element.23), calls=%async_computation.1 | async-start | bytes 524288 | tf_op jit(solution)/shard_map/all_to_all | solution.py:278
  31.8 6.2 %copy-start.2 = (bf16[2,1024,128]{2,1,0:T(8,128)(2,1)}, bf16[2,1024,128]{2,1,0:T(8,128)(2,1)S(1)}, u32[]{:S(2)}) copy-start(bf16[2,1024,128]{2,1,0:T(8,128)(2,1)S(1)} %collective-permute-done.rest_0_) | copy-start | bytes 1572868
  32.1 5.9 %copy-start.3 = (bf16[2,1024,128]{2,1,0:T(8,128)(2,1)}, bf16[2,1024,128]{2,1,0:T(8,128)(2,1)S(1)}, u32[]{:S(2)}) copy-start(bf16[2,1024,128]{2,1,0:T(8,128)(2,1)S(1)} %collective-permute-done.1.rest_1_) | copy-start | bytes 1572868
  52.7 17.5 %copy-start = (bf16[256,1024]{1,0:T(8,128)(2,1)S(1)}, bf16[256,1024]{1,0:T(8,128)(2,1)}, u32[]{:S(2)}) copy-start(bf16[256,1024]{1,0:T(8,128)(2,1)} %weight_ref.3) | copy-start | bytes 1572868

commit v10 on v9

--- a/solution.py
+++ b/solution.py
@@ -26,7 +26,7 @@
 def source(place, index, owners):
     if index == 0:
         return place
-    if index == 3:
+    if index == 2:
         return place + 1 - 2 * (place % 2)
     step = 4 - 8 * ((place // 4) % 2)
     return (place + (step if index == 1 else -step) + owners) % owners

time: 81.4 us -> 83.2 us (1.022)
  blocking collectives: 26.6 us -> 28.4 us
    all_to_all x1, waiting for transfers between devices: 2.89 us -> 0.96 us  [local(): queries = lax.all_to_all(queries, 'seq', 0, 0, tiled=True)]
    ppermute x3, waiting for transfers between devices: 6.22 us -> 8.13 us  [local(): lax.ppermute(share, 'seq', [(s, source(s, index + 1, owners)) for s in ra...]
    all_to_all x1, blocking collectives: 17.5 us -> 19.3 us  [local(): totals = lax.all_to_all(totals, 'seq', 0, 0, tiled=True)]
  transfers between devices with their start and end apart: 5 -> 5, of which waited for: 3 -> 2; matrix products, arithmetic and copies ran while one was open for 0% -> 0% of each run, Pallas kernels for 5% -> 5%
where the time goes in v10:
time: 83.2 us; the launch traced here: 82.7 us
  blocking collectives  28.4 us (34%)
  starting transfers between devices  27.9 us (34%)
  Pallas kernels  17 us (20%)
  waiting for transfers between devices  9.1 us (11%)
    all_to_all x1, blocking collectives, local(): totals = lax.all_to_all(totals, 'seq', 0, 0, tiled=True)  19.3 us
    ppermute x3, starting transfers between devices, local(): lax.ppermute(share, 'seq', [(s, source(s, index + 1, owners)) for s in ra...  12.5 us
    all_to_all x1, starting transfers between devices, local(): cand_parts = lax.all_to_all(copies, 'head', 0, 0, tiled=True)  9.21 us
    all_to_all x1, blocking collectives, local(): terms = lax.all_to_all(terms, 'head', 0, 0, tiled=True)  9.12 us
    pallas_call x1, Pallas kernels, local(): pl.pallas_call(functools.partial(attend_kernel, 1024, 256), out_shape=jax...  9.02 us
    ppermute x3, waiting for transfers between devices, local(): lax.ppermute(share, 'seq', [(s, source(s, index + 1, owners)) for s in ra...  8.13 us
    all_to_all x1, starting transfers between devices, local(): queries = lax.all_to_all(queries, 'seq', 0, 0, tiled=True)  6.2 us
    pallas_call x1, Pallas kernels, local(): pl.pallas_call(functools.partial(prepare_kernel, owners), out_shape=(jax....  2.78 us
  transfers between devices with their start and end apart: 5, of which 2 were waited for; matrix products, arithmetic and copies ran while one was open for 0% of the time, Pallas kernels for 5%

profile of v10, /device:TPU:2, one launch (start us, length us, event | category | flops | bytes accessed | tf_op | source)
XLA Modules:
  0.0 82.7 jit_solution(9859052208932370782)
XLA Ops:
  0.0 2.5 %share.1 = (bf16[2,1024,128]{2,1,0:T(8,128)(2,1)}, bf16[2,1024,128]{2,1,0:T(8,128)(2,1)}, bf16[2,1024,128]{2,1,0:T(8,128)(2,1)}, bf16[4,64,256]{2,1,0:T(8,128)(2...) custom-call(s32[1]{0:T(128)} %bitcast.place_ref, s32[1,64]{1,0:T(1,128)} %bitcast.6, ...), custom_call_target="tpu_custom_call" | custom-call | tf_op jit(solution)/shard_map/share/pallas_call | solution.py:237
  2.5 9.2 %all-to-all-start = ((bf16[4,64,256]{2,1,0:T(8,128)(2,1)}), bf16[4,64,256]{2,1,0:T(8,128)(2,1)S(1)}, u32[]{:S(2)}, u32[]{:S(2)}) async-start(bf16[4,64,256]{2,1,0:T(8,128)(2,1)} %get-tuple-element.21), calls=%async_computation | async-start | bytes 262144 | tf_op jit(solution)/shard_map/all_to_all | solution.py:263
  11.7 1.9 %collective-permute-start = (bf16[2,1024,128]{2,1,0:T(8,128)(2,1)}, bf16[2,1024,128]{2,1,0:T(8,128)(2,1)S(1)}, u32[]{:S(2)}, u32[]{:S(2)}) collective-permute-start(bf16[2,1024,128]{2,1,0:T(8,128)(2,1)} %get-tuple-element.17), channel_id=1, source_target_pairs={{0,64},{16,80},{32,96},{48,112},{64,0},{80,16},{96,32},{112,48},{1... | collective-permute-start | bytes 1572872 | tf_op jit(solution)/shard_map/ppermute | solution.py:259
  13.7 1.9 %collective-permute-start.1 = (bf16[2,1024,128]{2,1,0:T(8,128)(2,1)}, bf16[2,1024,128]{2,1,0:T(8,128)(2,1)S(1)}, u32[]{:S(2)}, u32[]{:S(2)}) collective-permute-start(bf16[2,1024,128]{2,1,0:T(8,128)(2,1)} %get-tuple-element.18), channel_id=1, source_target_pairs={{0,16},{16,0},{32,48},{48,32},{64,80},{80,64},{96,112},{112,96},{1... | collective-permute-start | bytes 1572872 | tf_op jit(solution)/shard_map/ppermute | solution.py:259
  15.6 8.7 %collective-permute-start.2 = (bf16[2,1024,128]{2,1,0:T(8,128)(2,1)}, bf16[2,1024,128]{2,1,0:T(8,128)(2,1)}, u32[]{:S(2)}, u32[]{:S(2)}) collective-permute-start(bf16[2,1024,128]{2,1,0:T(8,128)(2,1)} %get-tuple-element.19), channel_id=1, source_target_pairs={{0,448},{16,464},{32,480},{48,496},{64,128},{80,144},{96,160},{112... | collective-permute-start | bytes 1572872 | tf_op jit(solution)/shard_map/ppermute | solution.py:259
  24.3 0.2 copy.8
  24.5 0.0 all-to-all-done.cand_ref
  24.5 1.0 %project.1 = (bf16[32,32,128]{2,1,0:T(8,128)(2,1)}, bf16[64,256]{1,0:T(8,128)(2,1)S(1)}) custom-call(bf16[4,64,256]{2,1,0:T(8,128)(2,1)S(1)} %all-to-all-done.cand_ref, bf16[1024,512]{1,0:T(8,128)(2,1)S(1)} %bitcast.4), custom_call_target="tpu_custom_call" | custom-call | tf_op jit(solution)/shard_map/project/pallas_call | solution.py:264
  25.5 0.0 copy-start.1
  25.5 6.2 %all-to-all-start.1 = ((bf16[32,32,128]{2,1,0:T(8,128)(2,1)}), bf16[32,32,128]{2,1,0:T(8,128)(2,1)S(1)}, u32[]{:S(2)}, u32[]{:S(2)}) async-start(bf16[32,32,128]{2,1,0:T(8,128)(2,1)} %get-tuple-element.23), calls=%async_computation.1 | async-start | bytes 524288 | tf_op jit(solution)/shard_map/all_to_all | solution.py:278
  31.8 0.0 collective-permute-done.rest_0_
  31.8 0.0 copy-start.2
  31.8 0.0 collective-permute-done.1.rest_1_
  31.8 0.0 copy-start.3
  31.8 8.1 %collective-permute-done.2.rest_2_ = bf16[2,1024,128]{2,1,0:T(8,128)(2,1)} collective-permute-done((bf16[2,1024,128]{2,1,0:T(8,128)(2,1)}, bf16[2,1024,128]{2,1,0:T(8,128)(2,1)}, u32[]{:S(2)}, u32[]{:S(2)}) %collective-permute-start.2) | collective-permute-done | bytes 524320 | tf_op jit(solution)/shard_map/ppermute | solution.py:259
  39.9 0.0 copy-done.2
  39.9 0.0 copy-done.3
  39.9 0.0 copy-done.1
  39.9 2.8 %prepare.1 = (bf16[128,4096]{1,0:T(8,128)(2,1)S(1)}, bf16[4096,128]{1,0:T(8,128)(2,1)S(1)}, bf16[64,64]{1,0:T(8,128)(2,1)S(1)}) custom-call(s32[1]{0:T(128)} %bitcast.place_ref, s32[2]{0:T(128)S(1)} %copy-done.1, s32[1,64]{1,0:T(1,128)} %bitcast.7, bf16[2,1024,256]{2,1,0:T(8,128)(2,1)} %key_ref.3, bf16[2,1024,256]{2,1,0:T(8,128)(2,1)} %value_ref.3, ...), custom_call_target="tpu_custom_call" | custom-call | tf_op jit(solution)/shard_map/prepare/pallas_call | solution.py:279
  42.7 1.0 %all-to-all-done.1.query_ref = bf16[32,32,128]{2,1,0:T(8,128)(2,1)S(1)} async-done(((bf16[32,32,128]{2,1,0:T(8,128)(2,1)}), bf16[32,32,128]{2,1,0:T(8,128)(2,1)S(1)}, u32[]{:S(2)}, u32[]{:S(2)}) %all-to-all-start.1) | async-done | bytes 262176 | tf_op jit(solution)/shard_map/all_to_all | solution.py:278
  43.7 9.0 %attend.1 = bf16[32,32,128]{2,1,0:T(8,128)(2,1)S(1)} custom-call(bf16[32,32,128]{2,1,0:T(8,128)(2,1)S(1)} %all-to-all-done.1.query_ref, bf16[128,4096]{1,0:T(8,128)(2,1)S(1)} %get-tuple-element.24.keys, bf16[4096,128]{1,0:T(8,128)(2,1)S(1)} %get-tuple-element.25.values), custom_call_target="tpu_custom_call" | custom-call | tf_op jit(solution)/shard_map/attend/pallas_call | solution.py:295
  52.7 0.0 copy-start
  52.7 19.3 %all_to_all.20.partial_ref = bf16[32,32,128]{2,1,0:T(8,128)(2,1)S(1)} all-to-all(bf16[32,32,128]{2,1,0:T(8,128)(2,1)S(1)} %attend.1), channel_id=1, replica_groups=mesh['seq'=32,'head'=4,'user'=4] {'seq'}, dimensions={0} | all-to-all | bytes 524288 | tf_op jit(solution)/shard_map/all_to_all | solution.py:303
  72.0 0.0 copy-done
  72.0 1.0 %finish.1 = bf16[4,64,256]{2,1,0:T(8,128)(2,1)S(1)} custom-call(s32[2]{0:T(128)S(1)} %copy-done.1, bf16[64,64]{1,0:T(8,128)(2,1)S(1)} %get-tuple-element.20.back_ref, bf16[32,32,128]{2,1,0:T(8,128)(2,1)S(1)} %all_to_all.20.partial_ref, bf16[64,256]{1,0:T(8,128)(2,1)S(1)} %get-tuple-element.26.gate_ref, bf16[256,1024]{1,0:T(8,128)(2,1)S(1)} %copy-done), custom_call_target="tpu_custom_call" | custom-call | tf_op jit(solution)/shard_map/finish/pallas_call | solution.py:304
  73.0 9.1 %all_to_all.21.term_ref = bf16[4,64,256]{2,1,0:T(8,128)(2,1)S(1)} all-to-all(bf16[4,64,256]{2,1,0:T(8,128)(2,1)S(1)} %finish.1), channel_id=1, replica_groups=mesh['seq'=32,'head'=4,'user'=4] {'head'}, dimensions={0} | all-to-all | bytes 262144 | tf_op jit(solution)/shard_map/all_to_all | solution.py:312
  82.1 0.6 add.1
Async XLA Ops:
  2.5 22.0 %all-to-all-start = ((bf16[4,64,256]{2,1,0:T(8,128)(2,1)}), bf16[4,64,256]{2,1,0:T(8,128)(2,1)S(1)}, u32[]{:S(2)}, u32[]{:S(2)}) async-start(bf16[4,64,256]{2,1,0:T(8,128)(2,1)} %get-tuple-element.21), calls=%async_computation | async-start | bytes 262144 | tf_op jit(solution)/shard_map/all_to_all | solution.py:263
  11.7 20.0 %collective-permute-start = (bf16[2,1024,128]{2,1,0:T(8,128)(2,1)}, bf16[2,1024,128]{2,1,0:T(8,128)(2,1)S(1)}, u32[]{:S(2)}, u32[]{:S(2)}) collective-permute-start(bf16[2,1024,128]{2,1,0:T(8,128)(2,1)} %get-tuple-element.17), channel_id=1, source_target_pairs={{0,64},{16,80},{32,96},{48,112},{64,0},{80,16},{96,32},{112,48},{1... | collective-permute-start | bytes 1572872 | tf_op jit(solution)/shard_map/ppermute | solution.py:259
  13.7 18.1 %collective-permute-start.1 = (bf16[2,1024,128]{2,1,0:T(8,128)(2,1)}, bf16[2,1024,128]{2,1,0:T(8,128)(2,1)S(1)}, u32[]{:S(2)}, u32[]{:S(2)}) collective-permute-start(bf16[2,1024,128]{2,1,0:T(8,128)(2,1)} %get-tuple-element.18), channel_id=1, source_target_pairs={{0,16},{16,0},{32,48},{48,32},{64,80},{80,64},{96,112},{112,96},{1... | collective-permute-start | bytes 1572872 | tf_op jit(solution)/shard_map/ppermute | solution.py:259
  15.6 24.3 %collective-permute-start.2 = (bf16[2,1024,128]{2,1,0:T(8,128)(2,1)}, bf16[2,1024,128]{2,1,0:T(8,128)(2,1)}, u32[]{:S(2)}, u32[]{:S(2)}) collective-permute-start(bf16[2,1024,128]{2,1,0:T(8,128)(2,1)} %get-tuple-element.19), channel_id=1, source_target_pairs={{0,448},{16,464},{32,480},{48,496},{64,128},{80,144},{96,160},{112... | collective-permute-start | bytes 1572872 | tf_op jit(solution)/shard_map/ppermute | solution.py:259
  25.5 14.4 %copy-start.1 = (s32[2]{0:T(128)S(1)}, s32[2]{0:T(128)}, u32[]{:S(2)}) copy-start(s32[2]{0:T(128)} %length_ref.3) | copy-start | bytes 28
  25.5 18.1 %all-to-all-start.1 = ((bf16[32,32,128]{2,1,0:T(8,128)(2,1)}), bf16[32,32,128]{2,1,0:T(8,128)(2,1)S(1)}, u32[]{:S(2)}, u32[]{:S(2)}) async-start(bf16[32,32,128]{2,1,0:T(8,128)(2,1)} %get-tuple-element.23), calls=%async_computation.1 | async-start | bytes 524288 | tf_op jit(solution)/shard_map/all_to_all | solution.py:278
  31.8 8.2 %copy-start.2 = (bf16[2,1024,128]{2,1,0:T(8,128)(2,1)}, bf16[2,1024,128]{2,1,0:T(8,128)(2,1)S(1)}, u32[]{:S(2)}) copy-start(bf16[2,1024,128]{2,1,0:T(8,128)(2,1)S(1)} %collective-permute-done.rest_0_) | copy-start | bytes 1572868
  31.8 8.1 %copy-start.3 = (bf16[2,1024,128]{2,1,0:T(8,128)(2,1)}, bf16[2,1024,128]{2,1,0:T(8,128)(2,1)S(1)}, u32[]{:S(2)}) copy-start(bf16[2,1024,128]{2,1,0:T(8,128)(2,1)S(1)} %collective-permute-done.1.rest_1_) | copy-start | bytes 1572868
  52.7 19.3 %copy-start = (bf16[256,1024]{1,0:T(8,128)(2,1)S(1)}, bf16[256,1024]{1,0:T(8,128)(2,1)}, u32[]{:S(2)}) copy-start(bf16[256,1024]{1,0:T(8,128)(2,1)} %weight_ref.3) | copy-start | bytes 1572868

commit v11 on v9

--- a/solution.py
+++ b/solution.py
@@ -21,6 +21,10 @@
 
 def role(place):
     return (place // 4) % 2, (place // 8 + place) % 2
+
+
+def half_of(member):
+    return (member // 4 + member) % 2
 
 
 def source(place, index, owners):
@@ -52,12 +56,14 @@
 
 
 def project_kernel(cand_ref, weight_ref, query_ref, gate_ref):
-    slices, rows, depth = cand_ref.shape
+    members, share_rows, depth = cand_ref.shape
+    slices = members // USERS
+    rows = USERS * share_rows
     width = weight_ref.shape[1] // 2
     total = jnp.zeros((rows, 2 * width), jnp.float32)
     for part in range(slices):
         total += jnp.dot(
-            cand_ref[part],
+            jnp.concatenate([cand_ref[part], cand_ref[slices + part]], axis=0),
             weight_ref[part * depth : (part + 1) * depth, :],
             preferred_element_type=jnp.float32,
         )
@@ -65,12 +71,10 @@
     query = (projected[:, :width].astype(jnp.float32) * (0.5 * HEAD_DIM**-0.5)).astype(
         jnp.bfloat16
     )
-    _, block_rows, lanes = query_ref.shape
-    for owner in range(query_ref.shape[0]):
-        user, half = role(owner)
-        query_ref[owner] = query[
-            user * block_rows : (user + 1) * block_rows, half * lanes : (half + 1) * lanes
-        ]
+    lanes = query_ref.shape[2]
+    for member in range(query_ref.shape[0]):
+        half = half_of(member)
+        query_ref[member] = query[:, half * lanes : (half + 1) * lanes]
     gate_ref[...] = projected[:, width:]
 
 
@@ -109,8 +113,11 @@
         rows.dtype
     )
     out = []
-    for group in range(copy_ref.shape[0]):
-        out.append(pltpu.make_async_copy(rows, copy_ref.at[group], copy_sems.at[group]))
+    members, share_rows, _ = copy_ref.shape
+    for member in range(members):
+        user = member // (members // USERS)
+        mine = rows.at[user * share_rows : (user + 1) * share_rows]
+        out.append(pltpu.make_async_copy(mine, copy_ref.at[member], copy_sems.at[member]))
         out[-1].start()
     for index, out_ref in enumerate(out_refs):
         for kind in range(2):
@@ -183,18 +190,16 @@
     lax.fori_loop(0, blocks // step_blocks, step, 0)
 
 
-def finish_kernel(length_ref, back_ref, partial_ref, gate_ref, weight_ref, out_ref):
+def finish_kernel(place_ref, length_ref, partial_ref, gate_ref, weight_ref, out_ref):
     rows, width = gate_ref.shape
     sums = {}
-    for block in range(partial_ref.shape[0]):
-        term = partial_ref[block].astype(jnp.float32)
-        sums[role(block)] = sums[role(block)] + term if role(block) in sums else term
-    total = jnp.concatenate(
-        [jnp.concatenate([sums[user, half] for half in range(2)], axis=1) for user in range(USERS)],
-        axis=0,
-    )
-    row = lax.broadcasted_iota(jnp.int32, (rows, width), 0)
-    length = jnp.where(row < rows // USERS, length_ref[0], length_ref[1]).astype(jnp.float32)
+    for member in range(partial_ref.shape[0]):
+        term = partial_ref[member].astype(jnp.float32)
+        half = half_of(member)
+        sums[half] = sums[half] + term if half in sums else term
+    total = jnp.concatenate([sums[0], sums[1]], axis=1)
+    user, _ = role(place_ref[0])
+    length = jnp.full((rows, width), length_ref[user], jnp.int32).astype(jnp.float32)
     attn = total / length
     square = attn * attn
     mean = jnp.zeros((rows, width), jnp.float32)
@@ -204,19 +209,24 @@
         mean = jnp.where(mask, summed * (1.0 / HEAD_DIM), mean)
     normed = attn * lax.rsqrt(mean + 1e-06)
     gated = (normed * gate_ref[...].astype(jnp.float32)).astype(jnp.bfloat16)
-    gated = jnp.dot(back_ref[...], gated, preferred_element_type=jnp.float32).astype(jnp.bfloat16)
-    for part in range(out_ref.shape[0]):
-        out_ref[part] = jnp.dot(
+    members, share_rows, depth = out_ref.shape
+    slices = members // USERS
+    for part in range(slices):
+        term = jnp.dot(
             gated,
-            weight_ref[:, part * width : (part + 1) * width],
+            weight_ref[:, part * depth : (part + 1) * depth],
             preferred_element_type=jnp.float32,
         ).astype(out_ref.dtype)
-
-
-def add_kernel(cand_ref, term_ref, out_ref):
+        for block in range(USERS):
+            out_ref[block * slices + part] = term[block * share_rows : (block + 1) * share_rows]
+
+
+def add_kernel(cand_ref, back_ref, term_ref, out_ref):
+    slices = term_ref.shape[0] // USERS
     total = cand_ref[...].astype(jnp.float32)
-    for group in range(term_ref.shape[0]):
-        total += term_ref[group].astype(jnp.float32)
+    for part in range(slices):
+        term = jnp.concatenate([term_ref[part], term_ref[slices + part]], axis=0)
+        total += jnp.dot(back_ref[...], term, preferred_element_type=jnp.float32)
     out_ref[...] = total.astype(out_ref.dtype)
 
 
@@ -238,7 +248,7 @@
         functools.partial(share_kernel, owners),
         out_shape=[pltpu.HBM((2, positions, lanes), jnp.bfloat16)] * (SOURCES - 1)
         + [
-            pltpu.HBM((groups, rows, depth), jnp.bfloat16),
+            pltpu.HBM((USERS * groups, block_rows, depth), jnp.bfloat16),
             pltpu.VMEM((rows, depth), jnp.bfloat16),
             pltpu.VMEM(qu_weight.shape, jnp.bfloat16),
         ],
@@ -249,7 +259,7 @@
             pltpu.VMEM((rows, depth), jnp.bfloat16),
             pltpu.VMEM((SOURCES - 1, 2, positions, lanes), jnp.bfloat16),
             pltpu.SemaphoreType.DMA((SOURCES - 1, 2)),
-            pltpu.SemaphoreType.DMA((groups,)),
+            pltpu.SemaphoreType.DMA((USERS * groups,)),
             pltpu.SemaphoreType.DMA((3,)),
         ],
         compiler_params=PARAMS,
@@ -260,11 +270,26 @@
         for index, share in enumerate(shares)
     ]
 
-    cand_parts = lax.all_to_all(copies, "head", 0, 0, tiled=True)
+    pairs = [
+        [group * owners + first + 4 * user for user in range(USERS) for group in range(groups)]
+        for first in range(owners)
+        if role(first)[0] == 0
+    ]
+    of_user = [[s for s in range(owners) if role(s)[0] == user] for user in range(USERS)]
+
+    def over_pair(array):
+        return lax.all_to_all(
+            array, ("head", "seq"), 0, 0, tiled=True, axis_index_groups=pairs
+        )
+
+    def over_user(array):
+        return lax.all_to_all(array, "seq", 0, 0, tiled=True, axis_index_groups=of_user)
+
+    cand_parts = over_pair(copies)
     queries, gates = pl.pallas_call(
         project_kernel,
         out_shape=(
-            jax.ShapeDtypeStruct((owners, block_rows, lanes), jnp.bfloat16),
+            jax.ShapeDtypeStruct((owners // USERS, rows, lanes), jnp.bfloat16),
             jax.ShapeDtypeStruct((rows, width), jnp.bfloat16),
         ),
         in_specs=[VMEM] * 2,
@@ -275,7 +300,7 @@
         cand_parts,
         weight.reshape(qu_weight.shape[0], 2 * width),
     )
-    queries = lax.all_to_all(queries, "seq", 0, 0, tiled=True)
+    queries = over_user(queries)
     turned, live, back = pl.pallas_call(
         functools.partial(prepare_kernel, owners),
         out_shape=(
@@ -294,30 +319,29 @@
     )(place, lengths, *map(in_hbm, (users, keys, values, *history)))
     totals = pl.pallas_call(
         functools.partial(attend_kernel, 1024, 256),
-        out_shape=jax.ShapeDtypeStruct((owners, block_rows, lanes), jnp.bfloat16),
+        out_shape=jax.ShapeDtypeStruct((owners // USERS, rows, lanes), jnp.bfloat16),
         in_specs=[VMEM] * 3,
         out_specs=VMEM,
         compiler_params=ATTEND_PARAMS,
         name="attend",
     )(queries, turned, live)
-    totals = lax.all_to_all(totals, "seq", 0, 0, tiled=True)
+    totals = over_user(totals)
     terms = pl.pallas_call(
         finish_kernel,
-        out_shape=jax.ShapeDtypeStruct((groups, rows, depth), jnp.bfloat16),
-        in_specs=[SMEM] + [VMEM] * 4,
+        out_shape=jax.ShapeDtypeStruct((USERS * groups, block_rows, depth), jnp.bfloat16),
+        in_specs=[SMEM] * 2 + [VMEM] * 3,
         out_specs=VMEM,
         compiler_params=PARAMS,
         name="finish",
-    )(lengths, back, totals, gates, out_weight)
-    terms = lax.all_to_all(terms, "head", 0, 0, tiled=True)
+    )(place, lengths, totals, gates, out_weight)
     return pl.pallas_call(
         add_kernel,
         out_shape=jax.ShapeDtypeStruct((rows, depth), cand_rows.dtype),
-        in_specs=[VMEM, VMEM],
+        in_specs=[VMEM] * 3,
         out_specs=VMEM,
         compiler_params=PARAMS,
         name="add",
-    )(kept, terms)
+    )(kept, back, over_pair(terms))
 
 
 def solution(mesh):

time: 81.4 us -> 82.5 us (1.014)
  blocking collectives: 26.6 us -> 28.9 us
    all_to_all x2, waiting for transfers between devices: 2.9 us -> 0.56 us  [the longest x1 0.56 us: over_user(): lax.all_to_all(array, 'seq', 0, 0, tiled=True, axis_index_groups=of_user)]
    all_to_all x2, blocking collectives: 26.6 us -> 28.9 us  [the longest x1 19.2 us: over_user(): lax.all_to_all(array, 'seq', 0, 0, tiled=True, axis_index_groups=of_user)]
    ppermute x3, waiting for transfers between devices: 6.22 us -> 8.13 us  [local(): lax.ppermute(share, 'seq', [(s, source(s, index + 1, owners)) for s in ra...]
    all_to_all x2, starting transfers between devices: 15.4 us -> 13.6 us  [the longest x1 9.19 us: over_pair(): lax.all_to_all(array, ('head', 'seq'), 0, 0, tiled=True, axis_index_group...]
    ppermute x3, starting transfers between devices: 12.5 us -> 13.4 us  [local(): lax.ppermute(share, 'seq', [(s, source(s, index + 1, owners)) for s in ra...]
where the time goes in v11:
time: 82.5 us; the launch traced here: 82 us
  blocking collectives  28.9 us (35%)
  starting transfers between devices  27.1 us (33%)
  Pallas kernels  17 us (21%)
  waiting for transfers between devices  8.69 us (11%)
    all_to_all x1, blocking collectives, over_user(): lax.all_to_all(array, 'seq', 0, 0, tiled=True, axis_index_groups=of_user)  19.2 us
    ppermute x3, starting transfers between devices, local(): lax.ppermute(share, 'seq', [(s, source(s, index + 1, owners)) for s in ra...  13.4 us
    all_to_all x1, blocking collectives, over_pair(): lax.all_to_all(array, ('head', 'seq'), 0, 0, tiled=True, axis_index_group...  9.67 us
    all_to_all x1, starting transfers between devices, over_pair(): lax.all_to_all(array, ('head', 'seq'), 0, 0, tiled=True, axis_index_group...  9.19 us
    pallas_call x1, Pallas kernels, local(): pl.pallas_call(functools.partial(attend_kernel, 1024, 256), out_shape=jax...  9.02 us
    ppermute x3, waiting for transfers between devices, local(): lax.ppermute(share, 'seq', [(s, source(s, index + 1, owners)) for s in ra...  8.13 us
    all_to_all x1, starting transfers between devices, over_user(): lax.all_to_all(array, 'seq', 0, 0, tiled=True, axis_index_groups=of_user)  4.45 us
    pallas_call x1, Pallas kernels, local(): pl.pallas_call(functools.partial(prepare_kernel, owners), out_shape=(jax....  2.79 us
  transfers between devices with their start and end apart: 5, of which 3 were waited for; matrix products, arithmetic and copies ran while one was open for 0% of the time, Pallas kernels for 5%

profile of v11, /device:TPU:2, one launch (start us, length us, event | category | flops | bytes accessed | tf_op | source)
XLA Modules:
  0.0 82.0 jit_solution(7638166208031645759)
XLA Ops:
  0.0 2.6 %share.1 = (bf16[2,1024,128]{2,1,0:T(8,128)(2,1)}, bf16[2,1024,128]{2,1,0:T(8,128)(2,1)}, bf16[2,1024,128]{2,1,0:T(8,128)(2,1)}, bf16[8,32,256]{2,1,0:T(8,128)(2...) custom-call(s32[1]{0:T(128)} %bitcast.place_ref, s32[1,64]{1,0:T(1,128)} %bitcast.6, ...), custom_call_target="tpu_custom_call" | custom-call | tf_op jit(solution)/shard_map/share/pallas_call | solution.py:247
  2.6 9.2 %all-to-all-start = ((bf16[8,32,256]{2,1,0:T(8,128)(2,1)}), bf16[8,32,256]{2,1,0:T(8,128)(2,1)S(1)}, u32[]{:S(2)}, u32[]{:S(2)}) async-start(bf16[8,32,256]{2,1,0:T(8,128)(2,1)} %get-tuple-element.21), calls=%async_computation | async-start | bytes 262144 | tf_op jit(solution)/shard_map/all_to_all | solution.py:281
  11.8 3.4 %collective-permute-start = (bf16[2,1024,128]{2,1,0:T(8,128)(2,1)}, bf16[2,1024,128]{2,1,0:T(8,128)(2,1)S(1)}, u32[]{:S(2)}, u32[]{:S(2)}) collective-permute-start(bf16[2,1024,128]{2,1,0:T(8,128)(2,1)} %get-tuple-element.17), channel_id=1, source_target_pairs={{0,64},{16,80},{32,96},{48,112},{64,0},{80,16},{96,32},{112,48},{1... | collective-permute-start | bytes 1572872 | tf_op jit(solution)/shard_map/ppermute | solution.py:269
  15.2 6.6 %collective-permute-start.1 = (bf16[2,1024,128]{2,1,0:T(8,128)(2,1)}, bf16[2,1024,128]{2,1,0:T(8,128)(2,1)S(1)}, u32[]{:S(2)}, u32[]{:S(2)}) collective-permute-start(bf16[2,1024,128]{2,1,0:T(8,128)(2,1)} %get-tuple-element.18), channel_id=1, source_target_pairs={{0,448},{16,464},{32,480},{48,496},{64,128},{80,144},{96,160},{112... | collective-permute-start | bytes 1572872 | tf_op jit(solution)/shard_map/ppermute | solution.py:269
  21.7 3.5 %collective-permute-start.2 = (bf16[2,1024,128]{2,1,0:T(8,128)(2,1)}, bf16[2,1024,128]{2,1,0:T(8,128)(2,1)}, u32[]{:S(2)}, u32[]{:S(2)}) collective-permute-start(bf16[2,1024,128]{2,1,0:T(8,128)(2,1)} %get-tuple-element.19), channel_id=1, source_target_pairs={{0,16},{16,0},{32,48},{48,32},{64,80},{80,64},{96,112},{112,96},{1... | collective-permute-start | bytes 1572872 | tf_op jit(solution)/shard_map/ppermute | solution.py:269
  25.2 0.2 copy.8
  25.5 0.0 all-to-all-done.cand_ref
  25.5 1.0 %project.1 = (bf16[16,64,128]{2,1,0:T(8,128)(2,1)}, bf16[64,256]{1,0:T(8,128)(2,1)S(1)}) custom-call(bf16[8,32,256]{2,1,0:T(8,128)(2,1)S(1)} %all-to-all-done.cand_ref, bf16[1024,512]{1,0:T(8,128)(2,1)S(1)} %bitcast.4), custom_call_target="tpu_custom_call" | custom-call | tf_op jit(solution)/shard_map/project/pallas_call | solution.py:289
  26.5 0.0 copy-start.1
  26.5 4.5 %all-to-all-start.1 = ((bf16[16,64,128]{2,1,0:T(8,128)(2,1)}), bf16[16,64,128]{2,1,0:T(8,128)(2,1)S(1)}, u32[]{:S(2)}, u32[]{:S(2)}) async-start(bf16[16,64,128]{2,1,0:T(8,128)(2,1)} %get-tuple-element.23), calls=%async_computation.1 | async-start | bytes 524288 | tf_op jit(solution)/shard_map/all_to_all | solution.py:286
  31.0 0.0 collective-permute-done.rest_0_
  31.0 0.0 copy-start.2
  31.0 2.1 %collective-permute-done.1.rest_1_ = bf16[2,1024,128]{2,1,0:T(8,128)(2,1)S(1)} collective-permute-done((bf16[2,1024,128]{2,1,0:T(8,128)(2,1)}, bf16[2,1024,128]{2,1,0:T(8,128)(2,1)S(1)}, u32[]{:S(2)}, u32[]{:S(2)}) %collective-permute-start.1) | collective-permute-done | bytes 524320 | tf_op jit(solution)/shard_map/ppermute | solution.py:269
  33.1 0.0 copy-start.3
  33.1 6.0 %collective-permute-done.2.rest_2_ = bf16[2,1024,128]{2,1,0:T(8,128)(2,1)} collective-permute-done((bf16[2,1024,128]{2,1,0:T(8,128)(2,1)}, bf16[2,1024,128]{2,1,0:T(8,128)(2,1)}, u32[]{:S(2)}, u32[]{:S(2)}) %collective-permute-start.2) | collective-permute-done | bytes 524320 | tf_op jit(solution)/shard_map/ppermute | solution.py:269
  39.1 0.0 copy-done.2
  39.1 0.0 copy-done.3
  39.1 0.0 copy-done.1
  39.1 2.8 %prepare.1 = (bf16[128,4096]{1,0:T(8,128)(2,1)S(1)}, bf16[4096,128]{1,0:T(8,128)(2,1)S(1)}, bf16[64,64]{1,0:T(8,128)(2,1)S(1)}) custom-call(s32[1]{0:T(128)} %bitcast.place_ref, s32[2]{0:T(128)S(1)} %copy-done.1, s32[1,64]{1,0:T(1,128)} %bitcast.7, bf16[2,1024,256]{2,1,0:T(8,128)(2,1)} %key_ref.3, bf16[2,1024,256]{2,1,0:T(8,128)(2,1)} %value_ref.3, ...), custom_call_target="tpu_custom_call" | custom-call | tf_op jit(solution)/shard_map/prepare/pallas_call | solution.py:304
  41.9 0.6 all-to-all-done.1.query_ref
  42.5 9.0 %attend.1 = bf16[16,64,128]{2,1,0:T(8,128)(2,1)S(1)} custom-call(bf16[16,64,128]{2,1,0:T(8,128)(2,1)S(1)} %all-to-all-done.1.query_ref, bf16[128,4096]{1,0:T(8,128)(2,1)S(1)} %get-tuple-element.24.keys, bf16[4096,128]{1,0:T(8,128)(2,1)S(1)} %get-tuple-element.25.values), custom_call_target="tpu_custom_call" | custom-call | tf_op jit(solution)/shard_map/attend/pallas_call | solution.py:320
  51.5 0.0 copy-start
  51.5 19.2 %all_to_all.20.partial_ref = bf16[16,64,128]{2,1,0:T(8,128)(2,1)S(1)} all-to-all(bf16[16,64,128]{2,1,0:T(8,128)(2,1)S(1)} %attend.1), channel_id=1, replica_groups={{0,16,32,48,128,144,160,176,256,272,288,304,384,400,416,432},{64,80,96,..., dimensions={0} | all-to-all | bytes 524288 | tf_op jit(solution)/shard_map/all_to_all | solution.py:286
  70.7 0.0 copy-done
  70.8 0.8 %finish.1 = bf16[8,32,256]{2,1,0:T(8,128)(2,1)S(1)} custom-call(s32[1]{0:T(128)} %bitcast.place_ref, s32[2]{0:T(128)S(1)} %copy-done.1, bf16[16,64,128]{2,1,0:T(8,128)(2,1)S(1)} %all_to_all.20.partial_ref, bf16[64,256]{1,0:T(8,128)(2,1)S(1)} %get-tuple-element.26.gate_ref, bf16[256,1024]{1,0:T(8,128)(2,1)S(1)} %copy-done), custom_call_target="tpu_custom_call" | custom-call | tf_op jit(solution)/shard_map/finish/pallas_call | solution.py:329
  71.6 9.7 %all_to_all.21.term_ref = bf16[8,32,256]{2,1,0:T(8,128)(2,1)S(1)} all-to-all(bf16[8,32,256]{2,1,0:T(8,128)(2,1)S(1)} %finish.1), channel_id=1, replica_groups={{0,4,8,12,64,68,72,76},{16,20,24,28,80,84,88,92},{32,36,40,44,96,100,10..., dimensions={0} | all-to-all | bytes 262144 | tf_op jit(solution)/shard_map/all_to_all | solution.py:281
  81.2 0.8 add.1
Async XLA Ops:
  2.6 22.9 %all-to-all-start = ((bf16[8,32,256]{2,1,0:T(8,128)(2,1)}), bf16[8,32,256]{2,1,0:T(8,128)(2,1)S(1)}, u32[]{:S(2)}, u32[]{:S(2)}) async-start(bf16[8,32,256]{2,1,0:T(8,128)(2,1)} %get-tuple-element.21), calls=%async_computation | async-start | bytes 262144 | tf_op jit(solution)/shard_map/all_to_all | solution.py:281
  11.8 19.2 %collective-permute-start = (bf16[2,1024,128]{2,1,0:T(8,128)(2,1)}, bf16[2,1024,128]{2,1,0:T(8,128)(2,1)S(1)}, u32[]{:S(2)}, u32[]{:S(2)}) collective-permute-start(bf16[2,1024,128]{2,1,0:T(8,128)(2,1)} %get-tuple-element.17), channel_id=1, source_target_pairs={{0,64},{16,80},{32,96},{48,112},{64,0},{80,16},{96,32},{112,48},{1... | collective-permute-start | bytes 1572872 | tf_op jit(solution)/shard_map/ppermute | solution.py:269
  15.2 17.9 %collective-permute-start.1 = (bf16[2,1024,128]{2,1,0:T(8,128)(2,1)}, bf16[2,1024,128]{2,1,0:T(8,128)(2,1)S(1)}, u32[]{:S(2)}, u32[]{:S(2)}) collective-permute-start(bf16[2,1024,128]{2,1,0:T(8,128)(2,1)} %get-tuple-element.18), channel_id=1, source_target_pairs={{0,448},{16,464},{32,480},{48,496},{64,128},{80,144},{96,160},{112... | collective-permute-start | bytes 1572872 | tf_op jit(solution)/shard_map/ppermute | solution.py:269
  21.7 17.4 %collective-permute-start.2 = (bf16[2,1024,128]{2,1,0:T(8,128)(2,1)}, bf16[2,1024,128]{2,1,0:T(8,128)(2,1)}, u32[]{:S(2)}, u32[]{:S(2)}) collective-permute-start(bf16[2,1024,128]{2,1,0:T(8,128)(2,1)} %get-tuple-element.19), channel_id=1, source_target_pairs={{0,16},{16,0},{32,48},{48,32},{64,80},{80,64},{96,112},{112,96},{1... | collective-permute-start | bytes 1572872 | tf_op jit(solution)/shard_map/ppermute | solution.py:269
  26.5 12.6 %copy-start.1 = (s32[2]{0:T(128)S(1)}, s32[2]{0:T(128)}, u32[]{:S(2)}) copy-start(s32[2]{0:T(128)} %length_ref.3) | copy-start | bytes 28
  26.5 16.0 %all-to-all-start.1 = ((bf16[16,64,128]{2,1,0:T(8,128)(2,1)}), bf16[16,64,128]{2,1,0:T(8,128)(2,1)S(1)}, u32[]{:S(2)}, u32[]{:S(2)}) async-start(bf16[16,64,128]{2,1,0:T(8,128)(2,1)} %get-tuple-element.23), calls=%async_computation.1 | async-start | bytes 524288 | tf_op jit(solution)/shard_map/all_to_all | solution.py:286
  31.0 8.1 %copy-start.2 = (bf16[2,1024,128]{2,1,0:T(8,128)(2,1)}, bf16[2,1024,128]{2,1,0:T(8,128)(2,1)S(1)}, u32[]{:S(2)}) copy-start(bf16[2,1024,128]{2,1,0:T(8,128)(2,1)S(1)} %collective-permute-done.rest_0_) | copy-start | bytes 1572868
  33.1 6.0 %copy-start.3 = (bf16[2,1024,128]{2,1,0:T(8,128)(2,1)}, bf16[2,1024,128]{2,1,0:T(8,128)(2,1)S(1)}, u32[]{:S(2)}) copy-start(bf16[2,1024,128]{2,1,0:T(8,128)(2,1)S(1)} %collective-permute-done.1.rest_1_) | copy-start | bytes 1572868
  51.5 19.2 %copy-start = (bf16[256,1024]{1,0:T(8,128)(2,1)S(1)}, bf16[256,1024]{1,0:T(8,128)(2,1)}, u32[]{:S(2)}) copy-start(bf16[256,1024]{1,0:T(8,128)(2,1)} %weight_ref.3) | copy-start | bytes 1572868

commit v12 on v9

--- a/solution.py
+++ b/solution.py
@@ -29,7 +29,7 @@
     if index == 3:
         return place + 1 - 2 * (place % 2)
     step = 4 - 8 * ((place // 4) % 2)
-    return (place + (step if index == 1 else -step) + owners) % owners
+    return (place + (step if index == 2 else -step) + owners) % owners
 
 
 def head_mask(shape, head):

time: 81.4 us -> 81.8 us (level)
  no operation moved by 1% of the time
where the time goes in v12:
time: 81.8 us; the launch traced here: 81.3 us
  starting transfers between devices  27.9 us (34%)
  blocking collectives  27 us (33%)
  Pallas kernels  17 us (21%)
  waiting for transfers between devices  9.06 us (11%)
    all_to_all x1, blocking collectives, local(): totals = lax.all_to_all(totals, 'seq', 0, 0, tiled=True)  17.9 us
    ppermute x3, starting transfers between devices, local(): lax.ppermute(share, 'seq', [(s, source(s, index + 1, owners)) for s in ra...  12 us
    all_to_all x1, starting transfers between devices, local(): cand_parts = lax.all_to_all(copies, 'head', 0, 0, tiled=True)  9.21 us
    all_to_all x1, blocking collectives, local(): terms = lax.all_to_all(terms, 'head', 0, 0, tiled=True)  9.12 us
    pallas_call x1, Pallas kernels, local(): pl.pallas_call(functools.partial(attend_kernel, 1024, 256), out_shape=jax...  9.02 us
    all_to_all x1, starting transfers between devices, local(): queries = lax.all_to_all(queries, 'seq', 0, 0, tiled=True)  6.72 us
    ppermute x3, waiting for transfers between devices, local(): lax.ppermute(share, 'seq', [(s, source(s, index + 1, owners)) for s in ra...  5.79 us
    all_to_all x1, waiting for transfers between devices, local(): queries = lax.all_to_all(queries, 'seq', 0, 0, tiled=True)  3.27 us
  transfers between devices with their start and end apart: 5, of which 3 were waited for; matrix products, arithmetic and copies ran while one was open for 0% of the time, Pallas kernels for 5%

profile of v12, /device:TPU:2, one launch (start us, length us, event | category | flops | bytes accessed | tf_op | source)
XLA Modules:
  0.0 81.3 jit_solution(18077437884549555476)
XLA Ops:
  0.0 2.5 %share.1 = (bf16[2,1024,128]{2,1,0:T(8,128)(2,1)}, bf16[2,1024,128]{2,1,0:T(8,128)(2,1)}, bf16[2,1024,128]{2,1,0:T(8,128)(2,1)}, bf16[4,64,256]{2,1,0:T(8,128)(2...) custom-call(s32[1]{0:T(128)} %bitcast.place_ref, s32[1,64]{1,0:T(1,128)} %bitcast.6, ...), custom_call_target="tpu_custom_call" | custom-call | tf_op jit(solution)/shard_map/share/pallas_call | solution.py:237
  2.5 9.2 %all-to-all-start = ((bf16[4,64,256]{2,1,0:T(8,128)(2,1)}), bf16[4,64,256]{2,1,0:T(8,128)(2,1)S(1)}, u32[]{:S(2)}, u32[]{:S(2)}) async-start(bf16[4,64,256]{2,1,0:T(8,128)(2,1)} %get-tuple-element.21), calls=%async_computation | async-start | bytes 262144 | tf_op jit(solution)/shard_map/all_to_all | solution.py:263
  11.7 6.6 %collective-permute-start = (bf16[2,1024,128]{2,1,0:T(8,128)(2,1)}, bf16[2,1024,128]{2,1,0:T(8,128)(2,1)S(1)}, u32[]{:S(2)}, u32[]{:S(2)}) collective-permute-start(bf16[2,1024,128]{2,1,0:T(8,128)(2,1)} %get-tuple-element.17), channel_id=1, source_target_pairs={{0,448},{16,464},{32,480},{48,496},{64,128},{80,144},{96,160},{112... | collective-permute-start | bytes 1572872 | tf_op jit(solution)/shard_map/ppermute | solution.py:259
  18.3 1.9 %collective-permute-start.1 = (bf16[2,1024,128]{2,1,0:T(8,128)(2,1)}, bf16[2,1024,128]{2,1,0:T(8,128)(2,1)S(1)}, u32[]{:S(2)}, u32[]{:S(2)}) collective-permute-start(bf16[2,1024,128]{2,1,0:T(8,128)(2,1)} %get-tuple-element.18), channel_id=1, source_target_pairs={{0,64},{16,80},{32,96},{48,112},{64,0},{80,16},{96,32},{112,48},{1... | collective-permute-start | bytes 1572872 | tf_op jit(solution)/shard_map/ppermute | solution.py:259
  20.2 3.5 %collective-permute-start.2 = (bf16[2,1024,128]{2,1,0:T(8,128)(2,1)}, bf16[2,1024,128]{2,1,0:T(8,128)(2,1)}, u32[]{:S(2)}, u32[]{:S(2)}) collective-permute-start(bf16[2,1024,128]{2,1,0:T(8,128)(2,1)} %get-tuple-element.19), channel_id=1, source_target_pairs={{0,16},{16,0},{32,48},{48,32},{64,80},{80,64},{96,112},{112,96},{1... | collective-permute-start | bytes 1572872 | tf_op jit(solution)/shard_map/ppermute | solution.py:259
  23.7 0.2 copy.8
  24.0 0.0 all-to-all-done.cand_ref
  24.0 1.0 %project.1 = (bf16[32,32,128]{2,1,0:T(8,128)(2,1)}, bf16[64,256]{1,0:T(8,128)(2,1)S(1)}) custom-call(bf16[4,64,256]{2,1,0:T(8,128)(2,1)S(1)} %all-to-all-done.cand_ref, bf16[1024,512]{1,0:T(8,128)(2,1)S(1)} %bitcast.4), custom_call_target="tpu_custom_call" | custom-call | tf_op jit(solution)/shard_map/project/pallas_call | solution.py:264
  25.0 0.0 copy-start.1
  25.0 6.7 %all-to-all-start.1 = ((bf16[32,32,128]{2,1,0:T(8,128)(2,1)}), bf16[32,32,128]{2,1,0:T(8,128)(2,1)S(1)}, u32[]{:S(2)}, u32[]{:S(2)}) async-start(bf16[32,32,128]{2,1,0:T(8,128)(2,1)} %get-tuple-element.23), calls=%async_computation.1 | async-start | bytes 524288 | tf_op jit(solution)/shard_map/all_to_all | solution.py:278
  31.7 0.0 collective-permute-done.rest_0_
  31.8 0.0 copy-start.2
  31.8 2.0 %collective-permute-done.1.rest_1_ = bf16[2,1024,128]{2,1,0:T(8,128)(2,1)S(1)} collective-permute-done((bf16[2,1024,128]{2,1,0:T(8,128)(2,1)}, bf16[2,1024,128]{2,1,0:T(8,128)(2,1)S(1)}, u32[]{:S(2)}, u32[]{:S(2)}) %collective-permute-start.1) | collective-permute-done | bytes 524320 | tf_op jit(solution)/shard_map/ppermute | solution.py:259
  33.8 0.0 copy-start.3
  33.8 3.8 %collective-permute-done.2.rest_2_ = bf16[2,1024,128]{2,1,0:T(8,128)(2,1)} collective-permute-done((bf16[2,1024,128]{2,1,0:T(8,128)(2,1)}, bf16[2,1024,128]{2,1,0:T(8,128)(2,1)}, u32[]{:S(2)}, u32[]{:S(2)}) %collective-permute-start.2) | collective-permute-done | bytes 524320 | tf_op jit(solution)/shard_map/ppermute | solution.py:259
  37.6 0.0 copy-done.2
  37.6 0.0 copy-done.3
  37.6 0.0 copy-done.1
  37.6 2.8 %prepare.1 = (bf16[128,4096]{1,0:T(8,128)(2,1)S(1)}, bf16[4096,128]{1,0:T(8,128)(2,1)S(1)}, bf16[64,64]{1,0:T(8,128)(2,1)S(1)}) custom-call(s32[1]{0:T(128)} %bitcast.place_ref, s32[2]{0:T(128)S(1)} %copy-done.1, s32[1,64]{1,0:T(1,128)} %bitcast.7, bf16[2,1024,256]{2,1,0:T(8,128)(2,1)} %key_ref.3, bf16[2,1024,256]{2,1,0:T(8,128)(2,1)} %value_ref.3, ...), custom_call_target="tpu_custom_call" | custom-call | tf_op jit(solution)/shard_map/prepare/pallas_call | solution.py:279
  40.4 3.3 %all-to-all-done.1.query_ref = bf16[32,32,128]{2,1,0:T(8,128)(2,1)S(1)} async-done(((bf16[32,32,128]{2,1,0:T(8,128)(2,1)}), bf16[32,32,128]{2,1,0:T(8,128)(2,1)S(1)}, u32[]{:S(2)}, u32[]{:S(2)}) %all-to-all-start.1) | async-done | bytes 262176 | tf_op jit(solution)/shard_map/all_to_all | solution.py:278
  43.6 9.0 %attend.1 = bf16[32,32,128]{2,1,0:T(8,128)(2,1)S(1)} custom-call(bf16[32,32,128]{2,1,0:T(8,128)(2,1)S(1)} %all-to-all-done.1.query_ref, bf16[128,4096]{1,0:T(8,128)(2,1)S(1)} %get-tuple-element.24.keys, bf16[4096,128]{1,0:T(8,128)(2,1)S(1)} %get-tuple-element.25.values), custom_call_target="tpu_custom_call" | custom-call | tf_op jit(solution)/shard_map/attend/pallas_call | solution.py:295
  52.7 0.0 copy-start
  52.7 17.9 %all_to_all.20.partial_ref = bf16[32,32,128]{2,1,0:T(8,128)(2,1)S(1)} all-to-all(bf16[32,32,128]{2,1,0:T(8,128)(2,1)S(1)} %attend.1), channel_id=1, replica_groups=mesh['seq'=32,'head'=4,'user'=4] {'seq'}, dimensions={0} | all-to-all | bytes 524288 | tf_op jit(solution)/shard_map/all_to_all | solution.py:303
  70.5 0.0 copy-done
  70.6 1.0 %finish.1 = bf16[4,64,256]{2,1,0:T(8,128)(2,1)S(1)} custom-call(s32[2]{0:T(128)S(1)} %copy-done.1, bf16[64,64]{1,0:T(8,128)(2,1)S(1)} %get-tuple-element.20.back_ref, bf16[32,32,128]{2,1,0:T(8,128)(2,1)S(1)} %all_to_all.20.partial_ref, bf16[64,256]{1,0:T(8,128)(2,1)S(1)} %get-tuple-element.26.gate_ref, bf16[256,1024]{1,0:T(8,128)(2,1)S(1)} %copy-done), custom_call_target="tpu_custom_call" | custom-call | tf_op jit(solution)/shard_map/finish/pallas_call | solution.py:304
  71.5 9.1 %all_to_all.21.term_ref = bf16[4,64,256]{2,1,0:T(8,128)(2,1)S(1)} all-to-all(bf16[4,64,256]{2,1,0:T(8,128)(2,1)S(1)} %finish.1), channel_id=1, replica_groups=mesh['seq'=32,'head'=4,'user'=4] {'head'}, dimensions={0} | all-to-all | bytes 262144 | tf_op jit(solution)/shard_map/all_to_all | solution.py:312
  80.6 0.6 add.1
Async XLA Ops:
  2.5 21.4 %all-to-all-start = ((bf16[4,64,256]{2,1,0:T(8,128)(2,1)}), bf16[4,64,256]{2,1,0:T(8,128)(2,1)S(1)}, u32[]{:S(2)}, u32[]{:S(2)}) async-start(bf16[4,64,256]{2,1,0:T(8,128)(2,1)} %get-tuple-element.21), calls=%async_computation | async-start | bytes 262144 | tf_op jit(solution)/shard_map/all_to_all | solution.py:263
  11.7 20.0 %collective-permute-start = (bf16[2,1024,128]{2,1,0:T(8,128)(2,1)}, bf16[2,1024,128]{2,1,0:T(8,128)(2,1)S(1)}, u32[]{:S(2)}, u32[]{:S(2)}) collective-permute-start(bf16[2,1024,128]{2,1,0:T(8,128)(2,1)} %get-tuple-element.17), channel_id=1, source_target_pairs={{0,448},{16,464},{32,480},{48,496},{64,128},{80,144},{96,160},{112... | collective-permute-start | bytes 1572872 | tf_op jit(solution)/shard_map/ppermute | solution.py:259
  18.3 15.5 %collective-permute-start.1 = (bf16[2,1024,128]{2,1,0:T(8,128)(2,1)}, bf16[2,1024,128]{2,1,0:T(8,128)(2,1)S(1)}, u32[]{:S(2)}, u32[]{:S(2)}) collective-permute-start(bf16[2,1024,128]{2,1,0:T(8,128)(2,1)} %get-tuple-element.18), channel_id=1, source_target_pairs={{0,64},{16,80},{32,96},{48,112},{64,0},{80,16},{96,32},{112,48},{1... | collective-permute-start | bytes 1572872 | tf_op jit(solution)/shard_map/ppermute | solution.py:259
  20.2 17.3 %collective-permute-start.2 = (bf16[2,1024,128]{2,1,0:T(8,128)(2,1)}, bf16[2,1024,128]{2,1,0:T(8,128)(2,1)}, u32[]{:S(2)}, u32[]{:S(2)}) collective-permute-start(bf16[2,1024,128]{2,1,0:T(8,128)(2,1)} %get-tuple-element.19), channel_id=1, source_target_pairs={{0,16},{16,0},{32,48},{48,32},{64,80},{80,64},{96,112},{112,96},{1... | collective-permute-start | bytes 1572872 | tf_op jit(solution)/shard_map/ppermute | solution.py:259
  25.0 12.6 %copy-start.1 = (s32[2]{0:T(128)S(1)}, s32[2]{0:T(128)}, u32[]{:S(2)}) copy-start(s32[2]{0:T(128)} %length_ref.3) | copy-start | bytes 28
  25.0 18.6 %all-to-all-start.1 = ((bf16[32,32,128]{2,1,0:T(8,128)(2,1)}), bf16[32,32,128]{2,1,0:T(8,128)(2,1)S(1)}, u32[]{:S(2)}, u32[]{:S(2)}) async-start(bf16[32,32,128]{2,1,0:T(8,128)(2,1)} %get-tuple-element.23), calls=%async_computation.1 | async-start | bytes 524288 | tf_op jit(solution)/shard_map/all_to_all | solution.py:278
  31.8 5.8 %copy-start.2 = (bf16[2,1024,128]{2,1,0:T(8,128)(2,1)}, bf16[2,1024,128]{2,1,0:T(8,128)(2,1)S(1)}, u32[]{:S(2)}) copy-start(bf16[2,1024,128]{2,1,0:T(8,128)(2,1)S(1)} %collective-permute-done.rest_0_) | copy-start | bytes 1572868
  33.8 3.8 %copy-start.3 = (bf16[2,1024,128]{2,1,0:T(8,128)(2,1)}, bf16[2,1024,128]{2,1,0:T(8,128)(2,1)S(1)}, u32[]{:S(2)}) copy-start(bf16[2,1024,128]{2,1,0:T(8,128)(2,1)S(1)} %collective-permute-done.1.rest_1_) | copy-start | bytes 1572868
  52.7 17.9 %copy-start = (bf16[256,1024]{1,0:T(8,128)(2,1)S(1)}, bf16[256,1024]{1,0:T(8,128)(2,1)}, u32[]{:S(2)}) copy-start(bf16[256,1024]{1,0:T(8,128)(2,1)} %weight_ref.3) | copy-start | bytes 1572868
